TPU v7x, 32 devices: a whole 2x2x4 slice. The times are simulated.
32 devices in a mesh: dp: 16 (over z, x, core), head: 2 (over y).
Axes of the slice: x: 2, y: 2, z: 4, core: 2. Of those that a mesh axis runs over, the one named last changes fastest.
Arguments:
- stream_x: bfloat16 [32768, 512], P(('dp', 'head')), may hold values from -6 to 6
- stream_y: bfloat16 [32768, 512], P(('dp', 'head')), may hold values from -6 to 6
- segments: int32 [32768], P('dp'), may hold values from 0 to 8, as said below
- keep_mask: int32 [32768], P('dp'), may hold values 0 or 1
- query_weight: bfloat16 [512, 512], P(None, 'head'), may hold values from -0.25 to 0.25
- key_weight: bfloat16 [512, 512], P(None, 'head'), may hold values from -0.25 to 0.25
- value_weight: bfloat16 [512, 512], P(None, 'head'), may hold values from -0.25 to 0.25
- output_weight: bfloat16 [512, 512], P('head'), may hold values from -1.5 to 1.5
- first_gain: float32 [512], replicated, may hold values from 0.5 to 1.5
- first_shift: float32 [512], replicated, may hold values from -2 to 2
- up_weight: bfloat16 [2048, 512], P(('dp', 'head')), may hold values from -0.25 to 0.25
- down_weight: bfloat16 [2048, 512], P(('dp', 'head')), may hold values from -0.125 to 0.125
- second_gain: float32 [512], replicated, may hold values from 0.5 to 1.5
- second_shift: float32 [512], replicated, may hold values from -2 to 2
- grad_stream: bfloat16 [32768, 512], P(('dp', 'head')), may hold values from -6 to 6
- grad_dual: bfloat16 [32768, 512], P(('dp', 'head')), may hold values from -6 to 6
Outputs:
- new_stream: bfloat16 [32768, 512], P(('dp', 'head'))
- new_dual: bfloat16 [32768, 512], P(('dp', 'head'))
- stream_grad: float32 [32768, 512], P(('dp', 'head'))
- query_grad: float32 [512, 512], P(None, 'head')
- key_grad: float32 [512, 512], P(None, 'head')
- value_grad: float32 [512, 512], P(None, 'head')
- output_grad: float32 [512, 512], P('head')
- first_gain_grad: float32 [512], replicated
- first_shift_grad: float32 [512], replicated
- up_grad: float32 [2048, 512], P(('dp', 'head'))
- down_grad: float32 [2048, 512], P(('dp', 'head'))
- second_gain_grad: float32 [512], replicated
- second_shift_grad: float32 [512], replicated
Inputs may be any that keep to these rules, and one draw needn't show every extreme that they name: `segments`: within each sequence of 1024 tokens the ids never fall; equal ids mark one document. Each sequence begins with id 0 and ends with the largest id.
All inputs are finite; a program needn't handle non-finite values. No bound on the sum of `keep_mask` on one device may be relied on, other than what follows from the above.
Results may differ from a plain program's by a relative error of at most 0.018.
Values may be sent and summed in bfloat16 or wider, within the bound.
No kernel may reach another device: no remote copies, remote signals or barrier semaphores. Data moves between devices by JAX's collectives and lax.ppermute only.
A program may use at most 128 MiB of HBM per device.

v0:
```python
import functools
import math

import jax
import jax.numpy as jnp
from jax import lax
from jax.experimental import pallas as pl
from jax.experimental.pallas import tpu as pltpu
from jax.sharding import PartitionSpec as P

HEADS = 8
BF = jnp.bfloat16
F32 = jnp.float32
LOG2E = 1.4426950408889634
NEG = -1e30
BLK = 256
MIB = 1 << 20
PAIR = 128
EXTRA = 32
VMEM = 58


def dot(a, b, left, right):
    return lax.dot_general(a, b, (((left,), (right,)), ((), ())), preferred_element_type=F32)


def nn(a, b):
    return dot(a, b, 1, 0)


def nt(a, b):
    return dot(a, b, 1, 1)


def tn(a, b):
    return dot(a, b, 0, 0)


def params(mib):
    return pltpu.CompilerParams(vmem_limit_bytes=mib * MIB)


def cost(us):
    return pl.CostEstimate(flops=int(us * 1e9), bytes_accessed=1 << 20, transcendentals=0)


def mask_kernel(x_ref, seg_ref, keep_ref, mask_ref, xt_ref):
    seq = x_ref.shape[0]
    seg = seg_ref[...]
    code = jnp.where(keep_ref[...] == 1, seg, -1).astype(F32)
    seg = seg.astype(F32)
    line = lambda v: jnp.concatenate([v[i:i + 1] for i in range(v.shape[0])], axis=1)
    seg_row = line(seg)
    code_col = jnp.broadcast_to(line(code), (128, seq)).T
    at = 0
    for kb in range(seq // BLK):
        rows = slice(kb * BLK, (kb + 1) * BLK)
        width = seq - kb * BLK
        same = jnp.concatenate([code_col[rows]] * (width // 128), axis=1) == seg_row[:, kb * BLK:]
        key = lax.broadcasted_iota(jnp.int32, (BLK, BLK), 0)
        query = lax.broadcasted_iota(jnp.int32, (BLK, BLK), 1)
        own = (same[:, :BLK] & (key <= query)) | (key == query)
        mask_ref[:, at:at + BLK] = jnp.where(own, 0.0, NEG)
        if width > BLK:
            mask_ref[:, at + BLK:at + width] = jnp.where(same[:, BLK:], 0.0, NEG)
        at += width
    xt_ref[...] = x_ref[...].T


def make_mask(x, seg, keep):
    seq, width = x.shape
    blocks = seq // BLK
    return pl.pallas_call(
        mask_kernel,
        out_shape=[jax.ShapeDtypeStruct((BLK, BLK * blocks * (blocks + 1) // 2), F32), jax.ShapeDtypeStruct((width, seq), BF)],
        compiler_params=params(10),
        cost_estimate=cost(2),
        name="make_mask",
    )(x, seg, keep)


def offset(kb, seq):
    return sum(seq - i * BLK for i in range(kb))


def attn_fwd_kernel(scale, xt_ref, w_ref, mask_ref, *refs):
    qkv_ref, att_ref, lse_ref = refs[-3:]
    seq = xt_ref.shape[1]
    qkv_ref[...] = nn(w_ref[:3 * PAIR], xt_ref[...]).astype(BF)
    for h in range(2):
        head = lambda i: slice(i * PAIR + 64 * h, i * PAIR + 64 * h + 64)
        keys = qkv_ref[head(1), :].T
        for qb in range(seq // BLK):
            cols = slice(qb * BLK, (qb + 1) * BLK)
            q = qkv_ref[head(0), cols]
            scores = []
            for kb in range(qb + 1):
                at = offset(kb, seq) + (qb - kb) * BLK
                scores.append(nn(keys[kb * BLK:(kb + 1) * BLK], q) * (scale * LOG2E) + mask_ref[:, at:at + BLK])
            m = functools.reduce(jnp.maximum, [jnp.max(s, axis=0, keepdims=True) for s in scores])
            out, l = 0.0, 0.0
            for kb, s in enumerate(scores):
                p = jnp.exp2(s - m)
                l = l + jnp.sum(p, axis=0, keepdims=True)
                out = out + nn(qkv_ref[head(2), kb * BLK:(kb + 1) * BLK], p.astype(BF))
            att_ref[head(0), cols] = (out / l).astype(BF)
            lse_ref[h:h + 1, cols] = m + jnp.log2(l)


def attn_fwd(xt, w, mask, scale, slot, held=()):
    width, seq = xt.shape
    full = lambda shape: pl.BlockSpec(shape, lambda p: (0,) * len(shape))
    own = lambda rows: pl.BlockSpec((None, rows, seq), lambda p: (slot, 0, 0))
    return pl.pallas_call(
        functools.partial(attn_fwd_kernel, scale),
        grid=(1,),
        in_specs=[full((width, seq)), full(w.shape), full(mask.shape)] + [pl.BlockSpec(memory_space=pl.ANY)] * len(held),
        out_specs=[own(3 * PAIR), own(PAIR), own(2)],
        out_shape=[pltpu.HBM((2, 3 * PAIR, seq), BF), jax.ShapeDtypeStruct((2, PAIR, seq), BF), jax.ShapeDtypeStruct((2, 2, seq), F32)],
        input_output_aliases={3 + i: i for i in range(len(held))},
        compiler_params=params(12),
        cost_estimate=cost(5),
        name="attn_fwd",
    )(xt, w, mask, *held)


def attn_bwd_kernel(scale, xt_ref, qkv_ref, att_ref, do_ref, gb_ref, lse_ref, vec_ref, mask_ref, g_ref, other_ref, mine_ref, pay_ref, dq_ref):
    width, seq = xt_ref.shape
    dq_ref[...] = jnp.zeros_like(dq_ref)

    for h in range(2):
        head = lambda i: slice(i * PAIR + 64 * h, i * PAIR + 64 * h + 64)
        own = head(0)
        keys, values = qkv_ref[head(1), :].T, qkv_ref[head(2), :].T
        delta = jnp.sum(do_ref[own, :].astype(F32) * att_ref[own, :].astype(F32), axis=0, keepdims=True)
        lse = lse_ref[h:h + 1, :]
        for kb in range(seq // BLK):
            rows = slice(kb * BLK, (kb + 1) * BLK)
            lo, at = kb * BLK, offset(kb, seq)
            q, dout = qkv_ref[own, lo:], do_ref[own, lo:]
            s = nn(keys[rows], q) * (scale * LOG2E) + mask_ref[:, at:at + seq - lo]
            p = jnp.exp2(s - lse[:, lo:])
            dp = nn(values[rows], dout)
            ds = (p * (dp - delta[:, lo:])).astype(BF)
            g_ref[head(2), rows] = nt(dout, p.astype(BF)).astype(BF)
            g_ref[head(1), rows] = (nt(q, ds) * scale).astype(BF)
            dq_ref[own, lo:] += nn(qkv_ref[head(1), rows], ds)
    g_ref[0:PAIR, :] = (dq_ref[...] * scale).astype(BF)
    pay_ref[0:width, 0:3 * PAIR] = nt(xt_ref[...], g_ref[...]).astype(BF)
    pay_ref[0:width, 3 * PAIR:] = nt(gb_ref[...], att_ref[...]).astype(BF)
    pay_ref[width:, :] = jnp.concatenate([vec_ref[...], jnp.zeros((EXTRA - 8, 4 * PAIR), F32)], axis=0).astype(BF)

    @pl.when(pl.program_id(0) == 0)
    def _():
        other_ref[...] = pay_ref[...]

    @pl.when(pl.program_id(0) == 1)
    def _():
        mine_ref[...] = pay_ref[...]


def attn_bwd(xt, qkv, att, do, gb, lse, vec, mask, scale):
    width, seq = xt.shape
    full = lambda shape: pl.BlockSpec(shape, lambda p: (0,) * len(shape))
    own = lambda rows: pl.BlockSpec((None, rows, seq), lambda p: (p, 0, 0))
    pay = (width + EXTRA, 4 * PAIR)
    return pl.pallas_call(
        functools.partial(attn_bwd_kernel, scale),
        grid=(2,),
        in_specs=[full((width, seq)), own(3 * PAIR), own(PAIR), own(PAIR), full((width, seq)), own(2), full(vec.shape), full(mask.shape)],
        out_specs=[own(3 * PAIR), full(pay), full(pay)],
        out_shape=[pltpu.HBM((2, 3 * PAIR, seq), BF), jax.ShapeDtypeStruct(pay, BF), jax.ShapeDtypeStruct(pay, BF)],
        scratch_shapes=[pltpu.VMEM(pay, BF), pltpu.VMEM((PAIR, seq), F32)],
        compiler_params=params(16),
        cost_estimate=cost(11),
        name="attn_bwd",
    )(xt, qkv, att, do, gb, lse, vec, mask)


def gelu_parts(h):
    phi = 0.5 * lax.erf(h * math.sqrt(0.5)) + 0.5
    slope = jnp.exp2(h * h * (-0.5 * LOG2E)) * (1.0 / math.sqrt(2.0 * math.pi))
    return h * phi, phi + h * slope


def mean_of(v):
    return jnp.sum(v, axis=-1, keepdims=True) * (1.0 / v.shape[-1])


def normed(z):
    c = z - mean_of(z)
    rstd = lax.rsqrt(mean_of(c * c) + 1e-5)
    return c * rstd, rstd


def norm_back(w, zhat, rstd):
    return rstd * (w - mean_of(w) - zhat * mean_of(w * zhat))


def row_specs(blk):
    row = lambda w: pl.BlockSpec((blk, w), lambda p: (p, 0))
    full = lambda shape: pl.BlockSpec(shape, lambda p: (0,) * len(shape))
    return row, full


def column(rows, blk):
    return pl.BlockSpec((2, rows, blk), lambda p: (0, 0, p))


def joined(refs):
    return jnp.concatenate([ref[i] for ref in refs for i in range(2)], axis=0)


def out_spec(width):
    return pl.BlockSpec((PAIR, width), lambda p: (3, 0))


def first_kernel(pairs, pieces, x_ref, *refs):
    att, refs = refs[:pairs // 2], refs[pairs // 2:]
    wo, refs = refs[:pairs], refs[pairs:]
    ffw, refs = refs[:pieces], refs[pieces:]
    g1_ref, b1_ref, mixed_ref, low_ref, act_ref, der_ref, ffn_ref = refs
    branch = nn(joined(att).T, jnp.concatenate([w[...] for w in wo], axis=0))
    mixed = x_ref[...].astype(F32) + branch
    mixed_ref[...] = mixed
    zhat, _ = normed(mixed)
    low = (zhat * g1_ref[...] + b1_ref[...]).astype(BF)
    low_ref[...] = low
    at = 0
    for w in ffw:
        n = w.shape[1]
        val, der = gelu_parts(nt(low, w[0]))
        act_ref[:, at:at + n] = val.astype(BF)
        der_ref[:, at:at + n] = der.astype(BF)
        at += n
    ffn_ref[...] = nn(act_ref[...], jnp.concatenate([w[1] for w in ffw], axis=0))


def first_part(x, att, wo, ffw, g1, b1, blk=256):
    seq, width = x.shape
    ff = sum(w.shape[1] for w in ffw)
    row, full = row_specs(blk)
    sd = lambda w, t: jax.ShapeDtypeStruct((seq, w), t)
    return pl.pallas_call(
        functools.partial(first_kernel, len(wo), len(ffw)),
        grid=(seq // blk,),
        in_specs=[row(width)] + [column(PAIR, blk)] * len(att) + [out_spec(width)] * len(wo) + [full(w.shape) for w in ffw] + [full((1, width))] * 2,
        out_specs=[row(width), row(width), row(ff), row(ff), row(width)],
        out_shape=[sd(width, F32), sd(width, BF), sd(ff, BF), sd(ff, BF), sd(width, F32)],
        compiler_params=params(10),
        cost_estimate=cost(8),
        name="first_part",
    )(x, *att, *wo, *ffw, g1, b1)


def second_kernel(pairs, pa, pb, x_ref, y_ref, gs_ref, gd_ref, mixed_ref, low_ref, ffn_ref, der_a_ref, *refs):
    wo, refs = refs[:pairs], refs[pairs:]
    ffa, refs = refs[:pa], refs[pa:]
    ffb, refs = refs[:pb], refs[pb:]
    (g1_ref, b1_ref, g2_ref, b2_ref, ns_ref, nd_ref, act_ref, dh_ref, gf_ref, gm_ref, gb_ref, *rest) = refs
    do, (vec_ref, der_ref) = rest[:pairs // 2], rest[pairs // 2:]
    @pl.when(pl.program_id(0) == 0)
    def _():
        vec_ref[...] = jnp.zeros_like(vec_ref)
    mixed = mixed_ref[...]
    zhat1, rstd1 = normed(mixed)
    first = zhat1 * g1_ref[...] + b1_ref[...]
    low = low_ref[...]
    at = 0
    for w in ffb:
        n = w.shape[1]
        val, der = gelu_parts(nt(low, w[0]))
        act_ref[:, at:at + n] = val.astype(BF)
        der_ref[:, at:at + n] = der.astype(BF)
        at += n
    ffn = ffn_ref[...] + nn(act_ref[...], jnp.concatenate([w[1] for w in ffb], axis=0))
    zhat2, rstd2 = normed(first + ffn)
    ns_ref[...] = (zhat2 * g2_ref[...] + b2_ref[...]).astype(BF)
    nd_ref[...] = (y_ref[...].astype(F32) + (mixed - x_ref[...].astype(F32)) + ffn).astype(BF)
    u = gs_ref[...].astype(F32)
    second = norm_back(u * g2_ref[...], zhat2, rstd2)
    gd = gd_ref[...].astype(F32)
    gf = (second + gd).astype(BF)
    gf_ref[...] = gf
    at = 0
    for side, der, base in ((ffa, der_a_ref, 0), (ffb, der_ref, der_a_ref.shape[1])):
        for w in side:
            n = w.shape[1]
            dh_ref[:, at:at + n] = (nt(gf, w[1]) * der[:, at - base:at - base + n].astype(F32)).astype(BF)
            at += n
    gfirst = second + nn(dh_ref[...], jnp.concatenate([w[0] for w in ffa + ffb], axis=0))
    gm = norm_back(gfirst * g1_ref[...], zhat1, rstd1)
    gm_ref[...] = gm
    gb = (gm + gd).astype(BF)
    gb_ref[...] = gb.T
    dout = nt(gb, jnp.concatenate([w[...] for w in wo], axis=0)).astype(BF).T
    for i in range(pairs):
        do[i // 2][i % 2] = dout[i * PAIR:(i + 1) * PAIR]
    fold = lambda v: jnp.sum(v, axis=0, keepdims=True)
    vec_ref[...] += jnp.concatenate([fold(gfirst * zhat1), fold(gfirst), fold(u * zhat2), fold(u), jnp.zeros((4, u.shape[1]), F32)], axis=0)


def second_part(x, y, gs, gd, mixed, low, ffn, der, wo, ffa, ffb, g1, b1, g2, b2, blk=256):
    seq, width = x.shape
    fa, fb = sum(w.shape[1] for w in ffa), sum(w.shape[1] for w in ffb)
    row, full = row_specs(blk)
    sd = lambda w, t: jax.ShapeDtypeStruct((seq, w), t)
    return pl.pallas_call(
        functools.partial(second_kernel, len(wo), len(ffa), len(ffb)),
        grid=(seq // blk,),
        in_specs=[row(width)] * 7 + [row(fa)] + [out_spec(width)] * len(wo) + [full(w.shape) for w in (*ffa, *ffb)] + [full((1, width))] * 4,
        out_specs=[row(width), row(width), row(fb), row(fa + fb), row(width), row(width), pl.BlockSpec((width, blk), lambda p: (0, p))] + [column(PAIR, blk)] * (len(wo) // 2) + [full((8, width))],
        out_shape=[sd(width, BF), sd(width, BF), sd(fb, BF), sd(fa + fb, BF), sd(width, BF), pltpu.HBM((seq, width), F32), jax.ShapeDtypeStruct((width, seq), BF)] + [jax.ShapeDtypeStruct((2, PAIR, seq), BF)] * (len(wo) // 2) + [jax.ShapeDtypeStruct((8, width), F32)],
        scratch_shapes=[pltpu.VMEM((blk, fb), BF)],
        compiler_params=params(14),
        cost_estimate=cost(18),
        name="second_part",
    )(x, y, gs, gd, mixed, low, ffn, der, *wo, *ffa, *ffb, g1, b1, g2, b2)


def wgrad_kernel(act_a_ref, act_b_ref, dh_ref, gf_ref, low_ref, out_ref):
    out_ref[0] = tn(dh_ref[...], low_ref[...]).astype(BF)
    @pl.when(pl.program_id(0) == 0)
    def _():
        out_ref[1] = tn(act_a_ref[...], gf_ref[...]).astype(BF)
    @pl.when(pl.program_id(0) == 1)
    def _():
        out_ref[1] = tn(act_b_ref[...], gf_ref[...]).astype(BF)


def wgrad(act_a, act_b, dh, gf, low, which):
    seq, width = gf.shape
    b = act_a.shape[1] // 2
    full = lambda shape: pl.BlockSpec(shape, lambda p: (0,) * len(shape))
    half = pl.BlockSpec((seq, b), lambda p: (0, which))
    return pl.pallas_call(
        wgrad_kernel,
        grid=(2,),
        in_specs=[half, half, pl.BlockSpec((seq, b), lambda p: (0, 2 * p + which)), full((seq, width)), full((seq, width))],
        out_specs=pl.BlockSpec((None, 2, b, width), lambda p: (p, 0, 0, 0)),
        out_shape=jax.ShapeDtypeStruct((2, 2, b, width), BF),
        compiler_params=params(10),
        cost_estimate=cost(6),
        name="wgrad",
    )(act_a, act_b, dh, gf, low)


def sgrad_kernel(pairs, gm_ref, *refs):
    g, refs = refs[:pairs // 2], refs[pairs // 2:]
    w, (out_ref,) = refs[:pairs], refs[pairs:]
    left = joined(g).T
    out_ref[...] = gm_ref[...] + nn(left, jnp.concatenate([a[...] for a in w], axis=0))


def sgrad(gm, g, w, blk=256):
    seq, width = gm.shape
    row, full = row_specs(blk)
    return pl.pallas_call(
        functools.partial(sgrad_kernel, len(w)),
        grid=(seq // blk,),
        in_specs=[row(width)] + [column(3 * PAIR, blk)] * len(g) + [full((3 * PAIR, width))] * len(w),
        out_specs=row(width),
        out_shape=jax.ShapeDtypeStruct((seq, width), F32),
        compiler_params=params(8),
        cost_estimate=cost(4),
        name="sgrad",
    )(gm, *g, *w)


def prep_kernel(place_ref, wq_ref, wk_ref, wv_ref, wo_ref, up_ref, down_ref, mine_ref, other_ref, ffw_ref):
    ffw_ref[0] = up_ref[...]
    ffw_ref[1] = down_ref[...]
    for out_ref, which in ((mine_ref, place_ref[0]), (other_ref, 1 - place_ref[0])):
        part = pl.ds(pl.multiple_of(which * PAIR, PAIR), PAIR)
        for i, ref in enumerate((wq_ref, wk_ref, wv_ref)):
            out_ref[i * PAIR:(i + 1) * PAIR, :] = ref[:, part].T
        out_ref[3 * PAIR:, :] = wo_ref[part, :]


def prep(core, wq, wk, wv, wo, up, down):
    width = wq.shape[0]
    sd = lambda *shape: jax.ShapeDtypeStruct(shape, BF)
    here = lambda v: pltpu.with_memory_space_constraint(v, pltpu.HBM)
    vmem = pl.BlockSpec()
    return pl.pallas_call(
        prep_kernel,
        in_specs=[pl.BlockSpec(memory_space=pltpu.SMEM)] + [vmem] * 6,
        out_shape=[sd(4 * PAIR, width), sd(4 * PAIR, width), sd(2, *up.shape)],
        compiler_params=params(8),
        cost_estimate=cost(2),
        name="prep",
    )(core.reshape(1), *map(here, (wq, wk, wv, wo, up, down)))


def finish_kernel(core_ref, mine_ref, other_ref, dq_ref, dk_ref, dv_ref, og_ref, vec_ref):
    width = dq_ref.shape[0]
    own = core_ref[0] == 0
    mine, other = mine_ref[...].astype(F32), other_ref[...].astype(F32)
    left, right = jnp.where(own, mine, other), jnp.where(own, other, mine)
    for i, ref in enumerate((dq_ref, dk_ref, dv_ref)):
        cols = slice(i * PAIR, (i + 1) * PAIR)
        ref[:, :PAIR] = left[:width, cols]
        ref[:, PAIR:] = right[:width, cols]
    og_ref[:PAIR, :] = left[:width, 3 * PAIR:].T
    og_ref[PAIR:, :] = right[:width, 3 * PAIR:].T
    vec_ref[...] = mine[width:width + 8]


def finish(core, mine, other):
    width = mine.shape[1]
    sd = lambda *shape: jax.ShapeDtypeStruct(shape, F32)
    vmem = pl.BlockSpec(memory_space=pltpu.VMEM)
    return pl.pallas_call(
        finish_kernel,
        in_specs=[pl.BlockSpec(memory_space=pltpu.SMEM), vmem, vmem],
        out_shape=[sd(width, 2 * PAIR)] * 3 + [sd(2 * PAIR, width), sd(8, width)],
        compiler_params=params(8),
        cost_estimate=cost(3),
        name="finish",
    )(core.reshape(1), mine, other)


def after(value, *earlier):
    return lax.optimization_barrier((value, earlier))[0]


def body(
    dp_size,
    head_size,
    stream_x,
    stream_y,
    segments,
    keep_mask,
    query_weight,
    key_weight,
    value_weight,
    output_weight,
    first_gain,
    first_shift,
    up_weight,
    down_weight,
    second_gain,
    second_shift,
    grad_stream,
    grad_dual,
):
    seq, width = stream_x.shape
    cols = query_weight.shape[1]
    scale = 1.0 / math.sqrt(width // HEADS)
    total = dp_size * head_size
    core_step = head_size
    head_steps = [1 << b for b in range(head_size.bit_length() - 1)]
    chip_steps = [core_step << b for b in range(1, dp_size.bit_length() - 1)]
    fast = cols == 2 * PAIR and head_size == 2

    def swap(value, even_step, odd_step=None):
        odd_step = even_step if odd_step is None else odd_step
        pairs = [
            (i, i ^ (odd_step if i // core_step % 2 else even_step)) for i in range(total)
        ]
        return lax.ppermute(value, ("dp", "head"), pairs)

    def pick(low, first, second):
        return jnp.where(low, first, second)

    index = lax.axis_index("dp") * head_size + lax.axis_index("head")
    bit_of = lambda step: (index >> (step.bit_length() - 1)) & 1
    core = bit_of(core_step)
    row = lambda vec: vec.reshape(1, width)
    g1, b1, g2, b2 = row(first_gain), row(first_shift), row(second_gain), row(second_shift)

    even = [chip_steps[-1]] + chip_steps[:-1] + head_steps
    odd = [chip_steps[-1]] + chip_steps[1:-1] + head_steps + chip_steps[:1]
    steps = list(zip(even, odd))

    tokens = lambda v: lax.dynamic_slice_in_dim(v.reshape(-1, 128), lax.axis_index("head") * (seq // 128), seq // 128)
    mask, xt = make_mask(stream_x, tokens(segments), tokens(keep_mask))
    fwd = functools.partial(attn_fwd, xt, mask=mask, scale=scale)

    if fast:
        s0, s1, s2 = chip_steps
        bit0, bit1 = bit_of(s0), bit_of(s1)
        core, first_low, second_low = lax.optimization_barrier((core, pick(core == 0, bit0, bit1) == 0, pick(core == 0, bit1, bit0) == 0))
        mine, other, ffw = prep(core, query_weight, key_weight, value_weight, output_weight, up_weight, down_weight)
        far_mine = swap(mine, head_steps[0])
        got = swap(ffw, *steps[0])
        near = fwd(mine, slot=1)
        ffw = jnp.concatenate([ffw, after(got, near[1])], axis=1)
        got = swap(ffw, *steps[1])
        near = fwd(after(other, ffw), slot=0, held=near)
        ffw = jnp.concatenate([ffw, after(got, near[1])], axis=1)
        got = swap(ffw, *steps[2])
        far_mine = after(far_mine, near[1])
        far_other = swap(far_mine, core_step)
        far = fwd(after(far_mine, ffw), slot=1)
        ffw = jnp.concatenate([ffw, after(got, far[1])], axis=1)
        got = swap(ffw, *steps[3])
        part = swap(ffw, core_step)
        far = fwd(after(far_other, ffw), slot=0, held=far)
        weights = [other, mine, far_other, far_mine]
        side_a = [ffw, part]
    else:
        ffw = jnp.stack([up_weight, down_weight])
        stacked = jnp.stack([query_weight.T, key_weight.T, value_weight.T, output_weight])
        for step in head_steps:
            stacked = jnp.concatenate([stacked, swap(stacked, step)], axis=1)
        weights = [stacked[:, i:i + PAIR].reshape(4 * PAIR, width) for i in range(0, width, PAIR)]
        near = fwd(weights[1], slot=1, held=fwd(weights[0], slot=0))
        far = fwd(weights[3], slot=1, held=fwd(weights[2], slot=0))
        for a, b in steps[:-1]:
            ffw = jnp.concatenate([ffw, swap(ffw, a, b)], axis=1)
        got = swap(ffw, *steps[-1])
        side_a = [ffw, swap(ffw, core_step)]

    mixed, low, act_a, der_a, ffn_a = first_part(stream_x, [near[1], far[1]], weights, side_a, g1, b1)
    got = after(got, mixed)
    side_b = [got, swap(got, core_step)]
    ns, nd, act_b, dh, gf, gm, gb, do_near, do_far, vec = second_part(
        stream_x, stream_y, grad_stream, grad_dual, mixed, low, ffn_a, der_a, weights, side_a, side_b, g1, b1, g2, b2
    )

    ffgrad = lambda which, *earlier: wgrad(act_a, act_b, after(dh, *earlier), gf, low, which)

    def bwd(group, do, *earlier):
        qkv, att, lse = group
        return attn_bwd(xt, qkv, att, after(do, *earlier), gb, lse, vec, mask, scale)

    def halves(own, received):
        n = own.shape[1] // 2
        return own[:, n:] + received[:, n:], own[:, :n] + received[:, :n]

    g_far, pay_far_other, pay_far = bwd(far, do_far)
    if fast:
        crossed_pay = swap(pay_far_other, core_step)
        theirs = ffgrad(1, pay_far)
        crossed = swap(theirs, core_step)
        pay_far = pay_far + after(crossed_pay, theirs)
        from_head = swap(pay_far, head_steps[0])
        g_near, pay_other, pay_mine = bwd(near, do_near, pay_far)
        crossed_pay = swap(pay_other, core_step)
        ours = ffgrad(0, pay_mine)
        whole = pay_mine + after(crossed_pay, ours) + from_head
        whole = jnp.concatenate([whole[:width], pay_far[width:] + from_head[width:]], axis=0)

        def split(low, value):
            n = value.shape[0] // 2
            return pick(low, value[n:], value[:n]), pick(low, value[:n], value[n:])

        def merge(low, own, received):
            return pick(low, jnp.concatenate([own, received]), jnp.concatenate([received, own]))

        sent, kept = split(first_low, whole)
        got = swap(sent, s0, s1)
        crossed, ours = after((crossed, ours), sent)
        part_b = ours[1] + crossed[1]
        recv = swap(part_b, *steps[3])
        part = ours[0] + crossed[0]
        sg = sgrad(gm, [g_near, after(g_far, part_b)], weights)
        sent, kept = split(second_low, kept + after(got, part, sg))
        got = swap(sent, s1, s0)
        whole = kept + got
        got = swap(whole, s2)
        sent, part = halves(part, after(recv, whole))
        recv = swap(sent, *steps[2])
        whole = whole + after(got, sent)
        got = swap(whole, s1, s0)
        sent, part = halves(part, after(recv, whole))
        recv = swap(sent, *steps[1])
        whole = merge(second_low, whole, after(got, sent))
        got = swap(whole, s0, s1)
        sent, part = halves(part, after(recv, whole))
        recv = swap(sent, *steps[0])
        whole = merge(first_low, whole, after(got, sent))
        got = swap(whole, core_step)
        part = part.astype(F32) + recv.astype(F32)
        *dw, out_grad, vec = finish(core, whole, got)
    else:
        g_near, pay_near_other, pay_near = bwd(near, do_near)
        crossed = swap(ffgrad(1), core_step)
        ours = ffgrad(0)
        part = ours[0] + crossed[0] + swap(ours[1] + crossed[1], *steps[-1])
        for a, b in steps[-2::-1]:
            n = part.shape[1] // 2
            recv = swap(part[:, n:], a, b)
            part = part[:, :n].astype(F32) + recv.astype(F32)
            part = part.astype(BF) if n > up_weight.shape[0] else part
        pays = [pay_near_other, pay_near, pay_far_other, pay_far]
        low_vec = pay_near[width:]
        pays = jnp.stack([pay[:width] for pay in pays]).reshape(len(pays), width, 4, PAIR)
        pays = pays.transpose(2, 1, 0, 3).reshape(4, width, width)
        for step in head_steps[::-1]:
            n = pays.shape[2] // 2
            pays = pays[:, :, :n] + swap(pays[:, :, n:], step)
            low_vec = low_vec + swap(low_vec, step)
        for step in [core_step] + chip_steps:
            pays = pays + swap(pays, step)
            low_vec = low_vec + swap(low_vec, step)
        pays = pays.astype(F32)
        dw, out_grad = [pays[0], pays[1], pays[2]], pays[3].T
        vec = low_vec[:4].astype(F32)
        sg = sgrad(gm, [g_near, g_far], weights)

    return (
        ns, nd, sg, dw[0], dw[1], dw[2], out_grad,
        vec[0], vec[1], part[0], part[1], vec[2], vec[3],
    )


def solution(mesh):
    both = ("dp", "head")
    rows, cols, whole = P(both, None), P(None, "head"), P()
    in_specs = (
        rows, rows, P("dp"), P("dp"), cols, cols, cols, P("head", None),
        whole, whole, rows, rows, whole, whole, rows, rows,
    )
    out_specs = (
        rows, rows, rows, cols, cols, cols, P("head", None),
        whole, whole, rows, rows, whole, whole,
    )
    inner = functools.partial(body, mesh.shape["dp"], mesh.shape["head"])
    return jax.shard_map(inner, mesh=mesh, in_specs=in_specs, out_specs=out_specs, check_vma=False)
```

profile of v0, /device:TPU:0, one launch (start us, length us, event | category | flops | bytes accessed | tf_op | source)
XLA Modules:
  0.0 136.4 jit_solution(3606567420716188572)
XLA Ops:
  2.3 4.1 %collective-permute-start = (bf16[2,64,512]{2,1,0:T(8,128)(2,1)S(1)}, bf16[2,64,512]{2,1,0:T(8,128)(2,1)S(1)}, u32[]{:S(2)}, u32[]{:S(2)}) collective-permute-start(bf16[2,64,512]{2,1,0:T(8,128)(2,1)S(1)} %get-tuple-element.85), channel_id=1, source_target_pairs={{0,16},{1,17},{2,18},{3,19},{4,20},{5,21},{6,22},{7,23},{8,24},{9,... | collective-permute-start | bytes 393224 | tf_op jit(solution)/shard_map/ppermute | solution.py:461
  8.5 3.4 %attn_fwd.4 = (bf16[2,384,1024]{2,1,0:T(8,128)(2,1)}, bf16[2,128,1024]{2,1,0:T(8,128)(2,1)S(1)}, f32[2,2,1024]{2,1,0:T(2,128)S(1)}) custom-call(bf16[512,1024]{1,0:T(8,128)(2,1)S(1)} %get-tuple-element.82.xt_ref, bf16[512,512]{1,0:T(8,128)(2,1)S(1)} %get-tuple-element.86.w_ref.refs_3_.refs_1_, f32[256,2560]{1,0:T(8,128)S(1)} %get-tuple-element.87.mask_ref), custom_call_target="tpu_custom_call" | custom-call | flops 5000000000 | bytes 1048576 | tf_op jit(solution)/shard_map/attn_fwd/pallas_call | solution.py:114
  14.3 4.1 %attn_fwd.5 = (bf16[2,384,1024]{2,1,0:T(8,128)(2,1)}, bf16[2,128,1024]{2,1,0:T(8,128)(2,1)S(1)}, f32[2,2,1024]{2,1,0:T(2,128)S(1)}) custom-call(bf16[512,1024]{1,0:T(8,128)(2,1)S(1)} %get-tuple-element.82.xt_ref, bf16[512,512]{1,0:T(8,128)(2,1)S(1)} %get-tuple-element.90.w_ref.refs_2_.refs_0_, ...), custom_call_target="tpu_custom_call", output_to_operand_aliasing={{0}: (3, {}), {1}: (4, {}), {2}: (5, {})} | custom-call | flops 5000000000 | bytes 1048576 | tf_op jit(solution)/shard_map/attn_fwd/pallas_call | solution.py:114
  20.1 3.4 %attn_fwd.6 = (bf16[2,384,1024]{2,1,0:T(8,128)(2,1)}, bf16[2,128,1024]{2,1,0:T(8,128)(2,1)S(1)}, f32[2,2,1024]{2,1,0:T(2,128)S(1)}) custom-call(bf16[512,1024]{1,0:T(8,128)(2,1)S(1)} %get-tuple-element.82.xt_ref, bf16[512,512]{1,0:T(8,128)(2,1)S(1)} %collective-permute-done.1.w_ref.refs_5_.refs_3_, f32[256,2560]{1,0:T(8,128)S(1)} %get-tuple-element.87.mask_ref), custom_call_target="tpu_custom_call" | custom-call | flops 5000000000 | bytes 1048576 | tf_op jit(solution)/shard_map/attn_fwd/pallas_call | solution.py:114
  23.5 4.9 %collective-permute-done.4 = bf16[2,256,512]{2,1,0:T(8,128)(2,1)S(1)} collective-permute-done((bf16[2,256,512]{2,1,0:T(8,128)(2,1)S(1)}, bf16[2,256,512]{2,1,0:T(8,128)(2,1)S(1)}, u32[]{:S(2)}, u32[]{:S(2)}) %collective-permute-start.4) | collective-permute-done | bytes 524320 | tf_op jit(solution)/shard_map/ppermute | solution.py:461
  31.9 4.3 %attn_fwd.7 = (bf16[2,384,1024]{2,1,0:T(8,128)(2,1)}, bf16[2,128,1024]{2,1,0:T(8,128)(2,1)S(1)}, f32[2,2,1024]{2,1,0:T(2,128)S(1)}) custom-call(bf16[512,1024]{1,0:T(8,128)(2,1)S(1)} %get-tuple-element.82.xt_ref, bf16[512,512]{1,0:T(8,128)(2,1)S(1)} %collective-permute-done.2.w_ref.refs_4_.refs_2_, ...), custom_call_target="tpu_custom_call", output_to_operand_aliasing={{0}: (3, {}), {1}: (4, {}), {2}: (5, {})} | custom-call | flops 5000000000 | bytes 1048576 | tf_op jit(solution)/shard_map/attn_fwd/pallas_call | solution.py:114
  36.3 6.0 %first_part.1 = (f32[1024,512]{1,0:T(8,128)S(1)}, bf16[1024,512]{1,0:T(8,128)(2,1)S(1)}, bf16[1024,1024]{1,0:T(8,128)(2,1)S(1)}, bf16[1024,1024]{1,0:T(8,128)(2,1)S(1)}, f32[1024,512]{1,0:T(8,128)S(1)}) custom-call(bf16[1024,512]{1,0:T(8,128)(2,1)S(1)} %copy-done, bf16[2,128,1024]{2,1,0:T(8,128)(2,1)S(1)} %get-tuple-element.93.refs_0_.att_ref, ...), custom_call_target="tpu_custom_call" | custom-call | flops 8000000000 | bytes 1048576 | tf_op jit(solution)/shard_map/first_part/pallas_call | solution.py:244
  43.8 2.7 %collective-permute-done.7.refs_7_ = bf16[2,512,512]{2,1,0:T(8,128)(2,1)S(1)} collective-permute-done((bf16[2,512,512]{2,1,0:T(8,128)(2,1)S(1)}, bf16[2,512,512]{2,1,0:T(8,128)(2,1)S(1)}, u32[]{:S(2)}, u32[]{:S(2)}) %collective-permute-start.7) | collective-permute-done | bytes 1048608 | tf_op jit(solution)/shard_map/ppermute | solution.py:461
  46.5 13.2 %second_part.1 = (bf16[1024,512]{1,0:T(8,128)(2,1)}, bf16[1024,512]{1,0:T(8,128)(2,1)}, bf16[1024,1024]{1,0:T(8,128)(2,1)S(1)}, bf16[1024,2048]{1,0:T(8,128)(2,1...) custom-call(bf16[1024,512]{1,0:T(8,128)(2,1)S(1)} %copy-done, ...), custom_call_target="tpu_custom_call" | custom-call | flops 17999998976 | bytes 1048576 | tf_op jit(solution)/shard_map/second_part/pallas_call | solution.py:308
  59.7 9.9 %attn_bwd.2 = (bf16[2,384,1024]{2,1,0:T(8,128)(2,1)}, bf16[544,512]{1,0:T(8,128)(2,1)S(1)}, bf16[544,512]{1,0:T(8,128)(2,1)S(1)}) custom-call(bf16[512,1024]{1,0:T(8,128)(2,1)S(1)} %get-tuple-element.82.xt_ref, bf16[2,384,1024]{2,1,0:T(8,128)(2,1)S(1)} %copy-done.11, bf16[2,128,1024]{2,1,0:T(8,128)(2,1)S(1)} %get-tuple-element.102.refs_1_.att_ref, ...), custom_call_target="tpu_custom_call" | custom-call | flops 11000000512 | bytes 1048576 | tf_op jit(solution)/shard_map/attn_bwd/pallas_call | solution.py:167
  69.8 3.3 %wgrad.2 = bf16[2,2,512,512]{3,2,1,0:T(8,128)(2,1)S(1)} custom-call(bf16[1024,1024]{1,0:T(8,128)(2,1)S(1)} %get-tuple-element.120.act_a_ref, bf16[1024,1024]{1,0:T(8,128)(2,1)S(1)} %get-tuple-element.121.act_b_ref, bf16[1024,2048]{1,0:T(8,128)(2,1)S(1)} %get-tuple-element.131.dh_ref, bf16[1024,512]{1,0:T(8,128)(2,1)S(1)} %get-tuple-element.124.gf_ref, ...), custom_call_target="tpu_custom_call" | custom-call | flops 6000000000 | bytes 1048576 | tf_op jit(solution)/shard_map/wgrad/pallas_call | solution.py:336
  73.7 1.6 %collective-permute-start.11 = (bf16[544,512]{1,0:T(8,128)(2,1)S(1)}, bf16[544,512]{1,0:T(8,128)(2,1)S(1)}, u32[]{:S(2)}, u32[]{:S(2)}) collective-permute-start(bf16[544,512]{1,0:T(8,128)(2,1)S(1)} %add.63), channel_id=1, source_target_pairs={{0,1},{1,0},{2,3},{3,2},{4,5},{5,4},{6,7},{7,6},{8,9},{9,8},{10,11... | collective-permute-start | bytes 1671176 | tf_op jit(solution)/shard_map/ppermute | solution.py:461
  75.3 9.9 %attn_bwd.3 = (bf16[2,384,1024]{2,1,0:T(8,128)(2,1)}, bf16[544,512]{1,0:T(8,128)(2,1)S(1)}, bf16[544,512]{1,0:T(8,128)(2,1)S(1)}) custom-call(bf16[512,1024]{1,0:T(8,128)(2,1)S(1)} %get-tuple-element.82.xt_ref, bf16[2,384,1024]{2,1,0:T(8,128)(2,1)S(1)} %copy-done.12, bf16[2,128,1024]{2,1,0:T(8,128)(2,1)S(1)} %get-tuple-element.93.refs_0_.att_ref, ...), custom_call_target="tpu_custom_call" | custom-call | flops 11000000512 | bytes 1048576 | tf_op jit(solution)/shard_map/attn_bwd/pallas_call | solution.py:167
  85.2 3.3 %wgrad.3 = bf16[2,2,512,512]{3,2,1,0:T(8,128)(2,1)S(1)} custom-call(bf16[1024,1024]{1,0:T(8,128)(2,1)S(1)} %get-tuple-element.120.act_a_ref, bf16[1024,1024]{1,0:T(8,128)(2,1)S(1)} %get-tuple-element.121.act_b_ref, bf16[1024,2048]{1,0:T(8,128)(2,1)S(1)} %get-tuple-element.131.dh_ref, bf16[1024,512]{1,0:T(8,128)(2,1)S(1)} %get-tuple-element.124.gf_ref, ...), custom_call_target="tpu_custom_call" | custom-call | flops 6000000000 | bytes 1048576 | tf_op jit(solution)/shard_map/wgrad/pallas_call | solution.py:336
  92.1 3.8 %sgrad.1 = f32[1024,512]{1,0:T(8,128)} custom-call(f32[1024,512]{1,0:T(8,128)S(1)} %copy-done.8, bf16[2,384,1024]{2,1,0:T(8,128)(2,1)S(1)} %copy-done.10, bf16[2,384,1024]{2,1,0:T(8,128)(2,1)S(1)} %copy-done.9, bf16[512,512]{1,0:T(8,128)(2,1)S(1)} %get-tuple-element.90.w_ref.refs_2_.refs_0_, bf16[512,512]{1,0:T(8,128)(2,1)S(1)} %get-tuple-element.86.w_ref.refs_3_.refs_1_, ...), custom_call_target="tpu_custom_call" | custom-call | flops 4000000000 | bytes 1048576 | tf_op jit(solution)/shard_map/sgrad/pallas_call | solution.py:358
  95.8 2.3 %collective-permute-done.12 = bf16[272,512]{1,0:T(8,128)(2,1)S(1)} collective-permute-done((bf16[272,512]{1,0:T(8,128)(2,1)S(1)}, bf16[272,512]{1,0:T(8,128)(2,1)S(1)}, u32[]{:S(2)}, u32[]{:S(2)}) %collective-permute-start.12) | collective-permute-done | bytes 278560 | tf_op jit(solution)/shard_map/ppermute | solution.py:461
  98.5 4.9 %collective-permute-done.13 = bf16[136,512]{1,0:T(8,128)(2,1)S(1)} collective-permute-done((bf16[136,512]{1,0:T(8,128)(2,1)S(1)}, bf16[136,512]{1,0:T(8,128)(2,1)S(1)}, u32[]{:S(2)}, u32[]{:S(2)}) %collective-permute-start.13) | collective-permute-done | bytes 139296 | tf_op jit(solution)/shard_map/ppermute | solution.py:461
  103.4 2.0 %collective-permute-done.15 = bf16[2,512,512]{2,1,0:T(8,128)(2,1)S(1)} collective-permute-done((bf16[2,512,512]{2,1,0:T(8,128)(2,1)S(1)}, bf16[2,512,512]{2,1,0:T(8,128)(2,1)S(1)}, u32[]{:S(2)}, u32[]{:S(2)}) %collective-permute-start.15) | collective-permute-done | bytes 1048608 | tf_op jit(solution)/shard_map/ppermute | solution.py:461
  106.4 3.3 %collective-permute-start.14 = (bf16[136,512]{1,0:T(8,128)(2,1)S(1)}, bf16[136,512]{1,0:T(8,128)(2,1)S(1)}, u32[]{:S(2)}, u32[]{:S(2)}) collective-permute-start(bf16[136,512]{1,0:T(8,128)(2,1)S(1)} %select_add_fusion.1), channel_id=1, source_target_pairs={{0,16},{1,17},{2,18},{3,19},{4,20},{5,21},{6,22},{7,23},{8,24},{9,... | collective-permute-start | bytes 417800 | tf_op jit(solution)/shard_map/ppermute | solution.py:461
  109.7 6.4 %collective-permute-done.14 = bf16[136,512]{1,0:T(8,128)(2,1)S(1)} collective-permute-done((bf16[136,512]{1,0:T(8,128)(2,1)S(1)}, bf16[136,512]{1,0:T(8,128)(2,1)S(1)}, u32[]{:S(2)}, u32[]{:S(2)}) %collective-permute-start.14) | collective-permute-done | bytes 139296 | tf_op jit(solution)/shard_map/ppermute | solution.py:461
  116.1 3.8 %collective-permute-start.16 = (bf16[136,512]{1,0:T(8,128)(2,1)S(1)}, bf16[136,512]{1,0:T(8,128)(2,1)S(1)}, u32[]{:S(2)}, u32[]{:S(2)}) collective-permute-start(bf16[136,512]{1,0:T(8,128)(2,1)S(1)} %add.74), channel_id=1, source_target_pairs={{0,8},{1,9},{2,6},{3,7},{4,12},{5,13},{6,2},{7,3},{8,0},{9,1},{10,... | collective-permute-start | bytes 417800 | tf_op jit(solution)/shard_map/ppermute | solution.py:461
  120.6 3.9 %collective-permute-done.16 = bf16[136,512]{1,0:T(8,128)(2,1)S(1)} collective-permute-done((bf16[136,512]{1,0:T(8,128)(2,1)S(1)}, bf16[136,512]{1,0:T(8,128)(2,1)S(1)}, u32[]{:S(2)}, u32[]{:S(2)}) %collective-permute-start.16) | collective-permute-done | bytes 139296 | tf_op jit(solution)/shard_map/ppermute | solution.py:461
  126.9 4.3 %collective-permute-done.18 = bf16[272,512]{1,0:T(8,128)(2,1)S(1)} collective-permute-done((bf16[272,512]{1,0:T(8,128)(2,1)S(1)}, bf16[272,512]{1,0:T(8,128)(2,1)S(1)}, u32[]{:S(2)}, u32[]{:S(2)}) %collective-permute-start.18) | collective-permute-done | bytes 278560 | tf_op jit(solution)/shard_map/ppermute | solution.py:461
  131.5 2.0 %collective-permute-done.21 = bf16[2,64,512]{2,1,0:T(8,128)(2,1)S(1)} collective-permute-done((bf16[2,64,512]{2,1,0:T(8,128)(2,1)S(1)}, bf16[2,64,512]{2,1,0:T(8,128)(2,1)S(1)}, u32[]{:S(2)}, u32[]{:S(2)}) %collective-permute-start.21) | collective-permute-done | bytes 131104 | tf_op jit(solution)/shard_map/ppermute | solution.py:461
  (87 shorter events, 24.6 us)
Async XLA Ops:
  2.3 10.4 %collective-permute-start = (bf16[2,64,512]{2,1,0:T(8,128)(2,1)S(1)}, bf16[2,64,512]{2,1,0:T(8,128)(2,1)S(1)}, u32[]{:S(2)}, u32[]{:S(2)}) collective-permute-start(bf16[2,64,512]{2,1,0:T(8,128)(2,1)S(1)} %get-tuple-element.85), channel_id=1, source_target_pairs={{0,16},{1,17},{2,18},{3,19},{4,20},{5,21},{6,22},{7,23},{8,24},{9,... | collective-permute-start | bytes 393224 | tf_op jit(solution)/shard_map/ppermute | solution.py:461
  6.4 13.8 %collective-permute-start.1 = (bf16[512,512]{1,0:T(8,128)(2,1)S(1)}, bf16[512,512]{1,0:T(8,128)(2,1)S(1)}, u32[]{:S(2)}, u32[]{:S(2)}) collective-permute-start(bf16[512,512]{1,0:T(8,128)(2,1)S(1)} %get-tuple-element.86.w_ref.refs_3_.refs_1_), channel_id=1, source_target_pairs={{0,1},{1,0},{2,3},{3,2},{4,5},{5,4},{6,7},{7,6},{8,9},{9,8},{10,11... | collective-permute-start | bytes 1572872 | tf_op jit(solution)/shard_map/ppermute | solution.py:461
  12.7 6.4 %collective-permute-start.3 = (bf16[2,128,512]{2,1,0:T(8,128)(2,1)S(1)}, bf16[2,128,512]{2,1,0:T(8,128)(2,1)S(1)}, u32[]{:S(2)}, u32[]{:S(2)}) collective-permute-start(bf16[2,128,512]{2,1,0:T(8,128)(2,1)S(1)} %get-tuple-element.163), channel_id=1, source_target_pairs={{0,4},{1,5},{2,10},{3,11},{4,0},{5,1},{6,14},{7,15},{8,12},{9,13},... | collective-permute-start | bytes 786440 | tf_op jit(solution)/shard_map/ppermute | solution.py:461
  19.2 9.2 %collective-permute-start.4 = (bf16[2,256,512]{2,1,0:T(8,128)(2,1)S(1)}, bf16[2,256,512]{2,1,0:T(8,128)(2,1)S(1)}, u32[]{:S(2)}, u32[]{:S(2)}) collective-permute-start(bf16[2,256,512]{2,1,0:T(8,128)(2,1)S(1)} %get-tuple-element.159), channel_id=1, source_target_pairs={{0,8},{1,9},{2,3},{3,2},{4,12},{5,13},{6,7},{7,6},{8,0},{9,1},{10,... | collective-permute-start | bytes 1572872 | tf_op jit(solution)/shard_map/ppermute | solution.py:461
  28.5 7.8 %collective-permute-start.5 = (bf16[2,512,512]{2,1,0:T(8,128)(2,1)S(1)}, bf16[2,512,512]{2,1,0:T(8,128)(2,1)S(1)}, u32[]{:S(2)}, u32[]{:S(2)}) collective-permute-start(bf16[2,512,512]{2,1,0:T(8,128)(2,1)S(1)} %constant_dynamic-update-slice_fusion.5.refs_6_.refs_4_), channel_id=1, source_target_pairs={{0,2},{1,3},{2,0},{3,1},{4,6},{5,7},{6,4},{7,5},{8,10},{9,11},{10,... | collective-permute-start | bytes 3145736 | tf_op jit(solution)/shard_map/ppermute | solution.py:461
  28.5 3.4 %collective-permute-start.2 = (bf16[512,512]{1,0:T(8,128)(2,1)S(1)}, bf16[512,512]{1,0:T(8,128)(2,1)S(1)}, u32[]{:S(2)}, u32[]{:S(2)}) collective-permute-start(bf16[512,512]{1,0:T(8,128)(2,1)S(1)} %collective-permute-done.1.w_ref.refs_5_.refs_3_), channel_id=1, source_target_pairs={{0,2},{1,3},{2,0},{3,1},{4,6},{5,7},{6,4},{7,5},{8,10},{9,11},{10,... | collective-permute-start | bytes 1572872 | tf_op jit(solution)/shard_map/ppermute | solution.py:461
  29.0 14.8 %collective-permute-start.6 = (bf16[2,512,512]{2,1,0:T(8,128)(2,1)S(1)}, bf16[2,512,512]{2,1,0:T(8,128)(2,1)S(1)}, u32[]{:S(2)}, u32[]{:S(2)}) collective-permute-start(bf16[2,512,512]{2,1,0:T(8,128)(2,1)S(1)} %constant_dynamic-update-slice_fusion.5.refs_6_.refs_4_), channel_id=1, source_target_pairs={{0,1},{1,0},{2,6},{3,7},{4,5},{5,4},{6,2},{7,3},{8,9},{9,8},{10,14... | collective-permute-start | bytes 3145736 | tf_op jit(solution)/shard_map/ppermute | solution.py:461
  36.3 10.2 %copy-start.1 = (bf16[1024,512]{1,0:T(8,128)(2,1)S(1)}, bf16[1024,512]{1,0:T(8,128)(2,1)}, u32[]{:S(2)}) copy-start(bf16[1024,512]{1,0:T(8,128)(2,1)} %y_ref.1) | copy-start | bytes 3145732
  43.8 2.7 %collective-permute-start.7 = (bf16[2,512,512]{2,1,0:T(8,128)(2,1)S(1)}, bf16[2,512,512]{2,1,0:T(8,128)(2,1)S(1)}, u32[]{:S(2)}, u32[]{:S(2)}) collective-permute-start(bf16[2,512,512]{2,1,0:T(8,128)(2,1)S(1)} %collective-permute-done.6.refs_6_), channel_id=1, source_target_pairs={{0,2},{1,3},{2,0},{3,1},{4,6},{5,7},{6,4},{7,5},{8,10},{9,11},{10,... | collective-permute-start | bytes 3145736 | tf_op jit(solution)/shard_map/ppermute | solution.py:461
  46.5 13.2 %copy-start.11 = (bf16[2,384,1024]{2,1,0:T(8,128)(2,1)S(1)}, bf16[2,384,1024]{2,1,0:T(8,128)(2,1)}, u32[]{:S(2)}) copy-start(bf16[2,384,1024]{2,1,0:T(8,128)(2,1)} %get-tuple-element.113.qkv_ref) | copy-start | bytes 4718596
  69.6 3.9 %collective-permute-start.8 = (bf16[544,512]{1,0:T(8,128)(2,1)S(1)}, bf16[544,512]{1,0:T(8,128)(2,1)S(1)}, u32[]{:S(2)}, u32[]{:S(2)}) collective-permute-start(bf16[544,512]{1,0:T(8,128)(2,1)S(1)} %get-tuple-element.119), channel_id=1, source_target_pairs={{0,2},{1,3},{2,0},{3,1},{4,6},{5,7},{6,4},{7,5},{8,10},{9,11},{10,... | collective-permute-start | bytes 1671176 | tf_op jit(solution)/shard_map/ppermute | solution.py:461
  73.1 17.3 %collective-permute-start.9 = (bf16[2,2,512,512]{3,2,1,0:T(8,128)(2,1)S(1)}, bf16[2,2,512,512]{3,2,1,0:T(8,128)(2,1)S(1)}, u32[]{:S(2)}, u32[]{:S(2)}) collective-permute-start(bf16[2,2,512,512]{3,2,1,0:T(8,128)(2,1)S(1)} %wgrad.2), channel_id=1, source_target_pairs={{0,2},{1,3},{2,0},{3,1},{4,6},{5,7},{6,4},{7,5},{8,10},{9,11},{10,... | collective-permute-start | bytes 6291464 | tf_op jit(solution)/shard_map/ppermute | solution.py:461
  73.7 14.8 %collective-permute-start.11 = (bf16[544,512]{1,0:T(8,128)(2,1)S(1)}, bf16[544,512]{1,0:T(8,128)(2,1)S(1)}, u32[]{:S(2)}, u32[]{:S(2)}) collective-permute-start(bf16[544,512]{1,0:T(8,128)(2,1)S(1)} %add.63), channel_id=1, source_target_pairs={{0,1},{1,0},{2,3},{3,2},{4,5},{5,4},{6,7},{7,6},{8,9},{9,8},{10,11... | collective-permute-start | bytes 1671176 | tf_op jit(solution)/shard_map/ppermute | solution.py:461
  85.2 3.3 %collective-permute-start.10 = (bf16[544,512]{1,0:T(8,128)(2,1)S(1)}, bf16[544,512]{1,0:T(8,128)(2,1)S(1)}, u32[]{:S(2)}, u32[]{:S(2)}) collective-permute-start(bf16[544,512]{1,0:T(8,128)(2,1)S(1)} %get-tuple-element.133), channel_id=1, source_target_pairs={{0,2},{1,3},{2,0},{3,1},{4,6},{5,7},{6,4},{7,5},{8,10},{9,11},{10,... | collective-permute-start | bytes 1671176 | tf_op jit(solution)/shard_map/ppermute | solution.py:461
  88.8 9.3 %collective-permute-start.12 = (bf16[272,512]{1,0:T(8,128)(2,1)S(1)}, bf16[272,512]{1,0:T(8,128)(2,1)S(1)}, u32[]{:S(2)}, u32[]{:S(2)}) collective-permute-start(bf16[272,512]{1,0:T(8,128)(2,1)S(1)} %broadcast_select_fusion), channel_id=1, source_target_pairs={{0,4},{1,5},{2,10},{3,11},{4,0},{5,1},{6,14},{7,15},{8,12},{9,13},... | collective-permute-start | bytes 835592 | tf_op jit(solution)/shard_map/ppermute | solution.py:461
  90.6 14.9 %collective-permute-start.15 = (bf16[2,512,512]{2,1,0:T(8,128)(2,1)S(1)}, bf16[2,512,512]{2,1,0:T(8,128)(2,1)S(1)}, u32[]{:S(2)}, u32[]{:S(2)}) collective-permute-start(bf16[2,512,512]{2,1,0:T(8,128)(2,1)S(1)} %get-tuple-element.152), channel_id=1, source_target_pairs={{0,1},{1,0},{2,6},{3,7},{4,5},{5,4},{6,2},{7,3},{8,9},{9,8},{10,14... | collective-permute-start | bytes 3145736 | tf_op jit(solution)/shard_map/ppermute | solution.py:461
  98.2 5.1 %collective-permute-start.13 = (bf16[136,512]{1,0:T(8,128)(2,1)S(1)}, bf16[136,512]{1,0:T(8,128)(2,1)S(1)}, u32[]{:S(2)}, u32[]{:S(2)}) collective-permute-start(bf16[136,512]{1,0:T(8,128)(2,1)S(1)} %broadcast_select_fusion.1), channel_id=1, source_target_pairs={{0,8},{1,9},{2,6},{3,7},{4,12},{5,13},{6,2},{7,3},{8,0},{9,1},{10,... | collective-permute-start | bytes 417800 | tf_op jit(solution)/shard_map/ppermute | solution.py:461
  105.6 14.4 %collective-permute-start.17 = (bf16[2,256,512]{2,1,0:T(8,128)(2,1)S(1)}, bf16[2,256,512]{2,1,0:T(8,128)(2,1)S(1)}, u32[]{:S(2)}, u32[]{:S(2)}) collective-permute-start(bf16[2,256,512]{2,1,0:T(8,128)(2,1)S(1)} %get-tuple-element.154), channel_id=1, source_target_pairs={{0,8},{1,9},{2,3},{3,2},{4,12},{5,13},{6,7},{7,6},{8,0},{9,1},{10,... | collective-permute-start | bytes 1572872 | tf_op jit(solution)/shard_map/ppermute | solution.py:461
  106.4 9.7 %collective-permute-start.14 = (bf16[136,512]{1,0:T(8,128)(2,1)S(1)}, bf16[136,512]{1,0:T(8,128)(2,1)S(1)}, u32[]{:S(2)}, u32[]{:S(2)}) collective-permute-start(bf16[136,512]{1,0:T(8,128)(2,1)S(1)} %select_add_fusion.1), channel_id=1, source_target_pairs={{0,16},{1,17},{2,18},{3,19},{4,20},{5,21},{6,22},{7,23},{8,24},{9,... | collective-permute-start | bytes 417800 | tf_op jit(solution)/shard_map/ppermute | solution.py:461
  116.1 8.4 %collective-permute-start.16 = (bf16[136,512]{1,0:T(8,128)(2,1)S(1)}, bf16[136,512]{1,0:T(8,128)(2,1)S(1)}, u32[]{:S(2)}, u32[]{:S(2)}) collective-permute-start(bf16[136,512]{1,0:T(8,128)(2,1)S(1)} %add.74), channel_id=1, source_target_pairs={{0,8},{1,9},{2,6},{3,7},{4,12},{5,13},{6,2},{7,3},{8,0},{9,1},{10,... | collective-permute-start | bytes 417800 | tf_op jit(solution)/shard_map/ppermute | solution.py:461
  120.0 6.4 %collective-permute-start.19 = (bf16[2,128,512]{2,1,0:T(8,128)(2,1)S(1)}, bf16[2,128,512]{2,1,0:T(8,128)(2,1)S(1)}, u32[]{:S(2)}, u32[]{:S(2)}) collective-permute-start(bf16[2,128,512]{2,1,0:T(8,128)(2,1)S(1)} %get-tuple-element.156), channel_id=1, source_target_pairs={{0,4},{1,5},{2,10},{3,11},{4,0},{5,1},{6,14},{7,15},{8,12},{9,13},... | collective-permute-start | bytes 786440 | tf_op jit(solution)/shard_map/ppermute | solution.py:461
  124.6 6.6 %collective-permute-start.18 = (bf16[272,512]{1,0:T(8,128)(2,1)S(1)}, bf16[272,512]{1,0:T(8,128)(2,1)S(1)}, u32[]{:S(2)}, u32[]{:S(2)}) collective-permute-start(bf16[272,512]{1,0:T(8,128)(2,1)S(1)} %maximum_select_fusion.1), channel_id=1, source_target_pairs={{0,4},{1,5},{2,10},{3,11},{4,0},{5,1},{6,14},{7,15},{8,12},{9,13},... | collective-permute-start | bytes 835592 | tf_op jit(solution)/shard_map/ppermute | solution.py:461
  126.5 7.0 %collective-permute-start.21 = (bf16[2,64,512]{2,1,0:T(8,128)(2,1)S(1)}, bf16[2,64,512]{2,1,0:T(8,128)(2,1)S(1)}, u32[]{:S(2)}, u32[]{:S(2)}) collective-permute-start(bf16[2,64,512]{2,1,0:T(8,128)(2,1)S(1)} %slice_add_fusion.5), channel_id=1, source_target_pairs={{0,16},{1,17},{2,18},{3,19},{4,20},{5,21},{6,22},{7,23},{8,24},{9,... | collective-permute-start | bytes 393224 | tf_op jit(solution)/shard_map/ppermute | solution.py:461
  131.4 2.8 %collective-permute-start.20 = (bf16[544,512]{1,0:T(8,128)(2,1)S(1)}, bf16[544,512]{1,0:T(8,128)(2,1)S(1)}, u32[]{:S(2)}, u32[]{:S(2)}) collective-permute-start(bf16[544,512]{1,0:T(8,128)(2,1)S(1)} %maximum_select_fusion.mine_ref), channel_id=1, source_target_pairs={{0,2},{1,3},{2,0},{3,1},{4,6},{5,7},{6,4},{7,5},{8,10},{9,11},{10,... | collective-permute-start | bytes 1671176 | tf_op jit(solution)/shard_map/ppermute | solution.py:461
  (13 other events, 86.6 us)
where the time goes:
time: 137 us; the launch traced here: 136 us
  Pallas kernels  68.2 us (50%)
  waiting for transfers between devices  38.9 us (28%)
  starting transfers between devices  25.4 us (19%)
  local copies, waits for them, and re-layouts  1.55 us (1%)
    ppermute x22, waiting for transfers between devices, swap(): return lax.ppermute(value, ('dp', 'head'), pairs)  38.9 us
    ppermute x22, starting transfers between devices, swap(): return lax.ppermute(value, ('dp', 'head'), pairs)  25.4 us
    pallas_call x2, Pallas kernels, attn_bwd(): pl.pallas_call(functools.partial(attn_bwd_kernel, scale), grid=(2,), in_s...  19.8 us
    pallas_call x4, Pallas kernels, attn_fwd(): pl.pallas_call(functools.partial(attn_fwd_kernel, scale), grid=(1,), in_s...  15.3 us
    pallas_call x1, Pallas kernels, second_part(): pl.pallas_call(functools.partial(second_kernel, len(wo), len(ffa), len(ff...  13.2 us
    pallas_call x2, Pallas kernels, wgrad(): pl.pallas_call(wgrad_kernel, grid=(2,), in_specs=[half, half, pl.BlockSpe...  6.56 us
    pallas_call x1, Pallas kernels, first_part(): pl.pallas_call(functools.partial(first_kernel, len(wo), len(ffw)), grid=(...  5.99 us
    pallas_call x1, Pallas kernels, sgrad(): pl.pallas_call(functools.partial(sgrad_kernel, len(w)), grid=(seq // blk,...  3.75 us
  transfers between devices with their start and end apart: 22, of which 14 were waited for; matrix products, arithmetic and copies ran while one was open for 1% of the time, Pallas kernels for 31%

commit v1 on v0

--- a/solution.py
+++ b/solution.py
@@ -83,14 +83,20 @@
     return sum(seq - i * BLK for i in range(kb))
 
 
-def attn_fwd_kernel(scale, xt_ref, w_ref, mask_ref, *refs):
-    qkv_ref, att_ref, lse_ref = refs[-3:]
+def block_at(kb, qb):
+    at = qb * (qb + 1) // 2 + kb
+    return slice(at * BLK, (at + 1) * BLK)
+
+
+def attn_fwd_kernel(scale, slot, xt_ref, w_ref, mask_ref, *refs):
+    qkv_ref, att_ref, inv_ref, prob_hbm, prob_ref, sems = refs[-6:]
     seq = xt_ref.shape[1]
+    copies = []
     qkv_ref[...] = nn(w_ref[:3 * PAIR], xt_ref[...]).astype(BF)
     for h in range(2):
         head = lambda i: slice(i * PAIR + 64 * h, i * PAIR + 64 * h + 64)
         keys = qkv_ref[head(1), :].T
-        for qb in range(seq // BLK):
+        for qb in reversed(range(seq // BLK)):
             cols = slice(qb * BLK, (qb + 1) * BLK)
             q = qkv_ref[head(0), cols]
             scores = []
@@ -102,9 +108,17 @@
             for kb, s in enumerate(scores):
                 p = jnp.exp2(s - m)
                 l = l + jnp.sum(p, axis=0, keepdims=True)
-                out = out + nn(qkv_ref[head(2), kb * BLK:(kb + 1) * BLK], p.astype(BF))
-            att_ref[head(0), cols] = (out / l).astype(BF)
-            lse_ref[h:h + 1, cols] = m + jnp.log2(l)
+                p = p.astype(BF)
+                prob_ref[h, :, block_at(kb, qb)] = p
+                out = out + nn(qkv_ref[head(2), kb * BLK:(kb + 1) * BLK], p)
+            inv = 1.0 / l
+            att_ref[head(0), cols] = (out * inv).astype(BF)
+            inv_ref[h:h + 1, cols] = inv
+            span = slice(block_at(0, qb).start, block_at(qb, qb).stop)
+            copies.append(pltpu.make_async_copy(prob_ref.at[h, :, span], prob_hbm.at[slot, h, :, span], sems.at[len(copies)]))
+            copies[-1].start()
+    for copy in copies:
+        copy.wait()
 
 
 def attn_fwd(xt, w, mask, scale, slot, held=()):
@@ -112,37 +126,36 @@
     full = lambda shape: pl.BlockSpec(shape, lambda p: (0,) * len(shape))
     own = lambda rows: pl.BlockSpec((None, rows, seq), lambda p: (slot, 0, 0))
     return pl.pallas_call(
-        functools.partial(attn_fwd_kernel, scale),
+        functools.partial(attn_fwd_kernel, scale, slot),
         grid=(1,),
         in_specs=[full((width, seq)), full(w.shape), full(mask.shape)] + [pl.BlockSpec(memory_space=pl.ANY)] * len(held),
-        out_specs=[own(3 * PAIR), own(PAIR), own(2)],
-        out_shape=[pltpu.HBM((2, 3 * PAIR, seq), BF), jax.ShapeDtypeStruct((2, PAIR, seq), BF), jax.ShapeDtypeStruct((2, 2, seq), F32)],
+        out_specs=[own(3 * PAIR), own(PAIR), own(2), pl.BlockSpec(memory_space=pl.ANY)],
+        out_shape=[jax.ShapeDtypeStruct((2, 3 * PAIR, seq), BF), jax.ShapeDtypeStruct((2, PAIR, seq), BF), jax.ShapeDtypeStruct((2, 2, seq), F32), pltpu.HBM((2, 2, *mask.shape), BF)],
+        scratch_shapes=[pltpu.VMEM((2, *mask.shape), BF), pltpu.SemaphoreType.DMA((2 * (seq // BLK),))],
         input_output_aliases={3 + i: i for i in range(len(held))},
-        compiler_params=params(12),
+        compiler_params=params(16),
         cost_estimate=cost(5),
         name="attn_fwd",
     )(xt, w, mask, *held)
 
 
-def attn_bwd_kernel(scale, xt_ref, qkv_ref, att_ref, do_ref, gb_ref, lse_ref, vec_ref, mask_ref, g_ref, other_ref, mine_ref, pay_ref, dq_ref):
+def attn_bwd_kernel(scale, xt_ref, qkv_ref, att_ref, do_ref, gb_ref, inv_ref, vec_ref, prob_ref, g_ref, other_ref, mine_ref, pay_ref, dq_ref):
     width, seq = xt_ref.shape
     dq_ref[...] = jnp.zeros_like(dq_ref)
-
     for h in range(2):
         head = lambda i: slice(i * PAIR + 64 * h, i * PAIR + 64 * h + 64)
         own = head(0)
-        keys, values = qkv_ref[head(1), :].T, qkv_ref[head(2), :].T
-        delta = jnp.sum(do_ref[own, :].astype(F32) * att_ref[own, :].astype(F32), axis=0, keepdims=True)
-        lse = lse_ref[h:h + 1, :]
+        values = qkv_ref[head(2), :].T
+        scaled = do_ref[own, :].astype(F32) * inv_ref[h:h + 1, :]
+        delta = jnp.sum(scaled * att_ref[own, :].astype(F32), axis=0, keepdims=True)
+        scaled = scaled.astype(BF)
         for kb in range(seq // BLK):
             rows = slice(kb * BLK, (kb + 1) * BLK)
-            lo, at = kb * BLK, offset(kb, seq)
-            q, dout = qkv_ref[own, lo:], do_ref[own, lo:]
-            s = nn(keys[rows], q) * (scale * LOG2E) + mask_ref[:, at:at + seq - lo]
-            p = jnp.exp2(s - lse[:, lo:])
-            dp = nn(values[rows], dout)
-            ds = (p * (dp - delta[:, lo:])).astype(BF)
-            g_ref[head(2), rows] = nt(dout, p.astype(BF)).astype(BF)
+            lo = kb * BLK
+            q, dout = qkv_ref[own, lo:], scaled[:, lo:]
+            p = jnp.concatenate([prob_ref[h, :, block_at(kb, qb)] for qb in range(kb, seq // BLK)], axis=1)
+            ds = (p.astype(F32) * (nn(values[rows], dout) - delta[:, lo:])).astype(BF)
+            g_ref[head(2), rows] = nt(dout, p).astype(BF)
             g_ref[head(1), rows] = (nt(q, ds) * scale).astype(BF)
             dq_ref[own, lo:] += nn(qkv_ref[head(1), rows], ds)
     g_ref[0:PAIR, :] = (dq_ref[...] * scale).astype(BF)
@@ -159,7 +172,7 @@
         mine_ref[...] = pay_ref[...]
 
 
-def attn_bwd(xt, qkv, att, do, gb, lse, vec, mask, scale):
+def attn_bwd(xt, qkv, att, do, gb, inv, vec, prob, scale):
     width, seq = xt.shape
     full = lambda shape: pl.BlockSpec(shape, lambda p: (0,) * len(shape))
     own = lambda rows: pl.BlockSpec((None, rows, seq), lambda p: (p, 0, 0))
@@ -167,14 +180,14 @@
     return pl.pallas_call(
         functools.partial(attn_bwd_kernel, scale),
         grid=(2,),
-        in_specs=[full((width, seq)), own(3 * PAIR), own(PAIR), own(PAIR), full((width, seq)), own(2), full(vec.shape), full(mask.shape)],
+        in_specs=[full((width, seq)), own(3 * PAIR), own(PAIR), own(PAIR), full((width, seq)), own(2), full(vec.shape), pl.BlockSpec((None, *prob.shape[1:]), lambda p: (p, 0, 0, 0))],
         out_specs=[own(3 * PAIR), full(pay), full(pay)],
         out_shape=[pltpu.HBM((2, 3 * PAIR, seq), BF), jax.ShapeDtypeStruct(pay, BF), jax.ShapeDtypeStruct(pay, BF)],
         scratch_shapes=[pltpu.VMEM(pay, BF), pltpu.VMEM((PAIR, seq), F32)],
         compiler_params=params(16),
         cost_estimate=cost(11),
         name="attn_bwd",
-    )(xt, qkv, att, do, gb, lse, vec, mask)
+    )(xt, qkv, att, do, gb, inv, vec, prob)
 
 
 def gelu_parts(h):
@@ -236,7 +249,7 @@
     ffn_ref[...] = nn(act_ref[...], jnp.concatenate([w[1] for w in ffw], axis=0))
 
 
-def first_part(x, att, wo, ffw, g1, b1, blk=256):
+def first_part(x, att, wo, ffw, g1, b1, blk=512):
     seq, width = x.shape
     ff = sum(w.shape[1] for w in ffw)
     row, full = row_specs(blk)
@@ -300,7 +313,7 @@
     vec_ref[...] += jnp.concatenate([fold(gfirst * zhat1), fold(gfirst), fold(u * zhat2), fold(u), jnp.zeros((4, u.shape[1]), F32)], axis=0)
 
 
-def second_part(x, y, gs, gd, mixed, low, ffn, der, wo, ffa, ffb, g1, b1, g2, b2, blk=256):
+def second_part(x, y, gs, gd, mixed, low, ffn, der, wo, ffa, ffb, g1, b1, g2, b2, blk=512):
     seq, width = x.shape
     fa, fb = sum(w.shape[1] for w in ffa), sum(w.shape[1] for w in ffb)
     row, full = row_specs(blk)
@@ -392,7 +405,7 @@
     )(core.reshape(1), *map(here, (wq, wk, wv, wo, up, down)))
 
 
-def finish_kernel(core_ref, mine_ref, other_ref, dq_ref, dk_ref, dv_ref, og_ref, vec_ref):
+def finish_kernel(core_ref, mine_ref, other_ref, dq_ref, dk_ref, dv_ref, og_ref, *refs):
     width = dq_ref.shape[0]
     own = core_ref[0] == 0
     mine, other = mine_ref[...].astype(F32), other_ref[...].astype(F32)
@@ -403,21 +416,23 @@
         ref[:, PAIR:] = right[:width, cols]
     og_ref[:PAIR, :] = left[:width, 3 * PAIR:].T
     og_ref[PAIR:, :] = right[:width, 3 * PAIR:].T
-    vec_ref[...] = mine[width:width + 8]
+    for i in range(4):
+        refs[i][...] = mine[width + i:width + i + 1]
 
 
 def finish(core, mine, other):
     width = mine.shape[1]
     sd = lambda *shape: jax.ShapeDtypeStruct(shape, F32)
     vmem = pl.BlockSpec(memory_space=pltpu.VMEM)
-    return pl.pallas_call(
+    *dw, og, v0, v1, v2, v3 = pl.pallas_call(
         finish_kernel,
-        in_specs=[pl.BlockSpec(memory_space=pltpu.SMEM), vmem, vmem],
-        out_shape=[sd(width, 2 * PAIR)] * 3 + [sd(2 * PAIR, width), sd(8, width)],
+        in_specs=[pl.BlockSpec(memory_space=pltpu.SMEM)] + [vmem] * 2,
+        out_shape=[sd(width, 2 * PAIR)] * 3 + [sd(2 * PAIR, width)] + [sd(1, width)] * 4,
         compiler_params=params(8),
         cost_estimate=cost(3),
         name="finish",
     )(core.reshape(1), mine, other)
+    return dw, og, [v.reshape(width) for v in (v0, v1, v2, v3)]
 
 
 def after(value, *earlier):
@@ -522,8 +537,8 @@
     ffgrad = lambda which, *earlier: wgrad(act_a, act_b, after(dh, *earlier), gf, low, which)
 
     def bwd(group, do, *earlier):
-        qkv, att, lse = group
-        return attn_bwd(xt, qkv, att, after(do, *earlier), gb, lse, vec, mask, scale)
+        qkv, att, inv, prob = group
+        return attn_bwd(xt, qkv, att, after(do, *earlier), gb, inv, vec, prob, scale)
 
     def halves(own, received):
         n = own.shape[1] // 2
@@ -573,7 +588,7 @@
         whole = merge(first_low, whole, after(got, sent))
         got = swap(whole, core_step)
         part = part.astype(F32) + recv.astype(F32)
-        *dw, out_grad, vec = finish(core, whole, got)
+        dw, out_grad, vec = finish(core, whole, got)
     else:
         g_near, pay_near_other, pay_near = bwd(near, do_near)
         crossed = swap(ffgrad(1), core_step)

time: 137 us -> 134 us (0.978)
  Pallas kernels: 68.2 us -> 64.9 us
  starting transfers between devices: 25.4 us -> 28.2 us
  waiting for transfers between devices: 38.9 us -> 37.4 us
    pallas_call x2, Pallas kernels: 19.8 us -> 16.7 us  [attn_bwd(): pl.pallas_call(functools.partial(attn_bwd_kernel, scale), grid=(2,), in_s...]
    ppermute x22, starting transfers between devices: 25.4 us -> 28.2 us  [swap(): return lax.ppermute(value, ('dp', 'head'), pairs)]
    ppermute x22, waiting for transfers between devices: 38.9 us -> 37.4 us  [swap(): return lax.ppermute(value, ('dp', 'head'), pairs)]
    pallas_call x4, Pallas kernels: 15.3 us -> 16.8 us  [attn_fwd(): pl.pallas_call(functools.partial(attn_fwd_kernel, scale, slot), grid=(1,)...]
where the time goes in v1:
time: 134 us
  Pallas kernels  64.9 us (48%)
  waiting for transfers between devices  37.4 us (28%)
  starting transfers between devices  28.2 us (21%)
    ppermute x22, waiting for transfers between devices, swap(): return lax.ppermute(value, ('dp', 'head'), pairs)  37.4 us
    ppermute x22, starting transfers between devices, swap(): return lax.ppermute(value, ('dp', 'head'), pairs)  28.2 us
    pallas_call x4, Pallas kernels, attn_fwd(): pl.pallas_call(functools.partial(attn_fwd_kernel, scale, slot), grid=(1,)...  16.8 us
    pallas_call x2, Pallas kernels, attn_bwd(): pl.pallas_call(functools.partial(attn_bwd_kernel, scale), grid=(2,), in_s...  16.7 us
    pallas_call x1, Pallas kernels, second_part(): pl.pallas_call(functools.partial(second_kernel, len(wo), len(ffa), len(ff...  12.5 us
    pallas_call x2, Pallas kernels, wgrad(): pl.pallas_call(wgrad_kernel, grid=(2,), in_specs=[half, half, pl.BlockSpe...  6.56 us
    pallas_call x1, Pallas kernels, first_part(): pl.pallas_call(functools.partial(first_kernel, len(wo), len(ffw)), grid=(...  4.87 us
    pallas_call x1, Pallas kernels, sgrad(): pl.pallas_call(functools.partial(sgrad_kernel, len(w)), grid=(seq // blk,...  3.75 us
  transfers between devices with their start and end apart: 22, of which 14 were waited for; matrix products, arithmetic and copies ran while one was open for 1% of the time, Pallas kernels for 31%

profile of v1, /device:TPU:0, one launch (start us, length us, event | category | flops | bytes accessed | tf_op | source)
XLA Modules:
  0.0 133.7 jit_solution(9046790299133573022)
XLA Ops:
  2.3 4.1 %collective-permute-start = (bf16[2,64,512]{2,1,0:T(8,128)(2,1)S(1)}, bf16[2,64,512]{2,1,0:T(8,128)(2,1)S(1)}, u32[]{:S(2)}, u32[]{:S(2)}) collective-permute-start(bf16[2,64,512]{2,1,0:T(8,128)(2,1)S(1)} %get-tuple-element.92), channel_id=1, source_target_pairs={{0,16},{1,17},{2,18},{3,19},{4,20},{5,21},{6,22},{7,23},{8,24},{9,... | collective-permute-start | bytes 393224 | tf_op jit(solution)/shard_map/ppermute | solution.py:476
  8.5 4.2 %attn_fwd.4 = (bf16[2,384,1024]{2,1,0:T(8,128)(2,1)S(1)}, bf16[2,128,1024]{2,1,0:T(8,128)(2,1)S(1)}, f32[2,2,1024]{2,1,0:T(2,128)S(1)}, bf16[2,2,256,2560]{3,2,1,0:T(8,128)(2,1)}) custom-call(bf16[512,1024]{1,0:T(8,128)(2,1)S(1)} %get-tuple-element.89.xt_ref, bf16[512,512]{1,0:T(8,128)(2,1)S(1)} %get-tuple-element.93.w_ref.refs_3_.refs_1_, ...), custom_call_target="tpu_custom_call" | custom-call | flops 5000000000 | bytes 1048576 | tf_op jit(solution)/shard_map/attn_fwd/pallas_call | solution.py:128
  14.3 4.2 %attn_fwd.5 = (bf16[2,384,1024]{2,1,0:T(8,128)(2,1)S(1)}, bf16[2,128,1024]{2,1,0:T(8,128)(2,1)S(1)}, f32[2,2,1024]{2,1,0:T(2,128)S(1)}, bf16[2,2,256,2560]{3,2,1,0:T(8,128)(2,1)}) custom-call(bf16[512,1024]{1,0:T(8,128)(2,1)S(1)} %get-tuple-element.89.xt_ref, ...), custom_call_target="tpu_custom_call", output_to_operand_aliasing={{0}: (3, {}), {1}: (4, {}), {2}: (5, {}), {3}: (6, {})} | custom-call | flops 5000000000 | bytes 1048576 | tf_op jit(solution)/shard_map/attn_fwd/pallas_call | solution.py:128
  20.8 4.2 %attn_fwd.6 = (bf16[2,384,1024]{2,1,0:T(8,128)(2,1)S(1)}, bf16[2,128,1024]{2,1,0:T(8,128)(2,1)S(1)}, f32[2,2,1024]{2,1,0:T(2,128)S(1)}, bf16[2,2,256,2560]{3,2,1,0:T(8,128)(2,1)}) custom-call(bf16[512,1024]{1,0:T(8,128)(2,1)S(1)} %get-tuple-element.89.xt_ref, bf16[512,512]{1,0:T(8,128)(2,1)S(1)} %collective-permute-done.1.w_ref.refs_5_.refs_3_, ...), custom_call_target="tpu_custom_call" | custom-call | flops 5000000000 | bytes 1048576 | tf_op jit(solution)/shard_map/attn_fwd/pallas_call | solution.py:128
  25.0 3.4 %collective-permute-done.4 = bf16[2,256,512]{2,1,0:T(8,128)(2,1)S(1)} collective-permute-done((bf16[2,256,512]{2,1,0:T(8,128)(2,1)S(1)}, bf16[2,256,512]{2,1,0:T(8,128)(2,1)S(1)}, u32[]{:S(2)}, u32[]{:S(2)}) %collective-permute-start.4) | collective-permute-done | bytes 524320 | tf_op jit(solution)/shard_map/ppermute | solution.py:476
  32.0 4.3 %attn_fwd.7 = (bf16[2,384,1024]{2,1,0:T(8,128)(2,1)S(1)}, bf16[2,128,1024]{2,1,0:T(8,128)(2,1)S(1)}, f32[2,2,1024]{2,1,0:T(2,128)S(1)}, bf16[2,2,256,2560]{3,2,1,0:T(8,128)(2,1)}) custom-call(bf16[512,1024]{1,0:T(8,128)(2,1)S(1)} %get-tuple-element.89.xt_ref, ...), custom_call_target="tpu_custom_call", output_to_operand_aliasing={{0}: (3, {}), {1}: (4, {}), {2}: (5, {}), {3}: (6, {})} | custom-call | flops 5000000000 | bytes 1048576 | tf_op jit(solution)/shard_map/attn_fwd/pallas_call | solution.py:128
  36.4 4.9 %first_part.1 = (f32[1024,512]{1,0:T(8,128)S(1)}, bf16[1024,512]{1,0:T(8,128)(2,1)S(1)}, bf16[1024,1024]{1,0:T(8,128)(2,1)S(1)}, bf16[1024,1024]{1,0:T(8,128)(2,1)S(1)}, f32[1024,512]{1,0:T(8,128)S(1)}) custom-call(bf16[1024,512]{1,0:T(8,128)(2,1)S(1)} %copy-done, bf16[2,128,1024]{2,1,0:T(8,128)(2,1)S(1)} %get-tuple-element.101.refs_0_.att_ref, ...), custom_call_target="tpu_custom_call" | custom-call | flops 8000000000 | bytes 1048576 | tf_op jit(solution)/shard_map/first_part/pallas_call | solution.py:257
  41.3 2.6 %collective-permute-done.6.refs_6_ = bf16[2,512,512]{2,1,0:T(8,128)(2,1)S(1)} collective-permute-done((bf16[2,512,512]{2,1,0:T(8,128)(2,1)S(1)}, bf16[2,512,512]{2,1,0:T(8,128)(2,1)S(1)}, u32[]{:S(2)}, u32[]{:S(2)}) %collective-permute-start.6) | collective-permute-done | bytes 1048608 | tf_op jit(solution)/shard_map/ppermute | solution.py:476
  43.9 2.7 %collective-permute-done.7.refs_7_ = bf16[2,512,512]{2,1,0:T(8,128)(2,1)S(1)} collective-permute-done((bf16[2,512,512]{2,1,0:T(8,128)(2,1)S(1)}, bf16[2,512,512]{2,1,0:T(8,128)(2,1)S(1)}, u32[]{:S(2)}, u32[]{:S(2)}) %collective-permute-start.7) | collective-permute-done | bytes 1048608 | tf_op jit(solution)/shard_map/ppermute | solution.py:476
  46.6 12.5 %second_part.1 = (bf16[1024,512]{1,0:T(8,128)(2,1)}, bf16[1024,512]{1,0:T(8,128)(2,1)}, bf16[1024,1024]{1,0:T(8,128)(2,1)S(1)}, bf16[1024,2048]{1,0:T(8,128)(2,1...) custom-call(bf16[1024,512]{1,0:T(8,128)(2,1)S(1)} %copy-done, ...), custom_call_target="tpu_custom_call" | custom-call | flops 17999998976 | bytes 1048576 | tf_op jit(solution)/shard_map/second_part/pallas_call | solution.py:321
  59.1 8.4 %attn_bwd.2 = (bf16[2,384,1024]{2,1,0:T(8,128)(2,1)}, bf16[544,512]{1,0:T(8,128)(2,1)S(1)}, bf16[544,512]{1,0:T(8,128)(2,1)S(1)}) custom-call(bf16[512,1024]{1,0:T(8,128)(2,1)S(1)} %get-tuple-element.89.xt_ref, bf16[2,384,1024]{2,1,0:T(8,128)(2,1)S(1)} %get-tuple-element.122.qkv_ref, bf16[2,128,1024]{2,1,0:T(8,128)(2,1)S(1)} %get-tuple-element.111.refs_1_.att_ref, ...), custom_call_target="tpu_custom_call" | custom-call | flops 11000000512 | bytes 1048576 | tf_op jit(solution)/shard_map/attn_bwd/pallas_call | solution.py:180
  67.6 3.3 %wgrad.2 = bf16[2,2,512,512]{3,2,1,0:T(8,128)(2,1)S(1)} custom-call(bf16[1024,1024]{1,0:T(8,128)(2,1)S(1)} %get-tuple-element.130.act_a_ref, bf16[1024,1024]{1,0:T(8,128)(2,1)S(1)} %get-tuple-element.131.act_b_ref, bf16[1024,2048]{1,0:T(8,128)(2,1)S(1)} %get-tuple-element.142.dh_ref, bf16[1024,512]{1,0:T(8,128)(2,1)S(1)} %get-tuple-element.134.gf_ref, ...), custom_call_target="tpu_custom_call" | custom-call | flops 6000000000 | bytes 1048576 | tf_op jit(solution)/shard_map/wgrad/pallas_call | solution.py:349
  73.1 8.4 %attn_bwd.3 = (bf16[2,384,1024]{2,1,0:T(8,128)(2,1)}, bf16[544,512]{1,0:T(8,128)(2,1)S(1)}, bf16[544,512]{1,0:T(8,128)(2,1)S(1)}) custom-call(bf16[512,1024]{1,0:T(8,128)(2,1)S(1)} %get-tuple-element.89.xt_ref, bf16[2,384,1024]{2,1,0:T(8,128)(2,1)S(1)} %get-tuple-element.120.qkv_ref, bf16[2,128,1024]{2,1,0:T(8,128)(2,1)S(1)} %get-tuple-element.101.refs_0_.att_ref, ...), custom_call_target="tpu_custom_call" | custom-call | flops 11000000512 | bytes 1048576 | tf_op jit(solution)/shard_map/attn_bwd/pallas_call | solution.py:180
  81.5 3.3 %wgrad.3 = bf16[2,2,512,512]{3,2,1,0:T(8,128)(2,1)S(1)} custom-call(bf16[1024,1024]{1,0:T(8,128)(2,1)S(1)} %get-tuple-element.130.act_a_ref, bf16[1024,1024]{1,0:T(8,128)(2,1)S(1)} %get-tuple-element.131.act_b_ref, bf16[1024,2048]{1,0:T(8,128)(2,1)S(1)} %get-tuple-element.142.dh_ref, bf16[1024,512]{1,0:T(8,128)(2,1)S(1)} %get-tuple-element.134.gf_ref, ...), custom_call_target="tpu_custom_call" | custom-call | flops 6000000000 | bytes 1048576 | tf_op jit(solution)/shard_map/wgrad/pallas_call | solution.py:349
  89.9 3.8 %sgrad.1 = f32[1024,512]{1,0:T(8,128)} custom-call(f32[1024,512]{1,0:T(8,128)S(1)} %copy-done.8, bf16[2,384,1024]{2,1,0:T(8,128)(2,1)S(1)} %copy-done.10, bf16[2,384,1024]{2,1,0:T(8,128)(2,1)S(1)} %copy-done.9, bf16[512,512]{1,0:T(8,128)(2,1)S(1)} %get-tuple-element.97.w_ref.refs_2_.refs_0_, bf16[512,512]{1,0:T(8,128)(2,1)S(1)} %get-tuple-element.93.w_ref.refs_3_.refs_1_, ...), custom_call_target="tpu_custom_call" | custom-call | flops 4000000000 | bytes 1048576 | tf_op jit(solution)/shard_map/sgrad/pallas_call | solution.py:371
  93.7 2.4 %collective-permute-done.12 = bf16[272,512]{1,0:T(8,128)(2,1)S(1)} collective-permute-done((bf16[272,512]{1,0:T(8,128)(2,1)S(1)}, bf16[272,512]{1,0:T(8,128)(2,1)S(1)}, u32[]{:S(2)}, u32[]{:S(2)}) %collective-permute-start.12) | collective-permute-done | bytes 278560 | tf_op jit(solution)/shard_map/ppermute | solution.py:476
  97.9 3.5 %collective-permute-done.13 = bf16[136,512]{1,0:T(8,128)(2,1)S(1)} collective-permute-done((bf16[136,512]{1,0:T(8,128)(2,1)S(1)}, bf16[136,512]{1,0:T(8,128)(2,1)S(1)}, u32[]{:S(2)}, u32[]{:S(2)}) %collective-permute-start.13) | collective-permute-done | bytes 139296 | tf_op jit(solution)/shard_map/ppermute | solution.py:476
  101.4 1.8 %collective-permute-done.15 = bf16[2,512,512]{2,1,0:T(8,128)(2,1)S(1)} collective-permute-done((bf16[2,512,512]{2,1,0:T(8,128)(2,1)S(1)}, bf16[2,512,512]{2,1,0:T(8,128)(2,1)S(1)}, u32[]{:S(2)}, u32[]{:S(2)}) %collective-permute-start.15) | collective-permute-done | bytes 1048608 | tf_op jit(solution)/shard_map/ppermute | solution.py:476
  104.9 2.5 %collective-permute-start.14 = (bf16[136,512]{1,0:T(8,128)(2,1)S(1)}, bf16[136,512]{1,0:T(8,128)(2,1)S(1)}, u32[]{:S(2)}, u32[]{:S(2)}) collective-permute-start(bf16[136,512]{1,0:T(8,128)(2,1)S(1)} %select_add_fusion.1), channel_id=1, source_target_pairs={{0,16},{1,17},{2,18},{3,19},{4,20},{5,21},{6,22},{7,23},{8,24},{9,... | collective-permute-start | bytes 417800 | tf_op jit(solution)/shard_map/ppermute | solution.py:476
  107.4 7.2 %collective-permute-done.14 = bf16[136,512]{1,0:T(8,128)(2,1)S(1)} collective-permute-done((bf16[136,512]{1,0:T(8,128)(2,1)S(1)}, bf16[136,512]{1,0:T(8,128)(2,1)S(1)}, u32[]{:S(2)}, u32[]{:S(2)}) %collective-permute-start.14) | collective-permute-done | bytes 139296 | tf_op jit(solution)/shard_map/ppermute | solution.py:476
  114.6 3.0 %collective-permute-start.16 = (bf16[136,512]{1,0:T(8,128)(2,1)S(1)}, bf16[136,512]{1,0:T(8,128)(2,1)S(1)}, u32[]{:S(2)}, u32[]{:S(2)}) collective-permute-start(bf16[136,512]{1,0:T(8,128)(2,1)S(1)} %add.74), channel_id=1, source_target_pairs={{0,8},{1,9},{2,6},{3,7},{4,12},{5,13},{6,2},{7,3},{8,0},{9,1},{10,... | collective-permute-start | bytes 417800 | tf_op jit(solution)/shard_map/ppermute | solution.py:476
  118.3 3.4 %collective-permute-done.16 = bf16[136,512]{1,0:T(8,128)(2,1)S(1)} collective-permute-done((bf16[136,512]{1,0:T(8,128)(2,1)S(1)}, bf16[136,512]{1,0:T(8,128)(2,1)S(1)}, u32[]{:S(2)}, u32[]{:S(2)}) %collective-permute-start.16) | collective-permute-done | bytes 139296 | tf_op jit(solution)/shard_map/ppermute | solution.py:476
  125.5 3.0 %collective-permute-done.18 = bf16[272,512]{1,0:T(8,128)(2,1)S(1)} collective-permute-done((bf16[272,512]{1,0:T(8,128)(2,1)S(1)}, bf16[272,512]{1,0:T(8,128)(2,1)S(1)}, u32[]{:S(2)}, u32[]{:S(2)}) %collective-permute-start.18) | collective-permute-done | bytes 278560 | tf_op jit(solution)/shard_map/ppermute | solution.py:476
  128.7 2.7 %collective-permute-done.21 = bf16[2,64,512]{2,1,0:T(8,128)(2,1)S(1)} collective-permute-done((bf16[2,64,512]{2,1,0:T(8,128)(2,1)S(1)}, bf16[2,64,512]{2,1,0:T(8,128)(2,1)S(1)}, u32[]{:S(2)}, u32[]{:S(2)}) %collective-permute-start.21) | collective-permute-done | bytes 131104 | tf_op jit(solution)/shard_map/ppermute | solution.py:476
  (92 shorter events, 29.2 us)
Async XLA Ops:
  2.3 10.4 %collective-permute-start = (bf16[2,64,512]{2,1,0:T(8,128)(2,1)S(1)}, bf16[2,64,512]{2,1,0:T(8,128)(2,1)S(1)}, u32[]{:S(2)}, u32[]{:S(2)}) collective-permute-start(bf16[2,64,512]{2,1,0:T(8,128)(2,1)S(1)} %get-tuple-element.92), channel_id=1, source_target_pairs={{0,16},{1,17},{2,18},{3,19},{4,20},{5,21},{6,22},{7,23},{8,24},{9,... | collective-permute-start | bytes 393224 | tf_op jit(solution)/shard_map/ppermute | solution.py:476
  6.4 14.5 %collective-permute-start.1 = (bf16[512,512]{1,0:T(8,128)(2,1)S(1)}, bf16[512,512]{1,0:T(8,128)(2,1)S(1)}, u32[]{:S(2)}, u32[]{:S(2)}) collective-permute-start(bf16[512,512]{1,0:T(8,128)(2,1)S(1)} %get-tuple-element.93.w_ref.refs_3_.refs_1_), channel_id=1, source_target_pairs={{0,1},{1,0},{2,3},{3,2},{4,5},{5,4},{6,7},{7,6},{8,9},{9,8},{10,11... | collective-permute-start | bytes 1572872 | tf_op jit(solution)/shard_map/ppermute | solution.py:476
  12.7 6.4 %collective-permute-start.3 = (bf16[2,128,512]{2,1,0:T(8,128)(2,1)S(1)}, bf16[2,128,512]{2,1,0:T(8,128)(2,1)S(1)}, u32[]{:S(2)}, u32[]{:S(2)}) collective-permute-start(bf16[2,128,512]{2,1,0:T(8,128)(2,1)S(1)} %get-tuple-element.177), channel_id=1, source_target_pairs={{0,4},{1,5},{2,10},{3,11},{4,0},{5,1},{6,14},{7,15},{8,12},{9,13},... | collective-permute-start | bytes 786440 | tf_op jit(solution)/shard_map/ppermute | solution.py:476
  19.2 9.2 %collective-permute-start.4 = (bf16[2,256,512]{2,1,0:T(8,128)(2,1)S(1)}, bf16[2,256,512]{2,1,0:T(8,128)(2,1)S(1)}, u32[]{:S(2)}, u32[]{:S(2)}) collective-permute-start(bf16[2,256,512]{2,1,0:T(8,128)(2,1)S(1)} %get-tuple-element.173), channel_id=1, source_target_pairs={{0,8},{1,9},{2,3},{3,2},{4,12},{5,13},{6,7},{7,6},{8,0},{9,1},{10,... | collective-permute-start | bytes 1572872 | tf_op jit(solution)/shard_map/ppermute | solution.py:476
  28.5 7.8 %collective-permute-start.5 = (bf16[2,512,512]{2,1,0:T(8,128)(2,1)S(1)}, bf16[2,512,512]{2,1,0:T(8,128)(2,1)S(1)}, u32[]{:S(2)}, u32[]{:S(2)}) collective-permute-start(bf16[2,512,512]{2,1,0:T(8,128)(2,1)S(1)} %constant_dynamic-update-slice_fusion.5.refs_6_.refs_4_), channel_id=1, source_target_pairs={{0,2},{1,3},{2,0},{3,1},{4,6},{5,7},{6,4},{7,5},{8,10},{9,11},{10,... | collective-permute-start | bytes 3145736 | tf_op jit(solution)/shard_map/ppermute | solution.py:476
  28.6 3.4 %collective-permute-start.2 = (bf16[512,512]{1,0:T(8,128)(2,1)S(1)}, bf16[512,512]{1,0:T(8,128)(2,1)S(1)}, u32[]{:S(2)}, u32[]{:S(2)}) collective-permute-start(bf16[512,512]{1,0:T(8,128)(2,1)S(1)} %collective-permute-done.1.w_ref.refs_5_.refs_3_), channel_id=1, source_target_pairs={{0,2},{1,3},{2,0},{3,1},{4,6},{5,7},{6,4},{7,5},{8,10},{9,11},{10,... | collective-permute-start | bytes 1572872 | tf_op jit(solution)/shard_map/ppermute | solution.py:476
  29.1 14.8 %collective-permute-start.6 = (bf16[2,512,512]{2,1,0:T(8,128)(2,1)S(1)}, bf16[2,512,512]{2,1,0:T(8,128)(2,1)S(1)}, u32[]{:S(2)}, u32[]{:S(2)}) collective-permute-start(bf16[2,512,512]{2,1,0:T(8,128)(2,1)S(1)} %constant_dynamic-update-slice_fusion.5.refs_6_.refs_4_), channel_id=1, source_target_pairs={{0,1},{1,0},{2,6},{3,7},{4,5},{5,4},{6,2},{7,3},{8,9},{9,8},{10,14... | collective-permute-start | bytes 3145736 | tf_op jit(solution)/shard_map/ppermute | solution.py:476
  36.4 36.7 %slice-start.2 = ((s8[5242880]{0:T(1024)(128)(4,1)}), s8[4194304]{0:T(1024)(128)(4,1)S(1)}, s32[]{:S(2)}) async-start(s8[5242880]{0:T(1024)(128)(4,1)} %bitcast.27), calls=%async_computation.2 | async-start | bytes 8388608
  43.9 2.7 %collective-permute-start.7 = (bf16[2,512,512]{2,1,0:T(8,128)(2,1)S(1)}, bf16[2,512,512]{2,1,0:T(8,128)(2,1)S(1)}, u32[]{:S(2)}, u32[]{:S(2)}) collective-permute-start(bf16[2,512,512]{2,1,0:T(8,128)(2,1)S(1)} %collective-permute-done.6.refs_6_), channel_id=1, source_target_pairs={{0,2},{1,3},{2,0},{3,1},{4,6},{5,7},{6,4},{7,5},{8,10},{9,11},{10,... | collective-permute-start | bytes 3145736 | tf_op jit(solution)/shard_map/ppermute | solution.py:476
  46.6 26.5 %slice-start.3 = ((s8[5242880]{0:T(1024)(128)(4,1)}), s8[1048576]{0:T(1024)(128)(4,1)S(1)}, s32[]{:S(2)}) async-start(s8[5242880]{0:T(1024)(128)(4,1)} %bitcast.27), calls=%async_computation.3 | async-start | bytes 2097152
  67.5 3.9 %collective-permute-start.8 = (bf16[544,512]{1,0:T(8,128)(2,1)S(1)}, bf16[544,512]{1,0:T(8,128)(2,1)S(1)}, u32[]{:S(2)}, u32[]{:S(2)}) collective-permute-start(bf16[544,512]{1,0:T(8,128)(2,1)S(1)} %get-tuple-element.129), channel_id=1, source_target_pairs={{0,2},{1,3},{2,0},{3,1},{4,6},{5,7},{6,4},{7,5},{8,10},{9,11},{10,... | collective-permute-start | bytes 1671176 | tf_op jit(solution)/shard_map/ppermute | solution.py:476
  70.9 17.2 %collective-permute-start.9 = (bf16[2,2,512,512]{3,2,1,0:T(8,128)(2,1)S(1)}, bf16[2,2,512,512]{3,2,1,0:T(8,128)(2,1)S(1)}, u32[]{:S(2)}, u32[]{:S(2)}) collective-permute-start(bf16[2,2,512,512]{3,2,1,0:T(8,128)(2,1)S(1)} %wgrad.2), channel_id=1, source_target_pairs={{0,2},{1,3},{2,0},{3,1},{4,6},{5,7},{6,4},{7,5},{8,10},{9,11},{10,... | collective-permute-start | bytes 6291464 | tf_op jit(solution)/shard_map/ppermute | solution.py:476
  71.5 14.7 %collective-permute-start.11 = (bf16[544,512]{1,0:T(8,128)(2,1)S(1)}, bf16[544,512]{1,0:T(8,128)(2,1)S(1)}, u32[]{:S(2)}, u32[]{:S(2)}) collective-permute-start(bf16[544,512]{1,0:T(8,128)(2,1)S(1)} %add.63), channel_id=1, source_target_pairs={{0,1},{1,0},{2,3},{3,2},{4,5},{5,4},{6,7},{7,6},{8,9},{9,8},{10,11... | collective-permute-start | bytes 1671176 | tf_op jit(solution)/shard_map/ppermute | solution.py:476
  81.5 3.3 %collective-permute-start.10 = (bf16[544,512]{1,0:T(8,128)(2,1)S(1)}, bf16[544,512]{1,0:T(8,128)(2,1)S(1)}, u32[]{:S(2)}, u32[]{:S(2)}) collective-permute-start(bf16[544,512]{1,0:T(8,128)(2,1)S(1)} %get-tuple-element.144), channel_id=1, source_target_pairs={{0,2},{1,3},{2,0},{3,1},{4,6},{5,7},{6,4},{7,5},{8,10},{9,11},{10,... | collective-permute-start | bytes 1671176 | tf_op jit(solution)/shard_map/ppermute | solution.py:476
  86.5 9.6 %collective-permute-start.12 = (bf16[272,512]{1,0:T(8,128)(2,1)S(1)}, bf16[272,512]{1,0:T(8,128)(2,1)S(1)}, u32[]{:S(2)}, u32[]{:S(2)}) collective-permute-start(bf16[272,512]{1,0:T(8,128)(2,1)S(1)} %broadcast_select_fusion), channel_id=1, source_target_pairs={{0,4},{1,5},{2,10},{3,11},{4,0},{5,1},{6,14},{7,15},{8,12},{9,13},... | collective-permute-start | bytes 835592 | tf_op jit(solution)/shard_map/ppermute | solution.py:476
  88.3 14.9 %collective-permute-start.15 = (bf16[2,512,512]{2,1,0:T(8,128)(2,1)S(1)}, bf16[2,512,512]{2,1,0:T(8,128)(2,1)S(1)}, u32[]{:S(2)}, u32[]{:S(2)}) collective-permute-start(bf16[2,512,512]{2,1,0:T(8,128)(2,1)S(1)} %get-tuple-element.166), channel_id=1, source_target_pairs={{0,1},{1,0},{2,6},{3,7},{4,5},{5,4},{6,2},{7,3},{8,9},{9,8},{10,14... | collective-permute-start | bytes 3145736 | tf_op jit(solution)/shard_map/ppermute | solution.py:476
  96.2 5.1 %collective-permute-start.13 = (bf16[136,512]{1,0:T(8,128)(2,1)S(1)}, bf16[136,512]{1,0:T(8,128)(2,1)S(1)}, u32[]{:S(2)}, u32[]{:S(2)}) collective-permute-start(bf16[136,512]{1,0:T(8,128)(2,1)S(1)} %broadcast_select_fusion.1), channel_id=1, source_target_pairs={{0,8},{1,9},{2,6},{3,7},{4,12},{5,13},{6,2},{7,3},{8,0},{9,1},{10,... | collective-permute-start | bytes 417800 | tf_op jit(solution)/shard_map/ppermute | solution.py:476
  103.3 14.4 %collective-permute-start.17 = (bf16[2,256,512]{2,1,0:T(8,128)(2,1)S(1)}, bf16[2,256,512]{2,1,0:T(8,128)(2,1)S(1)}, u32[]{:S(2)}, u32[]{:S(2)}) collective-permute-start(bf16[2,256,512]{2,1,0:T(8,128)(2,1)S(1)} %get-tuple-element.168), channel_id=1, source_target_pairs={{0,8},{1,9},{2,3},{3,2},{4,12},{5,13},{6,7},{7,6},{8,0},{9,1},{10,... | collective-permute-start | bytes 1572872 | tf_op jit(solution)/shard_map/ppermute | solution.py:476
  104.9 9.7 %collective-permute-start.14 = (bf16[136,512]{1,0:T(8,128)(2,1)S(1)}, bf16[136,512]{1,0:T(8,128)(2,1)S(1)}, u32[]{:S(2)}, u32[]{:S(2)}) collective-permute-start(bf16[136,512]{1,0:T(8,128)(2,1)S(1)} %select_add_fusion.1), channel_id=1, source_target_pairs={{0,16},{1,17},{2,18},{3,19},{4,20},{5,21},{6,22},{7,23},{8,24},{9,... | collective-permute-start | bytes 417800 | tf_op jit(solution)/shard_map/ppermute | solution.py:476
  114.6 7.1 %collective-permute-start.16 = (bf16[136,512]{1,0:T(8,128)(2,1)S(1)}, bf16[136,512]{1,0:T(8,128)(2,1)S(1)}, u32[]{:S(2)}, u32[]{:S(2)}) collective-permute-start(bf16[136,512]{1,0:T(8,128)(2,1)S(1)} %add.74), channel_id=1, source_target_pairs={{0,8},{1,9},{2,6},{3,7},{4,12},{5,13},{6,2},{7,3},{8,0},{9,1},{10,... | collective-permute-start | bytes 417800 | tf_op jit(solution)/shard_map/ppermute | solution.py:476
  117.8 6.4 %collective-permute-start.19 = (bf16[2,128,512]{2,1,0:T(8,128)(2,1)S(1)}, bf16[2,128,512]{2,1,0:T(8,128)(2,1)S(1)}, u32[]{:S(2)}, u32[]{:S(2)}) collective-permute-start(bf16[2,128,512]{2,1,0:T(8,128)(2,1)S(1)} %get-tuple-element.170), channel_id=1, source_target_pairs={{0,4},{1,5},{2,10},{3,11},{4,0},{5,1},{6,14},{7,15},{8,12},{9,13},... | collective-permute-start | bytes 786440 | tf_op jit(solution)/shard_map/ppermute | solution.py:476
  121.8 6.6 %collective-permute-start.18 = (bf16[272,512]{1,0:T(8,128)(2,1)S(1)}, bf16[272,512]{1,0:T(8,128)(2,1)S(1)}, u32[]{:S(2)}, u32[]{:S(2)}) collective-permute-start(bf16[272,512]{1,0:T(8,128)(2,1)S(1)} %maximum_select_fusion.1), channel_id=1, source_target_pairs={{0,4},{1,5},{2,10},{3,11},{4,0},{5,1},{6,14},{7,15},{8,12},{9,13},... | collective-permute-start | bytes 835592 | tf_op jit(solution)/shard_map/ppermute | solution.py:476
  124.2 7.2 %collective-permute-start.21 = (bf16[2,64,512]{2,1,0:T(8,128)(2,1)S(1)}, bf16[2,64,512]{2,1,0:T(8,128)(2,1)S(1)}, u32[]{:S(2)}, u32[]{:S(2)}) collective-permute-start(bf16[2,64,512]{2,1,0:T(8,128)(2,1)S(1)} %slice_add_fusion.5), channel_id=1, source_target_pairs={{0,16},{1,17},{2,18},{3,19},{4,20},{5,21},{6,22},{7,23},{8,24},{9,... | collective-permute-start | bytes 393224 | tf_op jit(solution)/shard_map/ppermute | solution.py:476
  128.7 3.5 %collective-permute-start.20 = (bf16[544,512]{1,0:T(8,128)(2,1)S(1)}, bf16[544,512]{1,0:T(8,128)(2,1)S(1)}, u32[]{:S(2)}, u32[]{:S(2)}) collective-permute-start(bf16[544,512]{1,0:T(8,128)(2,1)S(1)} %maximum_select_fusion.mine_ref), channel_id=1, source_target_pairs={{0,2},{1,3},{2,0},{3,1},{4,6},{5,7},{6,4},{7,5},{8,10},{9,11},{10,... | collective-permute-start | bytes 1671176 | tf_op jit(solution)/shard_map/ppermute | solution.py:476
  (15 other events, 126.9 us)

commit v2 on v1

--- a/solution.py
+++ b/solution.py
@@ -17,6 +17,9 @@
 MIB = 1 << 20
 PAIR = 128
 EXTRA = 32
+STREAM = 512
+LIM1 = 12
+LIM2 = 16
 VMEM = 58
 
 
@@ -133,7 +136,7 @@
         out_shape=[jax.ShapeDtypeStruct((2, 3 * PAIR, seq), BF), jax.ShapeDtypeStruct((2, PAIR, seq), BF), jax.ShapeDtypeStruct((2, 2, seq), F32), pltpu.HBM((2, 2, *mask.shape), BF)],
         scratch_shapes=[pltpu.VMEM((2, *mask.shape), BF), pltpu.SemaphoreType.DMA((2 * (seq // BLK),))],
         input_output_aliases={3 + i: i for i in range(len(held))},
-        compiler_params=params(16),
+        compiler_params=params(12),
         cost_estimate=cost(5),
         name="attn_fwd",
     )(xt, w, mask, *held)
@@ -184,7 +187,7 @@
         out_specs=[own(3 * PAIR), full(pay), full(pay)],
         out_shape=[pltpu.HBM((2, 3 * PAIR, seq), BF), jax.ShapeDtypeStruct(pay, BF), jax.ShapeDtypeStruct(pay, BF)],
         scratch_shapes=[pltpu.VMEM(pay, BF), pltpu.VMEM((PAIR, seq), F32)],
-        compiler_params=params(16),
+        compiler_params=params(12),
         cost_estimate=cost(11),
         name="attn_bwd",
     )(xt, qkv, att, do, gb, inv, vec, prob)
@@ -228,28 +231,33 @@
     return pl.BlockSpec((PAIR, width), lambda p: (3, 0))
 
 
-def first_kernel(pairs, pieces, x_ref, *refs):
+def first_kernel(pairs, pieces, x_ref, y_ref, *refs):
     att, refs = refs[:pairs // 2], refs[pairs // 2:]
     wo, refs = refs[:pairs], refs[pairs:]
     ffw, refs = refs[:pieces], refs[pieces:]
-    g1_ref, b1_ref, mixed_ref, low_ref, act_ref, der_ref, ffn_ref = refs
+    g1_ref, b1_ref, low_ref, act_ref, der_ref, zhat_ref, rstd_ref, sum_ref, dual_ref = refs
     branch = nn(joined(att).T, jnp.concatenate([w[...] for w in wo], axis=0))
-    mixed = x_ref[...].astype(F32) + branch
-    mixed_ref[...] = mixed
-    zhat, _ = normed(mixed)
-    low = (zhat * g1_ref[...] + b1_ref[...]).astype(BF)
+    zhat, rstd = normed(x_ref[...].astype(F32) + branch)
+    zhat_ref[...] = zhat.astype(BF)
+    rstd_ref[...] = jnp.broadcast_to(rstd, rstd_ref.shape)
+    first = zhat * g1_ref[...] + b1_ref[...]
+    low = first.astype(BF)
     low_ref[...] = low
+    acts = []
     at = 0
     for w in ffw:
         n = w.shape[1]
         val, der = gelu_parts(nt(low, w[0]))
-        act_ref[:, at:at + n] = val.astype(BF)
+        acts.append(val.astype(BF))
+        act_ref[:, at:at + n] = acts[-1]
         der_ref[:, at:at + n] = der.astype(BF)
         at += n
-    ffn_ref[...] = nn(act_ref[...], jnp.concatenate([w[1] for w in ffw], axis=0))
-
-
-def first_part(x, att, wo, ffw, g1, b1, blk=512):
+    ffn = nn(jnp.concatenate(acts, axis=1), jnp.concatenate([w[1] for w in ffw], axis=0))
+    sum_ref[...] = first + ffn
+    dual_ref[...] = y_ref[...].astype(F32) + branch + ffn
+
+
+def first_part(x, y, att, wo, ffw, g1, b1, blk=512):
     seq, width = x.shape
     ff = sum(w.shape[1] for w in ffw)
     row, full = row_specs(blk)
@@ -257,102 +265,126 @@
     return pl.pallas_call(
         functools.partial(first_kernel, len(wo), len(ffw)),
         grid=(seq // blk,),
-        in_specs=[row(width)] + [column(PAIR, blk)] * len(att) + [out_spec(width)] * len(wo) + [full(w.shape) for w in ffw] + [full((1, width))] * 2,
-        out_specs=[row(width), row(width), row(ff), row(ff), row(width)],
-        out_shape=[sd(width, F32), sd(width, BF), sd(ff, BF), sd(ff, BF), sd(width, F32)],
-        compiler_params=params(10),
+        in_specs=[row(width)] * 2 + [column(PAIR, blk)] * len(att) + [out_spec(width)] * len(wo) + [full(w.shape) for w in ffw] + [full((1, width))] * 2,
+        out_specs=[row(width), row(ff), row(ff), row(width), row(PAIR), row(width), row(width)],
+        out_shape=[sd(width, BF), sd(ff, BF), sd(ff, BF), sd(width, BF), sd(PAIR, F32), sd(width, F32), sd(width, F32)],
+        compiler_params=params(12),
         cost_estimate=cost(8),
         name="first_part",
-    )(x, *att, *wo, *ffw, g1, b1)
-
-
-def second_kernel(pairs, pa, pb, x_ref, y_ref, gs_ref, gd_ref, mixed_ref, low_ref, ffn_ref, der_a_ref, *refs):
-    wo, refs = refs[:pairs], refs[pairs:]
-    ffa, refs = refs[:pa], refs[pa:]
-    ffb, refs = refs[:pb], refs[pb:]
-    (g1_ref, b1_ref, g2_ref, b2_ref, ns_ref, nd_ref, act_ref, dh_ref, gf_ref, gm_ref, gb_ref, *rest) = refs
-    do, (vec_ref, der_ref) = rest[:pairs // 2], rest[pairs // 2:]
-    @pl.when(pl.program_id(0) == 0)
-    def _():
-        vec_ref[...] = jnp.zeros_like(vec_ref)
-    mixed = mixed_ref[...]
-    zhat1, rstd1 = normed(mixed)
-    first = zhat1 * g1_ref[...] + b1_ref[...]
-    low = low_ref[...]
+    )(x, y, *att, *wo, *ffw, g1, b1)
+
+
+def second_rows(rows, wo, ffa, ffb, gs_ref, gd_ref, low_ref, der_a_ref, zhat_ref, rstd_ref, sum_ref, dual_ref,
+                g1_ref, g2_ref, b2_ref, ns_ref, nd_ref, act_ref, dh_ref, gf_ref, gm_ref, gb_ref, *rest):
+    do, vec_ref = rest[:-1], rest[-1]
+    low = low_ref[rows, :]
+    ders, acts = [], []
+    at = 0
+    for w in ffa:
+        ders.append(der_a_ref[rows, at:at + w.shape[1]])
+        at += w.shape[1]
     at = 0
     for w in ffb:
         n = w.shape[1]
         val, der = gelu_parts(nt(low, w[0]))
-        act_ref[:, at:at + n] = val.astype(BF)
-        der_ref[:, at:at + n] = der.astype(BF)
+        acts.append(val.astype(BF))
+        ders.append(der.astype(BF))
+        act_ref[rows, at:at + n] = acts[-1]
         at += n
-    ffn = ffn_ref[...] + nn(act_ref[...], jnp.concatenate([w[1] for w in ffb], axis=0))
-    zhat2, rstd2 = normed(first + ffn)
-    ns_ref[...] = (zhat2 * g2_ref[...] + b2_ref[...]).astype(BF)
-    nd_ref[...] = (y_ref[...].astype(F32) + (mixed - x_ref[...].astype(F32)) + ffn).astype(BF)
-    u = gs_ref[...].astype(F32)
+        yield True
+    ffn = nn(jnp.concatenate(acts, axis=1), jnp.concatenate([w[1] for w in ffb], axis=0))
+    yield True
+    zhat2, rstd2 = normed(sum_ref[rows, :] + ffn)
+    ns_ref[rows, :] = (zhat2 * g2_ref[...] + b2_ref[...]).astype(BF)
+    nd_ref[rows, :] = (dual_ref[rows, :] + ffn).astype(BF)
+    u = gs_ref[rows, :].astype(F32)
     second = norm_back(u * g2_ref[...], zhat2, rstd2)
-    gd = gd_ref[...].astype(F32)
+    gd = gd_ref[rows, :].astype(F32)
     gf = (second + gd).astype(BF)
-    gf_ref[...] = gf
+    gf_ref[rows, :] = gf
+    fold = lambda v: jnp.sum(v, axis=0, keepdims=True)
+    vec = [fold(u * zhat2), fold(u)]
+    yield True
+    dhs = []
     at = 0
-    for side, der, base in ((ffa, der_a_ref, 0), (ffb, der_ref, der_a_ref.shape[1])):
-        for w in side:
-            n = w.shape[1]
-            dh_ref[:, at:at + n] = (nt(gf, w[1]) * der[:, at - base:at - base + n].astype(F32)).astype(BF)
-            at += n
-    gfirst = second + nn(dh_ref[...], jnp.concatenate([w[0] for w in ffa + ffb], axis=0))
-    gm = norm_back(gfirst * g1_ref[...], zhat1, rstd1)
-    gm_ref[...] = gm
+    for w, der in zip(ffa + ffb, ders):
+        n = w.shape[1]
+        dhs.append((nt(gf, w[1]) * der.astype(F32)).astype(BF))
+        dh_ref[rows, at:at + n] = dhs[-1]
+        at += n
+        yield True
+    gfirst = second + nn(jnp.concatenate(dhs, axis=1), jnp.concatenate([w[0] for w in ffa + ffb], axis=0))
+    yield True
+    zhat1 = zhat_ref[rows, :].astype(F32)
+    gm = norm_back(gfirst * g1_ref[...], zhat1, rstd_ref[rows, :1])
+    gm_ref[rows, :] = gm
     gb = (gm + gd).astype(BF)
-    gb_ref[...] = gb.T
-    dout = nt(gb, jnp.concatenate([w[...] for w in wo], axis=0)).astype(BF).T
-    for i in range(pairs):
-        do[i // 2][i % 2] = dout[i * PAIR:(i + 1) * PAIR]
-    fold = lambda v: jnp.sum(v, axis=0, keepdims=True)
-    vec_ref[...] += jnp.concatenate([fold(gfirst * zhat1), fold(gfirst), fold(u * zhat2), fold(u), jnp.zeros((4, u.shape[1]), F32)], axis=0)
-
-
-def second_part(x, y, gs, gd, mixed, low, ffn, der, wo, ffa, ffb, g1, b1, g2, b2, blk=512):
-    seq, width = x.shape
+    gb_ref[:, rows] = gb.T
+    vec_ref[...] += jnp.concatenate([fold(gfirst * zhat1), fold(gfirst), *vec, jnp.zeros((4, u.shape[1]), F32)], axis=0)
+    yield True
+    dout = nt(gb, wo).astype(BF).T
+    for i in range(2 * len(do)):
+        do[i // 2][i % 2, :, rows] = dout[i * PAIR:(i + 1) * PAIR]
+    yield True
+
+
+def interleave(streams):
+    waiting, running = list(streams), []
+    while waiting or running:
+        if waiting:
+            running.append(waiting.pop(0))
+        for stream in running[:]:
+            if next(stream, None) is None:
+                running.remove(stream)
+
+
+def second_kernel(pairs, pa, pb, *refs):
+    data, refs = refs[:8], refs[8:]
+    wo, refs = refs[:pairs], refs[pairs:]
+    ffa, refs = refs[:pa], refs[pa:]
+    ffb, refs = refs[:pb], refs[pb:]
+    vec_ref = refs[-1]
+
+    @pl.when(pl.program_id(0) == 0)
+    def _():
+        vec_ref[...] = jnp.zeros_like(vec_ref)
+
+    wo = jnp.concatenate([w[...] for w in wo], axis=0)
+    rows = data[0].shape[0]
+    interleave(second_rows(slice(lo, lo + STREAM), wo, ffa, ffb, *data, *refs) for lo in range(0, rows, STREAM))
+
+
+def second_part(gs, gd, low, der, zhat, rstd, total, dual, wo, ffa, ffb, g1, g2, b2, blk=512):
+    seq, width = gs.shape
     fa, fb = sum(w.shape[1] for w in ffa), sum(w.shape[1] for w in ffb)
     row, full = row_specs(blk)
     sd = lambda w, t: jax.ShapeDtypeStruct((seq, w), t)
     return pl.pallas_call(
         functools.partial(second_kernel, len(wo), len(ffa), len(ffb)),
         grid=(seq // blk,),
-        in_specs=[row(width)] * 7 + [row(fa)] + [out_spec(width)] * len(wo) + [full(w.shape) for w in (*ffa, *ffb)] + [full((1, width))] * 4,
+        in_specs=[row(width)] * 3 + [row(fa), row(width), row(PAIR), row(width), row(width)] + [out_spec(width)] * len(wo) + [full(w.shape) for w in (*ffa, *ffb)] + [full((1, width))] * 3,
         out_specs=[row(width), row(width), row(fb), row(fa + fb), row(width), row(width), pl.BlockSpec((width, blk), lambda p: (0, p))] + [column(PAIR, blk)] * (len(wo) // 2) + [full((8, width))],
         out_shape=[sd(width, BF), sd(width, BF), sd(fb, BF), sd(fa + fb, BF), sd(width, BF), pltpu.HBM((seq, width), F32), jax.ShapeDtypeStruct((width, seq), BF)] + [jax.ShapeDtypeStruct((2, PAIR, seq), BF)] * (len(wo) // 2) + [jax.ShapeDtypeStruct((8, width), F32)],
-        scratch_shapes=[pltpu.VMEM((blk, fb), BF)],
-        compiler_params=params(14),
+        compiler_params=params(12),
         cost_estimate=cost(18),
         name="second_part",
-    )(x, y, gs, gd, mixed, low, ffn, der, *wo, *ffa, *ffb, g1, b1, g2, b2)
-
-
-def wgrad_kernel(act_a_ref, act_b_ref, dh_ref, gf_ref, low_ref, out_ref):
-    out_ref[0] = tn(dh_ref[...], low_ref[...]).astype(BF)
-    @pl.when(pl.program_id(0) == 0)
-    def _():
-        out_ref[1] = tn(act_a_ref[...], gf_ref[...]).astype(BF)
-    @pl.when(pl.program_id(0) == 1)
-    def _():
-        out_ref[1] = tn(act_b_ref[...], gf_ref[...]).astype(BF)
+    )(gs, gd, low, der, zhat, rstd, total, dual, *wo, *ffa, *ffb, g1, g2, b2)
+
+
+def wgrad_kernel(which, act_a_ref, act_b_ref, dh_ref, gf_ref, low_ref, out_ref):
+    piece = act_a_ref.shape[1] // 2
+    for side, act_ref in enumerate((act_a_ref, act_b_ref)):
+        at = (2 * side + which) * piece
+        out_ref[side, 0] = tn(dh_ref[:, at:at + piece], low_ref[...]).astype(BF)
+        out_ref[side, 1] = tn(act_ref[:, which * piece:(which + 1) * piece], gf_ref[...]).astype(BF)
 
 
 def wgrad(act_a, act_b, dh, gf, low, which):
-    seq, width = gf.shape
-    b = act_a.shape[1] // 2
-    full = lambda shape: pl.BlockSpec(shape, lambda p: (0,) * len(shape))
-    half = pl.BlockSpec((seq, b), lambda p: (0, which))
-    return pl.pallas_call(
-        wgrad_kernel,
-        grid=(2,),
-        in_specs=[half, half, pl.BlockSpec((seq, b), lambda p: (0, 2 * p + which)), full((seq, width)), full((seq, width))],
-        out_specs=pl.BlockSpec((None, 2, b, width), lambda p: (p, 0, 0, 0)),
-        out_shape=jax.ShapeDtypeStruct((2, 2, b, width), BF),
-        compiler_params=params(10),
+    width = gf.shape[1]
+    return pl.pallas_call(
+        functools.partial(wgrad_kernel, which),
+        out_shape=jax.ShapeDtypeStruct((2, 2, act_a.shape[1] // 2, width), BF),
+        compiler_params=params(12),
         cost_estimate=cost(6),
         name="wgrad",
     )(act_a, act_b, dh, gf, low)
@@ -527,11 +559,11 @@
         got = swap(ffw, *steps[-1])
         side_a = [ffw, swap(ffw, core_step)]
 
-    mixed, low, act_a, der_a, ffn_a = first_part(stream_x, [near[1], far[1]], weights, side_a, g1, b1)
-    got = after(got, mixed)
+    low, act_a, der_a, *kept = first_part(stream_x, stream_y, [near[1], far[1]], weights, side_a, g1, b1)
+    got = after(got, low)
     side_b = [got, swap(got, core_step)]
     ns, nd, act_b, dh, gf, gm, gb, do_near, do_far, vec = second_part(
-        stream_x, stream_y, grad_stream, grad_dual, mixed, low, ffn_a, der_a, weights, side_a, side_b, g1, b1, g2, b2
+        grad_stream, grad_dual, low, der_a, *kept, weights, side_a, side_b, g1, g2, b2
     )
 
     ffgrad = lambda which, *earlier: wgrad(act_a, act_b, after(dh, *earlier), gf, low, which)

time: 134 us -> 132 us (0.985)
  Pallas kernels: 64.9 us -> 62.5 us
    pallas_call x2, Pallas kernels: 6.56 us -> 4.79 us  [wgrad(): pl.pallas_call(functools.partial(wgrad_kernel, which), out_shape=jax.Shap...]
  transfers between devices with their start and end apart: 22 -> 22, of which waited for: 14 -> 14; matrix products, arithmetic and copies ran while one was open for 1% -> 2% of each run, Pallas kernels for 31% -> 30%
where the time goes in v2:
time: 132 us
  Pallas kernels  62.5 us (47%)
  waiting for transfers between devices  38.4 us (29%)
  starting transfers between devices  27.7 us (21%)
    ppermute x22, waiting for transfers between devices, swap(): return lax.ppermute(value, ('dp', 'head'), pairs)  38.4 us
    ppermute x22, starting transfers between devices, swap(): return lax.ppermute(value, ('dp', 'head'), pairs)  27.7 us
    pallas_call x4, Pallas kernels, attn_fwd(): pl.pallas_call(functools.partial(attn_fwd_kernel, scale, slot), grid=(1,)...  17.1 us
    pallas_call x2, Pallas kernels, attn_bwd(): pl.pallas_call(functools.partial(attn_bwd_kernel, scale), grid=(2,), in_s...  16.7 us
    pallas_call x1, Pallas kernels, second_part(): pl.pallas_call(functools.partial(second_kernel, len(wo), len(ffa), len(ff...  11.6 us
    pallas_call x1, Pallas kernels, first_part(): pl.pallas_call(functools.partial(first_kernel, len(wo), len(ffw)), grid=(...  4.91 us
    pallas_call x2, Pallas kernels, wgrad(): pl.pallas_call(functools.partial(wgrad_kernel, which), out_shape=jax.Shap...  4.79 us
    pallas_call x1, Pallas kernels, sgrad(): pl.pallas_call(functools.partial(sgrad_kernel, len(w)), grid=(seq // blk,...  3.75 us
  transfers between devices with their start and end apart: 22, of which 14 were waited for; matrix products, arithmetic and copies ran while one was open for 2% of the time, Pallas kernels for 30%

profile of v2, /device:TPU:0, one launch (start us, length us, event | category | flops | bytes accessed | tf_op | source)
XLA Modules:
  0.0 131.9 jit_solution(5324316257681984854)
XLA Ops:
  2.3 4.1 %collective-permute-start = (bf16[2,64,512]{2,1,0:T(8,128)(2,1)S(1)}, bf16[2,64,512]{2,1,0:T(8,128)(2,1)S(1)}, u32[]{:S(2)}, u32[]{:S(2)}) collective-permute-start(bf16[2,64,512]{2,1,0:T(8,128)(2,1)S(1)} %get-tuple-element.94), channel_id=1, source_target_pairs={{0,16},{1,17},{2,18},{3,19},{4,20},{5,21},{6,22},{7,23},{8,24},{9,... | collective-permute-start | bytes 393224 | tf_op jit(solution)/shard_map/ppermute | solution.py:508
  8.5 4.2 %attn_fwd.4 = (bf16[2,384,1024]{2,1,0:T(8,128)(2,1)S(1)}, bf16[2,128,1024]{2,1,0:T(8,128)(2,1)S(1)}, f32[2,2,1024]{2,1,0:T(2,128)S(1)}, bf16[2,2,256,2560]{3,2,1,0:T(8,128)(2,1)}) custom-call(bf16[512,1024]{1,0:T(8,128)(2,1)S(1)} %get-tuple-element.91.xt_ref, bf16[512,512]{1,0:T(8,128)(2,1)S(1)} %get-tuple-element.95.w_ref.refs_3_.refs_9_, ...), custom_call_target="tpu_custom_call" | custom-call | flops 5000000000 | bytes 1048576 | tf_op jit(solution)/shard_map/attn_fwd/pallas_call | solution.py:131
  14.3 4.2 %attn_fwd.5 = (bf16[2,384,1024]{2,1,0:T(8,128)(2,1)S(1)}, bf16[2,128,1024]{2,1,0:T(8,128)(2,1)S(1)}, f32[2,2,1024]{2,1,0:T(2,128)S(1)}, bf16[2,2,256,2560]{3,2,1,0:T(8,128)(2,1)}) custom-call(bf16[512,1024]{1,0:T(8,128)(2,1)S(1)} %get-tuple-element.91.xt_ref, ...), custom_call_target="tpu_custom_call", output_to_operand_aliasing={{0}: (3, {}), {1}: (4, {}), {2}: (5, {}), {3}: (6, {})} | custom-call | flops 5000000000 | bytes 1048576 | tf_op jit(solution)/shard_map/attn_fwd/pallas_call | solution.py:131
  20.9 4.2 %attn_fwd.6 = (bf16[2,384,1024]{2,1,0:T(8,128)(2,1)S(1)}, bf16[2,128,1024]{2,1,0:T(8,128)(2,1)S(1)}, f32[2,2,1024]{2,1,0:T(2,128)S(1)}, bf16[2,2,256,2560]{3,2,1,0:T(8,128)(2,1)}) custom-call(bf16[512,1024]{1,0:T(8,128)(2,1)S(1)} %get-tuple-element.91.xt_ref, bf16[512,512]{1,0:T(8,128)(2,1)S(1)} %collective-permute-done.1.w_ref.refs_5_.refs_11_, ...), custom_call_target="tpu_custom_call" | custom-call | flops 5000000000 | bytes 1048576 | tf_op jit(solution)/shard_map/attn_fwd/pallas_call | solution.py:131
  25.1 3.4 %collective-permute-done.4 = bf16[2,256,512]{2,1,0:T(8,128)(2,1)S(1)} collective-permute-done((bf16[2,256,512]{2,1,0:T(8,128)(2,1)S(1)}, bf16[2,256,512]{2,1,0:T(8,128)(2,1)S(1)}, u32[]{:S(2)}, u32[]{:S(2)}) %collective-permute-start.4) | collective-permute-done | bytes 524320 | tf_op jit(solution)/shard_map/ppermute | solution.py:508
  32.0 4.4 %attn_fwd.7 = (bf16[2,384,1024]{2,1,0:T(8,128)(2,1)S(1)}, bf16[2,128,1024]{2,1,0:T(8,128)(2,1)S(1)}, f32[2,2,1024]{2,1,0:T(2,128)S(1)}, bf16[2,2,256,2560]{3,2,1,0:T(8,128)(2,1)}) custom-call(bf16[512,1024]{1,0:T(8,128)(2,1)S(1)} %get-tuple-element.91.xt_ref, ...), custom_call_target="tpu_custom_call", output_to_operand_aliasing={{0}: (3, {}), {1}: (4, {}), {2}: (5, {}), {3}: (6, {})} | custom-call | flops 5000000000 | bytes 1048576 | tf_op jit(solution)/shard_map/attn_fwd/pallas_call | solution.py:131
  36.5 4.9 %first_part.1 = (bf16[1024,512]{1,0:T(8,128)(2,1)S(1)}, bf16[1024,1024]{1,0:T(8,128)(2,1)S(1)}, bf16[1024,1024]{1,0:T(8,128)(2,1)S(1)}, bf16[1024,512]{1,0:T(8,1...) custom-call(bf16[1024,512]{1,0:T(8,128)(2,1)S(1)} %copy-done, ...), custom_call_target="tpu_custom_call" | custom-call | flops 8000000000 | bytes 1048576 | tf_op jit(solution)/shard_map/first_part/pallas_call | solution.py:265
  41.5 2.5 %collective-permute-done.6.refs_14_ = bf16[2,512,512]{2,1,0:T(8,128)(2,1)S(1)} collective-permute-done((bf16[2,512,512]{2,1,0:T(8,128)(2,1)S(1)}, bf16[2,512,512]{2,1,0:T(8,128)(2,1)S(1)}, u32[]{:S(2)}, u32[]{:S(2)}) %collective-permute-start.6) | collective-permute-done | bytes 1048608 | tf_op jit(solution)/shard_map/ppermute | solution.py:508
  43.9 2.7 %collective-permute-done.7.refs_15_ = bf16[2,512,512]{2,1,0:T(8,128)(2,1)S(1)} collective-permute-done((bf16[2,512,512]{2,1,0:T(8,128)(2,1)S(1)}, bf16[2,512,512]{2,1,0:T(8,128)(2,1)S(1)}, u32[]{:S(2)}, u32[]{:S(2)}) %collective-permute-start.7) | collective-permute-done | bytes 1048608 | tf_op jit(solution)/shard_map/ppermute | solution.py:508
  46.6 11.6 %second_part.1 = (bf16[1024,512]{1,0:T(8,128)(2,1)}, bf16[1024,512]{1,0:T(8,128)(2,1)}, bf16[1024,1024]{1,0:T(8,128)(2,1)S(1)}, bf16[1024,2048]{1,0:T(8,128)(2,1...) custom-call(bf16[1024,512]{1,0:T(8,128)(2,1)S(1)} %copy-done.2, ...), custom_call_target="tpu_custom_call" | custom-call | flops 17999998976 | bytes 1048576 | tf_op jit(solution)/shard_map/second_part/pallas_call | solution.py:362
  58.3 8.4 %attn_bwd.2 = (bf16[2,384,1024]{2,1,0:T(8,128)(2,1)}, bf16[544,512]{1,0:T(8,128)(2,1)S(1)}, bf16[544,512]{1,0:T(8,128)(2,1)S(1)}) custom-call(bf16[512,1024]{1,0:T(8,128)(2,1)S(1)} %get-tuple-element.91.xt_ref, bf16[2,384,1024]{2,1,0:T(8,128)(2,1)S(1)} %get-tuple-element.126.qkv_ref, bf16[2,128,1024]{2,1,0:T(8,128)(2,1)S(1)} %get-tuple-element.113.refs_1_.att_ref, ...), custom_call_target="tpu_custom_call" | custom-call | flops 11000000512 | bytes 1048576 | tf_op jit(solution)/shard_map/attn_bwd/pallas_call | solution.py:183
  66.8 2.4 %wgrad.2 = bf16[2,2,512,512]{3,2,1,0:T(8,128)(2,1)S(1)} custom-call(bf16[1024,1024]{1,0:T(8,128)(2,1)S(1)} %get-tuple-element.134.act_a_ref, bf16[1024,1024]{1,0:T(8,128)(2,1)S(1)} %get-tuple-element.135.act_b_ref, bf16[1024,2048]{1,0:T(8,128)(2,1)S(1)} %get-tuple-element.146.dh_ref, bf16[1024,512]{1,0:T(8,128)(2,1)S(1)} %get-tuple-element.138.gf_ref, ...), custom_call_target="tpu_custom_call" | custom-call | flops 6000000000 | bytes 1048576 | tf_op jit(solution)/shard_map/wgrad/pallas_call | solution.py:384
  71.3 8.4 %attn_bwd.3 = (bf16[2,384,1024]{2,1,0:T(8,128)(2,1)}, bf16[544,512]{1,0:T(8,128)(2,1)S(1)}, bf16[544,512]{1,0:T(8,128)(2,1)S(1)}) custom-call(bf16[512,1024]{1,0:T(8,128)(2,1)S(1)} %get-tuple-element.91.xt_ref, bf16[2,384,1024]{2,1,0:T(8,128)(2,1)S(1)} %get-tuple-element.124.qkv_ref, bf16[2,128,1024]{2,1,0:T(8,128)(2,1)S(1)} %get-tuple-element.103.refs_0_.att_ref, ...), custom_call_target="tpu_custom_call" | custom-call | flops 11000000512 | bytes 1048576 | tf_op jit(solution)/shard_map/attn_bwd/pallas_call | solution.py:183
  79.7 2.4 %wgrad.3 = bf16[2,2,512,512]{3,2,1,0:T(8,128)(2,1)S(1)} custom-call(bf16[1024,1024]{1,0:T(8,128)(2,1)S(1)} %get-tuple-element.134.act_a_ref, bf16[1024,1024]{1,0:T(8,128)(2,1)S(1)} %get-tuple-element.135.act_b_ref, bf16[1024,2048]{1,0:T(8,128)(2,1)S(1)} %get-tuple-element.146.dh_ref, bf16[1024,512]{1,0:T(8,128)(2,1)S(1)} %get-tuple-element.138.gf_ref, ...), custom_call_target="tpu_custom_call" | custom-call | flops 6000000000 | bytes 1048576 | tf_op jit(solution)/shard_map/wgrad/pallas_call | solution.py:384
  82.1 2.4 %collective-permute-done.11 = bf16[544,512]{1,0:T(8,128)(2,1)S(1)} collective-permute-done((bf16[544,512]{1,0:T(8,128)(2,1)S(1)}, bf16[544,512]{1,0:T(8,128)(2,1)S(1)}, u32[]{:S(2)}, u32[]{:S(2)}) %collective-permute-start.11) | collective-permute-done | bytes 557088 | tf_op jit(solution)/shard_map/ppermute | solution.py:508
  88.1 3.7 %sgrad.1 = f32[1024,512]{1,0:T(8,128)} custom-call(f32[1024,512]{1,0:T(8,128)S(1)} %copy-done.8, bf16[2,384,1024]{2,1,0:T(8,128)(2,1)S(1)} %copy-done.10, bf16[2,384,1024]{2,1,0:T(8,128)(2,1)S(1)} %copy-done.9, bf16[512,512]{1,0:T(8,128)(2,1)S(1)} %get-tuple-element.99.w_ref.refs_2_.refs_8_, bf16[512,512]{1,0:T(8,128)(2,1)S(1)} %get-tuple-element.95.w_ref.refs_3_.refs_9_, ...), custom_call_target="tpu_custom_call" | custom-call | flops 4000000000 | bytes 1048576 | tf_op jit(solution)/shard_map/sgrad/pallas_call | solution.py:403
  91.9 2.5 %collective-permute-done.12 = bf16[272,512]{1,0:T(8,128)(2,1)S(1)} collective-permute-done((bf16[272,512]{1,0:T(8,128)(2,1)S(1)}, bf16[272,512]{1,0:T(8,128)(2,1)S(1)}, u32[]{:S(2)}, u32[]{:S(2)}) %collective-permute-start.12) | collective-permute-done | bytes 278560 | tf_op jit(solution)/shard_map/ppermute | solution.py:508
  96.1 3.5 %collective-permute-done.13 = bf16[136,512]{1,0:T(8,128)(2,1)S(1)} collective-permute-done((bf16[136,512]{1,0:T(8,128)(2,1)S(1)}, bf16[136,512]{1,0:T(8,128)(2,1)S(1)}, u32[]{:S(2)}, u32[]{:S(2)}) %collective-permute-start.13) | collective-permute-done | bytes 139296 | tf_op jit(solution)/shard_map/ppermute | solution.py:508
  103.2 2.4 %collective-permute-start.14 = (bf16[136,512]{1,0:T(8,128)(2,1)S(1)}, bf16[136,512]{1,0:T(8,128)(2,1)S(1)}, u32[]{:S(2)}, u32[]{:S(2)}) collective-permute-start(bf16[136,512]{1,0:T(8,128)(2,1)S(1)} %select_add_fusion.1), channel_id=1, source_target_pairs={{0,16},{1,17},{2,18},{3,19},{4,20},{5,21},{6,22},{7,23},{8,24},{9,... | collective-permute-start | bytes 417800 | tf_op jit(solution)/shard_map/ppermute | solution.py:508
  105.6 7.3 %collective-permute-done.14 = bf16[136,512]{1,0:T(8,128)(2,1)S(1)} collective-permute-done((bf16[136,512]{1,0:T(8,128)(2,1)S(1)}, bf16[136,512]{1,0:T(8,128)(2,1)S(1)}, u32[]{:S(2)}, u32[]{:S(2)}) %collective-permute-start.14) | collective-permute-done | bytes 139296 | tf_op jit(solution)/shard_map/ppermute | solution.py:508
  112.9 3.0 %collective-permute-start.16 = (bf16[136,512]{1,0:T(8,128)(2,1)S(1)}, bf16[136,512]{1,0:T(8,128)(2,1)S(1)}, u32[]{:S(2)}, u32[]{:S(2)}) collective-permute-start(bf16[136,512]{1,0:T(8,128)(2,1)S(1)} %add.74), channel_id=1, source_target_pairs={{0,8},{1,9},{2,6},{3,7},{4,12},{5,13},{6,2},{7,3},{8,0},{9,1},{10,... | collective-permute-start | bytes 417800 | tf_op jit(solution)/shard_map/ppermute | solution.py:508
  116.5 3.5 %collective-permute-done.16 = bf16[136,512]{1,0:T(8,128)(2,1)S(1)} collective-permute-done((bf16[136,512]{1,0:T(8,128)(2,1)S(1)}, bf16[136,512]{1,0:T(8,128)(2,1)S(1)}, u32[]{:S(2)}, u32[]{:S(2)}) %collective-permute-start.16) | collective-permute-done | bytes 139296 | tf_op jit(solution)/shard_map/ppermute | solution.py:508
  123.7 3.0 %collective-permute-done.18 = bf16[272,512]{1,0:T(8,128)(2,1)S(1)} collective-permute-done((bf16[272,512]{1,0:T(8,128)(2,1)S(1)}, bf16[272,512]{1,0:T(8,128)(2,1)S(1)}, u32[]{:S(2)}, u32[]{:S(2)}) %collective-permute-start.18) | collective-permute-done | bytes 278560 | tf_op jit(solution)/shard_map/ppermute | solution.py:508
  127.1 2.5 %collective-permute-done.21 = bf16[2,64,512]{2,1,0:T(8,128)(2,1)S(1)} collective-permute-done((bf16[2,64,512]{2,1,0:T(8,128)(2,1)S(1)}, bf16[2,64,512]{2,1,0:T(8,128)(2,1)S(1)}, u32[]{:S(2)}, u32[]{:S(2)}) %collective-permute-start.21) | collective-permute-done | bytes 131104 | tf_op jit(solution)/shard_map/ppermute | solution.py:508
  (92 shorter events, 29.3 us)
Async XLA Ops:
  2.3 10.5 %collective-permute-start = (bf16[2,64,512]{2,1,0:T(8,128)(2,1)S(1)}, bf16[2,64,512]{2,1,0:T(8,128)(2,1)S(1)}, u32[]{:S(2)}, u32[]{:S(2)}) collective-permute-start(bf16[2,64,512]{2,1,0:T(8,128)(2,1)S(1)} %get-tuple-element.94), channel_id=1, source_target_pairs={{0,16},{1,17},{2,18},{3,19},{4,20},{5,21},{6,22},{7,23},{8,24},{9,... | collective-permute-start | bytes 393224 | tf_op jit(solution)/shard_map/ppermute | solution.py:508
  6.4 14.6 %collective-permute-start.1 = (bf16[512,512]{1,0:T(8,128)(2,1)S(1)}, bf16[512,512]{1,0:T(8,128)(2,1)S(1)}, u32[]{:S(2)}, u32[]{:S(2)}) collective-permute-start(bf16[512,512]{1,0:T(8,128)(2,1)S(1)} %get-tuple-element.95.w_ref.refs_3_.refs_9_), channel_id=1, source_target_pairs={{0,1},{1,0},{2,3},{3,2},{4,5},{5,4},{6,7},{7,6},{8,9},{9,8},{10,11... | collective-permute-start | bytes 1572872 | tf_op jit(solution)/shard_map/ppermute | solution.py:508
  12.8 6.4 %collective-permute-start.3 = (bf16[2,128,512]{2,1,0:T(8,128)(2,1)S(1)}, bf16[2,128,512]{2,1,0:T(8,128)(2,1)S(1)}, u32[]{:S(2)}, u32[]{:S(2)}) collective-permute-start(bf16[2,128,512]{2,1,0:T(8,128)(2,1)S(1)} %get-tuple-element.181), channel_id=1, source_target_pairs={{0,4},{1,5},{2,10},{3,11},{4,0},{5,1},{6,14},{7,15},{8,12},{9,13},... | collective-permute-start | bytes 786440 | tf_op jit(solution)/shard_map/ppermute | solution.py:508
  19.3 9.2 %collective-permute-start.4 = (bf16[2,256,512]{2,1,0:T(8,128)(2,1)S(1)}, bf16[2,256,512]{2,1,0:T(8,128)(2,1)S(1)}, u32[]{:S(2)}, u32[]{:S(2)}) collective-permute-start(bf16[2,256,512]{2,1,0:T(8,128)(2,1)S(1)} %get-tuple-element.177), channel_id=1, source_target_pairs={{0,8},{1,9},{2,3},{3,2},{4,12},{5,13},{6,7},{7,6},{8,0},{9,1},{10,... | collective-permute-start | bytes 1572872 | tf_op jit(solution)/shard_map/ppermute | solution.py:508
  28.5 7.9 %collective-permute-start.5 = (bf16[2,512,512]{2,1,0:T(8,128)(2,1)S(1)}, bf16[2,512,512]{2,1,0:T(8,128)(2,1)S(1)}, u32[]{:S(2)}, u32[]{:S(2)}) collective-permute-start(bf16[2,512,512]{2,1,0:T(8,128)(2,1)S(1)} %constant_dynamic-update-slice_fusion.5.refs_6_.refs_12_), channel_id=1, source_target_pairs={{0,2},{1,3},{2,0},{3,1},{4,6},{5,7},{6,4},{7,5},{8,10},{9,11},{10,... | collective-permute-start | bytes 3145736 | tf_op jit(solution)/shard_map/ppermute | solution.py:508
  28.6 3.4 %collective-permute-start.2 = (bf16[512,512]{1,0:T(8,128)(2,1)S(1)}, bf16[512,512]{1,0:T(8,128)(2,1)S(1)}, u32[]{:S(2)}, u32[]{:S(2)}) collective-permute-start(bf16[512,512]{1,0:T(8,128)(2,1)S(1)} %collective-permute-done.1.w_ref.refs_5_.refs_11_), channel_id=1, source_target_pairs={{0,2},{1,3},{2,0},{3,1},{4,6},{5,7},{6,4},{7,5},{8,10},{9,11},{10,... | collective-permute-start | bytes 1572872 | tf_op jit(solution)/shard_map/ppermute | solution.py:508
  29.1 14.8 %collective-permute-start.6 = (bf16[2,512,512]{2,1,0:T(8,128)(2,1)S(1)}, bf16[2,512,512]{2,1,0:T(8,128)(2,1)S(1)}, u32[]{:S(2)}, u32[]{:S(2)}) collective-permute-start(bf16[2,512,512]{2,1,0:T(8,128)(2,1)S(1)} %constant_dynamic-update-slice_fusion.5.refs_6_.refs_12_), channel_id=1, source_target_pairs={{0,1},{1,0},{2,6},{3,7},{4,5},{5,4},{6,2},{7,3},{8,9},{9,8},{10,14... | collective-permute-start | bytes 3145736 | tf_op jit(solution)/shard_map/ppermute | solution.py:508
  36.5 34.8 %slice-start.2 = ((s8[5242880]{0:T(1024)(128)(4,1)}), s8[4194304]{0:T(1024)(128)(4,1)S(1)}, s32[]{:S(2)}) async-start(s8[5242880]{0:T(1024)(128)(4,1)} %bitcast.26), calls=%async_computation.2 | async-start | bytes 8388608
  43.9 2.7 %collective-permute-start.7 = (bf16[2,512,512]{2,1,0:T(8,128)(2,1)S(1)}, bf16[2,512,512]{2,1,0:T(8,128)(2,1)S(1)}, u32[]{:S(2)}, u32[]{:S(2)}) collective-permute-start(bf16[2,512,512]{2,1,0:T(8,128)(2,1)S(1)} %collective-permute-done.6.refs_14_), channel_id=1, source_target_pairs={{0,2},{1,3},{2,0},{3,1},{4,6},{5,7},{6,4},{7,5},{8,10},{9,11},{10,... | collective-permute-start | bytes 3145736 | tf_op jit(solution)/shard_map/ppermute | solution.py:508
  46.6 24.7 %slice-start.3 = ((s8[5242880]{0:T(1024)(128)(4,1)}), s8[1048576]{0:T(1024)(128)(4,1)S(1)}, s32[]{:S(2)}) async-start(s8[5242880]{0:T(1024)(128)(4,1)} %bitcast.26), calls=%async_computation.3 | async-start | bytes 2097152
  66.6 3.0 %collective-permute-start.8 = (bf16[544,512]{1,0:T(8,128)(2,1)S(1)}, bf16[544,512]{1,0:T(8,128)(2,1)S(1)}, u32[]{:S(2)}, u32[]{:S(2)}) collective-permute-start(bf16[544,512]{1,0:T(8,128)(2,1)S(1)} %get-tuple-element.133), channel_id=1, source_target_pairs={{0,2},{1,3},{2,0},{3,1},{4,6},{5,7},{6,4},{7,5},{8,10},{9,11},{10,... | collective-permute-start | bytes 1671176 | tf_op jit(solution)/shard_map/ppermute | solution.py:508
  69.2 17.1 %collective-permute-start.9 = (bf16[2,2,512,512]{3,2,1,0:T(8,128)(2,1)S(1)}, bf16[2,2,512,512]{3,2,1,0:T(8,128)(2,1)S(1)}, u32[]{:S(2)}, u32[]{:S(2)}) collective-permute-start(bf16[2,2,512,512]{3,2,1,0:T(8,128)(2,1)S(1)} %wgrad.2), channel_id=1, source_target_pairs={{0,2},{1,3},{2,0},{3,1},{4,6},{5,7},{6,4},{7,5},{8,10},{9,11},{10,... | collective-permute-start | bytes 6291464 | tf_op jit(solution)/shard_map/ppermute | solution.py:508
  69.8 14.7 %collective-permute-start.11 = (bf16[544,512]{1,0:T(8,128)(2,1)S(1)}, bf16[544,512]{1,0:T(8,128)(2,1)S(1)}, u32[]{:S(2)}, u32[]{:S(2)}) collective-permute-start(bf16[544,512]{1,0:T(8,128)(2,1)S(1)} %add.63), channel_id=1, source_target_pairs={{0,1},{1,0},{2,3},{3,2},{4,5},{5,4},{6,7},{7,6},{8,9},{9,8},{10,11... | collective-permute-start | bytes 1671176 | tf_op jit(solution)/shard_map/ppermute | solution.py:508
  79.7 2.4 %collective-permute-start.10 = (bf16[544,512]{1,0:T(8,128)(2,1)S(1)}, bf16[544,512]{1,0:T(8,128)(2,1)S(1)}, u32[]{:S(2)}, u32[]{:S(2)}) collective-permute-start(bf16[544,512]{1,0:T(8,128)(2,1)S(1)} %get-tuple-element.148), channel_id=1, source_target_pairs={{0,2},{1,3},{2,0},{3,1},{4,6},{5,7},{6,4},{7,5},{8,10},{9,11},{10,... | collective-permute-start | bytes 1671176 | tf_op jit(solution)/shard_map/ppermute | solution.py:508
  84.7 9.6 %collective-permute-start.12 = (bf16[272,512]{1,0:T(8,128)(2,1)S(1)}, bf16[272,512]{1,0:T(8,128)(2,1)S(1)}, u32[]{:S(2)}, u32[]{:S(2)}) collective-permute-start(bf16[272,512]{1,0:T(8,128)(2,1)S(1)} %broadcast_select_fusion), channel_id=1, source_target_pairs={{0,4},{1,5},{2,10},{3,11},{4,0},{5,1},{6,14},{7,15},{8,12},{9,13},... | collective-permute-start | bytes 835592 | tf_op jit(solution)/shard_map/ppermute | solution.py:508
  86.6 14.9 %collective-permute-start.15 = (bf16[2,512,512]{2,1,0:T(8,128)(2,1)S(1)}, bf16[2,512,512]{2,1,0:T(8,128)(2,1)S(1)}, u32[]{:S(2)}, u32[]{:S(2)}) collective-permute-start(bf16[2,512,512]{2,1,0:T(8,128)(2,1)S(1)} %get-tuple-element.170), channel_id=1, source_target_pairs={{0,1},{1,0},{2,6},{3,7},{4,5},{5,4},{6,2},{7,3},{8,9},{9,8},{10,14... | collective-permute-start | bytes 3145736 | tf_op jit(solution)/shard_map/ppermute | solution.py:508
  94.5 5.1 %collective-permute-start.13 = (bf16[136,512]{1,0:T(8,128)(2,1)S(1)}, bf16[136,512]{1,0:T(8,128)(2,1)S(1)}, u32[]{:S(2)}, u32[]{:S(2)}) collective-permute-start(bf16[136,512]{1,0:T(8,128)(2,1)S(1)} %broadcast_select_fusion.1), channel_id=1, source_target_pairs={{0,8},{1,9},{2,6},{3,7},{4,12},{5,13},{6,2},{7,3},{8,0},{9,1},{10,... | collective-permute-start | bytes 417800 | tf_op jit(solution)/shard_map/ppermute | solution.py:508
  101.5 14.3 %collective-permute-start.17 = (bf16[2,256,512]{2,1,0:T(8,128)(2,1)S(1)}, bf16[2,256,512]{2,1,0:T(8,128)(2,1)S(1)}, u32[]{:S(2)}, u32[]{:S(2)}) collective-permute-start(bf16[2,256,512]{2,1,0:T(8,128)(2,1)S(1)} %get-tuple-element.172), channel_id=1, source_target_pairs={{0,8},{1,9},{2,3},{3,2},{4,12},{5,13},{6,7},{7,6},{8,0},{9,1},{10,... | collective-permute-start | bytes 1572872 | tf_op jit(solution)/shard_map/ppermute | solution.py:508
  103.2 9.7 %collective-permute-start.14 = (bf16[136,512]{1,0:T(8,128)(2,1)S(1)}, bf16[136,512]{1,0:T(8,128)(2,1)S(1)}, u32[]{:S(2)}, u32[]{:S(2)}) collective-permute-start(bf16[136,512]{1,0:T(8,128)(2,1)S(1)} %select_add_fusion.1), channel_id=1, source_target_pairs={{0,16},{1,17},{2,18},{3,19},{4,20},{5,21},{6,22},{7,23},{8,24},{9,... | collective-permute-start | bytes 417800 | tf_op jit(solution)/shard_map/ppermute | solution.py:508
  112.9 7.2 %collective-permute-start.16 = (bf16[136,512]{1,0:T(8,128)(2,1)S(1)}, bf16[136,512]{1,0:T(8,128)(2,1)S(1)}, u32[]{:S(2)}, u32[]{:S(2)}) collective-permute-start(bf16[136,512]{1,0:T(8,128)(2,1)S(1)} %add.74), channel_id=1, source_target_pairs={{0,8},{1,9},{2,6},{3,7},{4,12},{5,13},{6,2},{7,3},{8,0},{9,1},{10,... | collective-permute-start | bytes 417800 | tf_op jit(solution)/shard_map/ppermute | solution.py:508
  116.0 6.4 %collective-permute-start.19 = (bf16[2,128,512]{2,1,0:T(8,128)(2,1)S(1)}, bf16[2,128,512]{2,1,0:T(8,128)(2,1)S(1)}, u32[]{:S(2)}, u32[]{:S(2)}) collective-permute-start(bf16[2,128,512]{2,1,0:T(8,128)(2,1)S(1)} %get-tuple-element.174), channel_id=1, source_target_pairs={{0,4},{1,5},{2,10},{3,11},{4,0},{5,1},{6,14},{7,15},{8,12},{9,13},... | collective-permute-start | bytes 786440 | tf_op jit(solution)/shard_map/ppermute | solution.py:508
  120.1 6.6 %collective-permute-start.18 = (bf16[272,512]{1,0:T(8,128)(2,1)S(1)}, bf16[272,512]{1,0:T(8,128)(2,1)S(1)}, u32[]{:S(2)}, u32[]{:S(2)}) collective-permute-start(bf16[272,512]{1,0:T(8,128)(2,1)S(1)} %maximum_select_fusion.1), channel_id=1, source_target_pairs={{0,4},{1,5},{2,10},{3,11},{4,0},{5,1},{6,14},{7,15},{8,12},{9,13},... | collective-permute-start | bytes 835592 | tf_op jit(solution)/shard_map/ppermute | solution.py:508
  122.4 7.2 %collective-permute-start.21 = (bf16[2,64,512]{2,1,0:T(8,128)(2,1)S(1)}, bf16[2,64,512]{2,1,0:T(8,128)(2,1)S(1)}, u32[]{:S(2)}, u32[]{:S(2)}) collective-permute-start(bf16[2,64,512]{2,1,0:T(8,128)(2,1)S(1)} %slice_add_fusion.5), channel_id=1, source_target_pairs={{0,16},{1,17},{2,18},{3,19},{4,20},{5,21},{6,22},{7,23},{8,24},{9,... | collective-permute-start | bytes 393224 | tf_op jit(solution)/shard_map/ppermute | solution.py:508
  127.0 3.4 %collective-permute-start.20 = (bf16[544,512]{1,0:T(8,128)(2,1)S(1)}, bf16[544,512]{1,0:T(8,128)(2,1)S(1)}, u32[]{:S(2)}, u32[]{:S(2)}) collective-permute-start(bf16[544,512]{1,0:T(8,128)(2,1)S(1)} %maximum_select_fusion.mine_ref), channel_id=1, source_target_pairs={{0,2},{1,3},{2,0},{3,1},{4,6},{5,7},{6,4},{7,5},{8,10},{9,11},{10,... | collective-permute-start | bytes 1671176 | tf_op jit(solution)/shard_map/ppermute | solution.py:508
  (15 other events, 118.8 us)

commit v3 on v2

--- a/solution.py
+++ b/solution.py
@@ -572,9 +572,12 @@
         qkv, att, inv, prob = group
         return attn_bwd(xt, qkv, att, after(do, *earlier), gb, inv, vec, prob, scale)
 
-    def halves(own, received):
-        n = own.shape[1] // 2
-        return own[:, n:] + received[:, n:], own[:, :n] + received[:, :n]
+    def halves(own, received, groups=1):
+        pairs, rows, _ = own.shape
+        cut = lambda v: v.reshape(pairs, groups, 2, -1, width)
+        own, received = cut(own), cut(received)
+        both = [(own[:, :, i] + received[:, :, i]).reshape(pairs, rows // 2, width) for i in range(2)]
+        return both[1], both[0]
 
     g_far, pay_far_other, pay_far = bwd(far, do_far)
     if fast:
@@ -586,7 +589,11 @@
         g_near, pay_other, pay_mine = bwd(near, do_near, pay_far)
         crossed_pay = swap(pay_other, core_step)
         ours = ffgrad(0, pay_mine)
-        whole = pay_mine + after(crossed_pay, ours) + from_head
+        part_b = ours[1] + crossed[1]
+        recv = swap(part_b, *steps[3])
+        part = ours[0] + crossed[0]
+        crossed_pay, from_head = after((crossed_pay, from_head), part_b)
+        whole = pay_mine + crossed_pay + from_head
         whole = jnp.concatenate([whole[:width], pay_far[width:] + from_head[width:]], axis=0)
 
         def split(low, value):
@@ -598,22 +605,18 @@
 
         sent, kept = split(first_low, whole)
         got = swap(sent, s0, s1)
-        crossed, ours = after((crossed, ours), sent)
-        part_b = ours[1] + crossed[1]
-        recv = swap(part_b, *steps[3])
-        part = ours[0] + crossed[0]
-        sg = sgrad(gm, [g_near, after(g_far, part_b)], weights)
+        sg = sgrad(gm, [g_near, after(g_far, sent)], weights)
         sent, kept = split(second_low, kept + after(got, part, sg))
         got = swap(sent, s1, s0)
-        whole = kept + got
+        sent, part = halves(part, after(recv, sent), 2)
+        recv = swap(sent, *steps[1])
+        whole = kept + after(got, sent)
         got = swap(whole, s2)
-        sent, part = halves(part, after(recv, whole))
+        sent, part = halves(part, after(recv, sent))
         recv = swap(sent, *steps[2])
         whole = whole + after(got, sent)
         got = swap(whole, s1, s0)
-        sent, part = halves(part, after(recv, whole))
-        recv = swap(sent, *steps[1])
-        whole = merge(second_low, whole, after(got, sent))
+        whole = merge(second_low, whole, got)
         got = swap(whole, s0, s1)
         sent, part = halves(part, after(recv, whole))
         recv = swap(sent, *steps[0])

time: 132 us -> 128 us (0.970); the launches traced: 132 us -> 127 us
  waiting for transfers between devices: 38.4 us -> 29.3 us
  starting transfers between devices: 27.7 us -> 31.1 us
    ppermute x22, waiting for transfers between devices: 38.4 us -> 29.3 us  [swap(): return lax.ppermute(value, ('dp', 'head'), pairs)]
    ppermute x22, starting transfers between devices: 27.7 us -> 31.1 us  [swap(): return lax.ppermute(value, ('dp', 'head'), pairs)]
  transfers between devices with their start and end apart: 22 -> 22, of which waited for: 14 -> 15; matrix products, arithmetic and copies ran while one was open for 2% -> 2% of each run, Pallas kernels for 30% -> 31%
where the time goes in v3:
time: 128 us; the launch traced here: 127 us
  Pallas kernels  62.6 us (49%)
  starting transfers between devices  31.1 us (24%)
  waiting for transfers between devices  29.3 us (23%)
  other arithmetic  1.3 us (1%)
    ppermute x22, starting transfers between devices, swap(): return lax.ppermute(value, ('dp', 'head'), pairs)  31.1 us
    ppermute x22, waiting for transfers between devices, swap(): return lax.ppermute(value, ('dp', 'head'), pairs)  29.3 us
    pallas_call x4, Pallas kernels, attn_fwd(): pl.pallas_call(functools.partial(attn_fwd_kernel, scale, slot), grid=(1,)...  17.1 us
    pallas_call x2, Pallas kernels, attn_bwd(): pl.pallas_call(functools.partial(attn_bwd_kernel, scale), grid=(2,), in_s...  16.7 us
    pallas_call x1, Pallas kernels, second_part(): pl.pallas_call(functools.partial(second_kernel, len(wo), len(ffa), len(ff...  11.7 us
    pallas_call x1, Pallas kernels, first_part(): pl.pallas_call(functools.partial(first_kernel, len(wo), len(ffw)), grid=(...  4.92 us
    pallas_call x2, Pallas kernels, wgrad(): pl.pallas_call(functools.partial(wgrad_kernel, which), out_shape=jax.Shap...  4.8 us
    pallas_call x1, Pallas kernels, sgrad(): pl.pallas_call(functools.partial(sgrad_kernel, len(w)), grid=(seq // blk,...  3.74 us
  transfers between devices with their start and end apart: 22, of which 15 were waited for; matrix products, arithmetic and copies ran while one was open for 2% of the time, Pallas kernels for 31%

profile of v3, /device:TPU:0, one launch (start us, length us, event | category | flops | bytes accessed | tf_op | source)
XLA Modules:
  0.0 126.6 jit_solution(13408106665317981155)
XLA Ops:
  2.3 4.1 %collective-permute-start = (bf16[2,64,512]{2,1,0:T(8,128)(2,1)S(1)}, bf16[2,64,512]{2,1,0:T(8,128)(2,1)S(1)}, u32[]{:S(2)}, u32[]{:S(2)}) collective-permute-start(bf16[2,64,512]{2,1,0:T(8,128)(2,1)S(1)} %get-tuple-element.93), channel_id=1, source_target_pairs={{0,16},{1,17},{2,18},{3,19},{4,20},{5,21},{6,22},{7,23},{8,24},{9,... | collective-permute-start | bytes 393224 | tf_op jit(solution)/shard_map/ppermute | solution.py:508
  8.5 4.3 %attn_fwd.4 = (bf16[2,384,1024]{2,1,0:T(8,128)(2,1)S(1)}, bf16[2,128,1024]{2,1,0:T(8,128)(2,1)S(1)}, f32[2,2,1024]{2,1,0:T(2,128)S(1)}, bf16[2,2,256,2560]{3,2,1,0:T(8,128)(2,1)}) custom-call(bf16[512,1024]{1,0:T(8,128)(2,1)S(1)} %get-tuple-element.90.xt_ref, bf16[512,512]{1,0:T(8,128)(2,1)S(1)} %get-tuple-element.94.w_ref.refs_3_.refs_9_, ...), custom_call_target="tpu_custom_call" | custom-call | flops 5000000000 | bytes 1048576 | tf_op jit(solution)/shard_map/attn_fwd/pallas_call | solution.py:131
  14.4 4.2 %attn_fwd.5 = (bf16[2,384,1024]{2,1,0:T(8,128)(2,1)S(1)}, bf16[2,128,1024]{2,1,0:T(8,128)(2,1)S(1)}, f32[2,2,1024]{2,1,0:T(2,128)S(1)}, bf16[2,2,256,2560]{3,2,1,0:T(8,128)(2,1)}) custom-call(bf16[512,1024]{1,0:T(8,128)(2,1)S(1)} %get-tuple-element.90.xt_ref, ...), custom_call_target="tpu_custom_call", output_to_operand_aliasing={{0}: (3, {}), {1}: (4, {}), {2}: (5, {}), {3}: (6, {})} | custom-call | flops 5000000000 | bytes 1048576 | tf_op jit(solution)/shard_map/attn_fwd/pallas_call | solution.py:131
  19.3 1.6 %collective-permute-start.4 = (bf16[2,256,512]{2,1,0:T(8,128)(2,1)S(1)}, bf16[2,256,512]{2,1,0:T(8,128)(2,1)S(1)}, u32[]{:S(2)}, u32[]{:S(2)}) collective-permute-start(bf16[2,256,512]{2,1,0:T(8,128)(2,1)S(1)} %get-tuple-element.173), channel_id=1, source_target_pairs={{0,8},{1,9},{2,3},{3,2},{4,12},{5,13},{6,7},{7,6},{8,0},{9,1},{10,... | collective-permute-start | bytes 1572872 | tf_op jit(solution)/shard_map/ppermute | solution.py:508
  20.9 4.2 %attn_fwd.6 = (bf16[2,384,1024]{2,1,0:T(8,128)(2,1)S(1)}, bf16[2,128,1024]{2,1,0:T(8,128)(2,1)S(1)}, f32[2,2,1024]{2,1,0:T(2,128)S(1)}, bf16[2,2,256,2560]{3,2,1,0:T(8,128)(2,1)}) custom-call(bf16[512,1024]{1,0:T(8,128)(2,1)S(1)} %get-tuple-element.90.xt_ref, bf16[512,512]{1,0:T(8,128)(2,1)S(1)} %collective-permute-done.1.w_ref.refs_5_.refs_11_, ...), custom_call_target="tpu_custom_call" | custom-call | flops 5000000000 | bytes 1048576 | tf_op jit(solution)/shard_map/attn_fwd/pallas_call | solution.py:131
  25.2 3.4 %collective-permute-done.4 = bf16[2,256,512]{2,1,0:T(8,128)(2,1)S(1)} collective-permute-done((bf16[2,256,512]{2,1,0:T(8,128)(2,1)S(1)}, bf16[2,256,512]{2,1,0:T(8,128)(2,1)S(1)}, u32[]{:S(2)}, u32[]{:S(2)}) %collective-permute-start.4) | collective-permute-done | bytes 524320 | tf_op jit(solution)/shard_map/ppermute | solution.py:508
  32.1 4.4 %attn_fwd.7 = (bf16[2,384,1024]{2,1,0:T(8,128)(2,1)S(1)}, bf16[2,128,1024]{2,1,0:T(8,128)(2,1)S(1)}, f32[2,2,1024]{2,1,0:T(2,128)S(1)}, bf16[2,2,256,2560]{3,2,1,0:T(8,128)(2,1)}) custom-call(bf16[512,1024]{1,0:T(8,128)(2,1)S(1)} %get-tuple-element.90.xt_ref, ...), custom_call_target="tpu_custom_call", output_to_operand_aliasing={{0}: (3, {}), {1}: (4, {}), {2}: (5, {}), {3}: (6, {})} | custom-call | flops 5000000000 | bytes 1048576 | tf_op jit(solution)/shard_map/attn_fwd/pallas_call | solution.py:131
  36.6 4.9 %first_part.1 = (bf16[1024,512]{1,0:T(8,128)(2,1)S(1)}, bf16[1024,1024]{1,0:T(8,128)(2,1)S(1)}, bf16[1024,1024]{1,0:T(8,128)(2,1)S(1)}, bf16[1024,512]{1,0:T(8,1...) custom-call(bf16[1024,512]{1,0:T(8,128)(2,1)S(1)} %copy-done, ...), custom_call_target="tpu_custom_call" | custom-call | flops 8000000000 | bytes 1048576 | tf_op jit(solution)/shard_map/first_part/pallas_call | solution.py:265
  41.5 2.4 %collective-permute-done.6.refs_14_ = bf16[2,512,512]{2,1,0:T(8,128)(2,1)S(1)} collective-permute-done((bf16[2,512,512]{2,1,0:T(8,128)(2,1)S(1)}, bf16[2,512,512]{2,1,0:T(8,128)(2,1)S(1)}, u32[]{:S(2)}, u32[]{:S(2)}) %collective-permute-start.6) | collective-permute-done | bytes 1048608 | tf_op jit(solution)/shard_map/ppermute | solution.py:508
  44.0 2.7 %collective-permute-done.7.refs_15_ = bf16[2,512,512]{2,1,0:T(8,128)(2,1)S(1)} collective-permute-done((bf16[2,512,512]{2,1,0:T(8,128)(2,1)S(1)}, bf16[2,512,512]{2,1,0:T(8,128)(2,1)S(1)}, u32[]{:S(2)}, u32[]{:S(2)}) %collective-permute-start.7) | collective-permute-done | bytes 1048608 | tf_op jit(solution)/shard_map/ppermute | solution.py:508
  46.7 11.7 %second_part.1 = (bf16[1024,512]{1,0:T(8,128)(2,1)}, bf16[1024,512]{1,0:T(8,128)(2,1)}, bf16[1024,1024]{1,0:T(8,128)(2,1)S(1)}, bf16[1024,2048]{1,0:T(8,128)(2,1...) custom-call(bf16[1024,512]{1,0:T(8,128)(2,1)S(1)} %copy-done.2, ...), custom_call_target="tpu_custom_call" | custom-call | flops 17999998976 | bytes 1048576 | tf_op jit(solution)/shard_map/second_part/pallas_call | solution.py:362
  58.3 8.4 %attn_bwd.2 = (bf16[2,384,1024]{2,1,0:T(8,128)(2,1)}, bf16[544,512]{1,0:T(8,128)(2,1)S(1)}, bf16[544,512]{1,0:T(8,128)(2,1)S(1)}) custom-call(bf16[512,1024]{1,0:T(8,128)(2,1)S(1)} %get-tuple-element.90.xt_ref, bf16[2,384,1024]{2,1,0:T(8,128)(2,1)S(1)} %get-tuple-element.125.qkv_ref, bf16[2,128,1024]{2,1,0:T(8,128)(2,1)S(1)} %get-tuple-element.112.refs_1_.att_ref, ...), custom_call_target="tpu_custom_call" | custom-call | flops 11000000512 | bytes 1048576 | tf_op jit(solution)/shard_map/attn_bwd/pallas_call | solution.py:183
  66.8 2.4 %wgrad.2 = bf16[2,2,512,512]{3,2,1,0:T(8,128)(2,1)S(1)} custom-call(bf16[1024,1024]{1,0:T(8,128)(2,1)S(1)} %get-tuple-element.133.act_a_ref, bf16[1024,1024]{1,0:T(8,128)(2,1)S(1)} %get-tuple-element.134.act_b_ref, bf16[1024,2048]{1,0:T(8,128)(2,1)S(1)} %get-tuple-element.147.dh_ref, bf16[1024,512]{1,0:T(8,128)(2,1)S(1)} %get-tuple-element.137.gf_ref, ...), custom_call_target="tpu_custom_call" | custom-call | flops 6000000000 | bytes 1048576 | tf_op jit(solution)/shard_map/wgrad/pallas_call | solution.py:384
  71.4 8.4 %attn_bwd.3 = (bf16[2,384,1024]{2,1,0:T(8,128)(2,1)}, bf16[544,512]{1,0:T(8,128)(2,1)S(1)}, bf16[544,512]{1,0:T(8,128)(2,1)S(1)}) custom-call(bf16[512,1024]{1,0:T(8,128)(2,1)S(1)} %get-tuple-element.90.xt_ref, bf16[2,384,1024]{2,1,0:T(8,128)(2,1)S(1)} %get-tuple-element.123.qkv_ref, bf16[2,128,1024]{2,1,0:T(8,128)(2,1)S(1)} %get-tuple-element.102.refs_0_.att_ref, ...), custom_call_target="tpu_custom_call" | custom-call | flops 11000000512 | bytes 1048576 | tf_op jit(solution)/shard_map/attn_bwd/pallas_call | solution.py:183
  79.7 2.4 %wgrad.3 = bf16[2,2,512,512]{3,2,1,0:T(8,128)(2,1)S(1)} custom-call(bf16[1024,1024]{1,0:T(8,128)(2,1)S(1)} %get-tuple-element.133.act_a_ref, bf16[1024,1024]{1,0:T(8,128)(2,1)S(1)} %get-tuple-element.134.act_b_ref, bf16[1024,2048]{1,0:T(8,128)(2,1)S(1)} %get-tuple-element.147.dh_ref, bf16[1024,512]{1,0:T(8,128)(2,1)S(1)} %get-tuple-element.137.gf_ref, ...), custom_call_target="tpu_custom_call" | custom-call | flops 6000000000 | bytes 1048576 | tf_op jit(solution)/shard_map/wgrad/pallas_call | solution.py:384
  84.8 1.6 %collective-permute-start.12 = (bf16[272,512]{1,0:T(8,128)(2,1)S(1)}, bf16[272,512]{1,0:T(8,128)(2,1)S(1)}, u32[]{:S(2)}, u32[]{:S(2)}) collective-permute-start(bf16[272,512]{1,0:T(8,128)(2,1)S(1)} %broadcast_select_fusion), channel_id=1, source_target_pairs={{0,4},{1,5},{2,10},{3,11},{4,0},{5,1},{6,14},{7,15},{8,12},{9,13},... | collective-permute-start | bytes 835592 | tf_op jit(solution)/shard_map/ppermute | solution.py:508
  86.6 3.7 %sgrad.1 = f32[1024,512]{1,0:T(8,128)} custom-call(f32[1024,512]{1,0:T(8,128)S(1)} %copy-done.8, bf16[2,384,1024]{2,1,0:T(8,128)(2,1)S(1)} %copy-done.10, bf16[2,384,1024]{2,1,0:T(8,128)(2,1)S(1)} %copy-done.9, bf16[512,512]{1,0:T(8,128)(2,1)S(1)} %get-tuple-element.98.w_ref.refs_2_.refs_8_, bf16[512,512]{1,0:T(8,128)(2,1)S(1)} %get-tuple-element.94.w_ref.refs_3_.refs_9_, ...), custom_call_target="tpu_custom_call" | custom-call | flops 4000000000 | bytes 1048576 | tf_op jit(solution)/shard_map/sgrad/pallas_call | solution.py:403
  90.3 4.1 %collective-permute-done.12 = bf16[272,512]{1,0:T(8,128)(2,1)S(1)} collective-permute-done((bf16[272,512]{1,0:T(8,128)(2,1)S(1)}, bf16[272,512]{1,0:T(8,128)(2,1)S(1)}, u32[]{:S(2)}, u32[]{:S(2)}) %collective-permute-start.12) | collective-permute-done | bytes 278560 | tf_op jit(solution)/shard_map/ppermute | solution.py:508
  94.6 1.6 %collective-permute-start.13 = (bf16[136,512]{1,0:T(8,128)(2,1)S(1)}, bf16[136,512]{1,0:T(8,128)(2,1)S(1)}, u32[]{:S(2)}, u32[]{:S(2)}) collective-permute-start(bf16[136,512]{1,0:T(8,128)(2,1)S(1)} %broadcast_select_fusion.1), channel_id=1, source_target_pairs={{0,8},{1,9},{2,6},{3,7},{4,12},{5,13},{6,2},{7,3},{8,0},{9,1},{10,... | collective-permute-start | bytes 417800 | tf_op jit(solution)/shard_map/ppermute | solution.py:508
  99.8 2.0 %collective-permute-start.15 = (bf16[136,512]{1,0:T(8,128)(2,1)S(1)}, bf16[136,512]{1,0:T(8,128)(2,1)S(1)}, u32[]{:S(2)}, u32[]{:S(2)}) collective-permute-start(bf16[136,512]{1,0:T(8,128)(2,1)S(1)} %select_add_fusion.1), channel_id=1, source_target_pairs={{0,16},{1,17},{2,18},{3,19},{4,20},{5,21},{6,22},{7,23},{8,24},{9,... | collective-permute-start | bytes 417800 | tf_op jit(solution)/shard_map/ppermute | solution.py:508
  101.8 5.1 %collective-permute-done.16 = bf16[2,256,512]{2,1,0:T(8,128)(2,1)S(1)} collective-permute-done((bf16[2,256,512]{2,1,0:T(8,128)(2,1)S(1)}, bf16[2,256,512]{2,1,0:T(8,128)(2,1)S(1)}, u32[]{:S(2)}, u32[]{:S(2)}) %collective-permute-start.16) | collective-permute-done | bytes 524320 | tf_op jit(solution)/shard_map/ppermute | solution.py:508
  109.5 3.1 %collective-permute-done.17 = bf16[136,512]{1,0:T(8,128)(2,1)S(1)} collective-permute-done((bf16[136,512]{1,0:T(8,128)(2,1)S(1)}, bf16[136,512]{1,0:T(8,128)(2,1)S(1)}, u32[]{:S(2)}, u32[]{:S(2)}) %collective-permute-start.17) | collective-permute-done | bytes 139296 | tf_op jit(solution)/shard_map/ppermute | solution.py:508
  115.5 3.1 %collective-permute-start.21 = (bf16[2,64,512]{2,1,0:T(8,128)(2,1)S(1)}, bf16[2,64,512]{2,1,0:T(8,128)(2,1)S(1)}, u32[]{:S(2)}, u32[]{:S(2)}) collective-permute-start(bf16[2,64,512]{2,1,0:T(8,128)(2,1)S(1)} %fusion.6), channel_id=1, source_target_pairs={{0,16},{1,17},{2,18},{3,19},{4,20},{5,21},{6,22},{7,23},{8,24},{9,... | collective-permute-start | bytes 393224 | tf_op jit(solution)/shard_map/ppermute | solution.py:508
  119.6 3.9 %collective-permute-start.20 = (bf16[544,512]{1,0:T(8,128)(2,1)S(1)}, bf16[544,512]{1,0:T(8,128)(2,1)S(1)}, u32[]{:S(2)}, u32[]{:S(2)}) collective-permute-start(bf16[544,512]{1,0:T(8,128)(2,1)S(1)} %maximum_select_fusion.mine_ref), channel_id=1, source_target_pairs={{0,2},{1,3},{2,0},{3,1},{4,6},{5,7},{6,4},{7,5},{8,10},{9,11},{10,... | collective-permute-start | bytes 1671176 | tf_op jit(solution)/shard_map/ppermute | solution.py:508
  (93 shorter events, 27.8 us)
Async XLA Ops:
  2.3 10.5 %collective-permute-start = (bf16[2,64,512]{2,1,0:T(8,128)(2,1)S(1)}, bf16[2,64,512]{2,1,0:T(8,128)(2,1)S(1)}, u32[]{:S(2)}, u32[]{:S(2)}) collective-permute-start(bf16[2,64,512]{2,1,0:T(8,128)(2,1)S(1)} %get-tuple-element.93), channel_id=1, source_target_pairs={{0,16},{1,17},{2,18},{3,19},{4,20},{5,21},{6,22},{7,23},{8,24},{9,... | collective-permute-start | bytes 393224 | tf_op jit(solution)/shard_map/ppermute | solution.py:508
  6.4 14.6 %collective-permute-start.1 = (bf16[512,512]{1,0:T(8,128)(2,1)S(1)}, bf16[512,512]{1,0:T(8,128)(2,1)S(1)}, u32[]{:S(2)}, u32[]{:S(2)}) collective-permute-start(bf16[512,512]{1,0:T(8,128)(2,1)S(1)} %get-tuple-element.94.w_ref.refs_3_.refs_9_), channel_id=1, source_target_pairs={{0,1},{1,0},{2,3},{3,2},{4,5},{5,4},{6,7},{7,6},{8,9},{9,8},{10,11... | collective-permute-start | bytes 1572872 | tf_op jit(solution)/shard_map/ppermute | solution.py:508
  12.8 6.4 %collective-permute-start.3 = (bf16[2,128,512]{2,1,0:T(8,128)(2,1)S(1)}, bf16[2,128,512]{2,1,0:T(8,128)(2,1)S(1)}, u32[]{:S(2)}, u32[]{:S(2)}) collective-permute-start(bf16[2,128,512]{2,1,0:T(8,128)(2,1)S(1)} %get-tuple-element.177), channel_id=1, source_target_pairs={{0,4},{1,5},{2,10},{3,11},{4,0},{5,1},{6,14},{7,15},{8,12},{9,13},... | collective-permute-start | bytes 786440 | tf_op jit(solution)/shard_map/ppermute | solution.py:508
  19.3 9.2 %collective-permute-start.4 = (bf16[2,256,512]{2,1,0:T(8,128)(2,1)S(1)}, bf16[2,256,512]{2,1,0:T(8,128)(2,1)S(1)}, u32[]{:S(2)}, u32[]{:S(2)}) collective-permute-start(bf16[2,256,512]{2,1,0:T(8,128)(2,1)S(1)} %get-tuple-element.173), channel_id=1, source_target_pairs={{0,8},{1,9},{2,3},{3,2},{4,12},{5,13},{6,7},{7,6},{8,0},{9,1},{10,... | collective-permute-start | bytes 1572872 | tf_op jit(solution)/shard_map/ppermute | solution.py:508
  28.6 7.9 %collective-permute-start.5 = (bf16[2,512,512]{2,1,0:T(8,128)(2,1)S(1)}, bf16[2,512,512]{2,1,0:T(8,128)(2,1)S(1)}, u32[]{:S(2)}, u32[]{:S(2)}) collective-permute-start(bf16[2,512,512]{2,1,0:T(8,128)(2,1)S(1)} %constant_dynamic-update-slice_fusion.5.refs_6_.refs_12_), channel_id=1, source_target_pairs={{0,2},{1,3},{2,0},{3,1},{4,6},{5,7},{6,4},{7,5},{8,10},{9,11},{10,... | collective-permute-start | bytes 3145736 | tf_op jit(solution)/shard_map/ppermute | solution.py:508
  28.7 3.4 %collective-permute-start.2 = (bf16[512,512]{1,0:T(8,128)(2,1)S(1)}, bf16[512,512]{1,0:T(8,128)(2,1)S(1)}, u32[]{:S(2)}, u32[]{:S(2)}) collective-permute-start(bf16[512,512]{1,0:T(8,128)(2,1)S(1)} %collective-permute-done.1.w_ref.refs_5_.refs_11_), channel_id=1, source_target_pairs={{0,2},{1,3},{2,0},{3,1},{4,6},{5,7},{6,4},{7,5},{8,10},{9,11},{10,... | collective-permute-start | bytes 1572872 | tf_op jit(solution)/shard_map/ppermute | solution.py:508
  29.2 14.8 %collective-permute-start.6 = (bf16[2,512,512]{2,1,0:T(8,128)(2,1)S(1)}, bf16[2,512,512]{2,1,0:T(8,128)(2,1)S(1)}, u32[]{:S(2)}, u32[]{:S(2)}) collective-permute-start(bf16[2,512,512]{2,1,0:T(8,128)(2,1)S(1)} %constant_dynamic-update-slice_fusion.5.refs_6_.refs_12_), channel_id=1, source_target_pairs={{0,1},{1,0},{2,6},{3,7},{4,5},{5,4},{6,2},{7,3},{8,9},{9,8},{10,14... | collective-permute-start | bytes 3145736 | tf_op jit(solution)/shard_map/ppermute | solution.py:508
  36.6 34.8 %slice-start.2 = ((s8[5242880]{0:T(1024)(128)(4,1)}), s8[4194304]{0:T(1024)(128)(4,1)S(1)}, s32[]{:S(2)}) async-start(s8[5242880]{0:T(1024)(128)(4,1)} %bitcast.61), calls=%async_computation.2 | async-start | bytes 8388608
  44.0 2.7 %collective-permute-start.7 = (bf16[2,512,512]{2,1,0:T(8,128)(2,1)S(1)}, bf16[2,512,512]{2,1,0:T(8,128)(2,1)S(1)}, u32[]{:S(2)}, u32[]{:S(2)}) collective-permute-start(bf16[2,512,512]{2,1,0:T(8,128)(2,1)S(1)} %collective-permute-done.6.refs_14_), channel_id=1, source_target_pairs={{0,2},{1,3},{2,0},{3,1},{4,6},{5,7},{6,4},{7,5},{8,10},{9,11},{10,... | collective-permute-start | bytes 3145736 | tf_op jit(solution)/shard_map/ppermute | solution.py:508
  46.6 24.7 %slice-start.3 = ((s8[5242880]{0:T(1024)(128)(4,1)}), s8[1048576]{0:T(1024)(128)(4,1)S(1)}, s32[]{:S(2)}) async-start(s8[5242880]{0:T(1024)(128)(4,1)} %bitcast.61), calls=%async_computation.3 | async-start | bytes 2097152
  66.7 3.0 %collective-permute-start.8 = (bf16[544,512]{1,0:T(8,128)(2,1)S(1)}, bf16[544,512]{1,0:T(8,128)(2,1)S(1)}, u32[]{:S(2)}, u32[]{:S(2)}) collective-permute-start(bf16[544,512]{1,0:T(8,128)(2,1)S(1)} %get-tuple-element.132), channel_id=1, source_target_pairs={{0,2},{1,3},{2,0},{3,1},{4,6},{5,7},{6,4},{7,5},{8,10},{9,11},{10,... | collective-permute-start | bytes 1671176 | tf_op jit(solution)/shard_map/ppermute | solution.py:508
  69.2 12.9 %collective-permute-start.11 = (bf16[2,2,512,512]{3,2,1,0:T(8,128)(2,1)S(1)}, bf16[2,2,512,512]{3,2,1,0:T(8,128)(2,1)S(1)}, u32[]{:S(2)}, u32[]{:S(2)}) collective-permute-start(bf16[2,2,512,512]{3,2,1,0:T(8,128)(2,1)S(1)} %wgrad.2), channel_id=1, source_target_pairs={{0,2},{1,3},{2,0},{3,1},{4,6},{5,7},{6,4},{7,5},{8,10},{9,11},{10,... | collective-permute-start | bytes 6291464 | tf_op jit(solution)/shard_map/ppermute | solution.py:508
  69.8 14.7 %collective-permute-start.10 = (bf16[544,512]{1,0:T(8,128)(2,1)S(1)}, bf16[544,512]{1,0:T(8,128)(2,1)S(1)}, u32[]{:S(2)}, u32[]{:S(2)}) collective-permute-start(bf16[544,512]{1,0:T(8,128)(2,1)S(1)} %add.106), channel_id=1, source_target_pairs={{0,1},{1,0},{2,3},{3,2},{4,5},{5,4},{6,7},{7,6},{8,9},{9,8},{10,11... | collective-permute-start | bytes 1671176 | tf_op jit(solution)/shard_map/ppermute | solution.py:508
  79.7 3.4 %collective-permute-start.9 = (bf16[544,512]{1,0:T(8,128)(2,1)S(1)}, bf16[544,512]{1,0:T(8,128)(2,1)S(1)}, u32[]{:S(2)}, u32[]{:S(2)}) collective-permute-start(bf16[544,512]{1,0:T(8,128)(2,1)S(1)} %get-tuple-element.146), channel_id=1, source_target_pairs={{0,2},{1,3},{2,0},{3,1},{4,6},{5,7},{6,4},{7,5},{8,10},{9,11},{10,... | collective-permute-start | bytes 1671176 | tf_op jit(solution)/shard_map/ppermute | solution.py:508
  82.4 14.9 %collective-permute-start.14 = (bf16[2,512,512]{2,1,0:T(8,128)(2,1)S(1)}, bf16[2,512,512]{2,1,0:T(8,128)(2,1)S(1)}, u32[]{:S(2)}, u32[]{:S(2)}) collective-permute-start(bf16[2,512,512]{2,1,0:T(8,128)(2,1)S(1)} %get-tuple-element.168), channel_id=1, source_target_pairs={{0,1},{1,0},{2,6},{3,7},{4,5},{5,4},{6,2},{7,3},{8,9},{9,8},{10,14... | collective-permute-start | bytes 3145736 | tf_op jit(solution)/shard_map/ppermute | solution.py:508
  84.8 9.7 %collective-permute-start.12 = (bf16[272,512]{1,0:T(8,128)(2,1)S(1)}, bf16[272,512]{1,0:T(8,128)(2,1)S(1)}, u32[]{:S(2)}, u32[]{:S(2)}) collective-permute-start(bf16[272,512]{1,0:T(8,128)(2,1)S(1)} %broadcast_select_fusion), channel_id=1, source_target_pairs={{0,4},{1,5},{2,10},{3,11},{4,0},{5,1},{6,14},{7,15},{8,12},{9,13},... | collective-permute-start | bytes 835592 | tf_op jit(solution)/shard_map/ppermute | solution.py:508
  94.6 5.1 %collective-permute-start.13 = (bf16[136,512]{1,0:T(8,128)(2,1)S(1)}, bf16[136,512]{1,0:T(8,128)(2,1)S(1)}, u32[]{:S(2)}, u32[]{:S(2)}) collective-permute-start(bf16[136,512]{1,0:T(8,128)(2,1)S(1)} %broadcast_select_fusion.1), channel_id=1, source_target_pairs={{0,8},{1,9},{2,6},{3,7},{4,12},{5,13},{6,2},{7,3},{8,0},{9,1},{10,... | collective-permute-start | bytes 417800 | tf_op jit(solution)/shard_map/ppermute | solution.py:508
  97.3 9.6 %collective-permute-start.16 = (bf16[2,256,512]{2,1,0:T(8,128)(2,1)S(1)}, bf16[2,256,512]{2,1,0:T(8,128)(2,1)S(1)}, u32[]{:S(2)}, u32[]{:S(2)}) collective-permute-start(bf16[2,256,512]{2,1,0:T(8,128)(2,1)S(1)} %bitcast.70), channel_id=1, source_target_pairs={{0,4},{1,5},{2,10},{3,11},{4,0},{5,1},{6,14},{7,15},{8,12},{9,13},... | collective-permute-start | bytes 1572872 | tf_op jit(solution)/shard_map/ppermute | solution.py:508
  99.8 7.6 %collective-permute-start.15 = (bf16[136,512]{1,0:T(8,128)(2,1)S(1)}, bf16[136,512]{1,0:T(8,128)(2,1)S(1)}, u32[]{:S(2)}, u32[]{:S(2)}) collective-permute-start(bf16[136,512]{1,0:T(8,128)(2,1)S(1)} %select_add_fusion.1), channel_id=1, source_target_pairs={{0,16},{1,17},{2,18},{3,19},{4,20},{5,21},{6,22},{7,23},{8,24},{9,... | collective-permute-start | bytes 417800 | tf_op jit(solution)/shard_map/ppermute | solution.py:508
  107.4 5.2 %collective-permute-start.17 = (bf16[136,512]{1,0:T(8,128)(2,1)S(1)}, bf16[136,512]{1,0:T(8,128)(2,1)S(1)}, u32[]{:S(2)}, u32[]{:S(2)}) collective-permute-start(bf16[136,512]{1,0:T(8,128)(2,1)S(1)} %add.122), channel_id=1, source_target_pairs={{0,8},{1,9},{2,6},{3,7},{4,12},{5,13},{6,2},{7,3},{8,0},{9,1},{10,... | collective-permute-start | bytes 417800 | tf_op jit(solution)/shard_map/ppermute | solution.py:508
  109.0 6.5 %collective-permute-start.19 = (bf16[2,128,512]{2,1,0:T(8,128)(2,1)S(1)}, bf16[2,128,512]{2,1,0:T(8,128)(2,1)S(1)}, u32[]{:S(2)}, u32[]{:S(2)}) collective-permute-start(bf16[2,128,512]{2,1,0:T(8,128)(2,1)S(1)} %get-tuple-element.170), channel_id=1, source_target_pairs={{0,8},{1,9},{2,3},{3,2},{4,12},{5,13},{6,7},{7,6},{8,0},{9,1},{10,... | collective-permute-start | bytes 786440 | tf_op jit(solution)/shard_map/ppermute | solution.py:508
  112.7 6.6 %collective-permute-start.18 = (bf16[272,512]{1,0:T(8,128)(2,1)S(1)}, bf16[272,512]{1,0:T(8,128)(2,1)S(1)}, u32[]{:S(2)}, u32[]{:S(2)}) collective-permute-start(bf16[272,512]{1,0:T(8,128)(2,1)S(1)} %maximum_select_fusion.1), channel_id=1, source_target_pairs={{0,4},{1,5},{2,10},{3,11},{4,0},{5,1},{6,14},{7,15},{8,12},{9,13},... | collective-permute-start | bytes 835592 | tf_op jit(solution)/shard_map/ppermute | solution.py:508
  115.5 8.0 %collective-permute-start.21 = (bf16[2,64,512]{2,1,0:T(8,128)(2,1)S(1)}, bf16[2,64,512]{2,1,0:T(8,128)(2,1)S(1)}, u32[]{:S(2)}, u32[]{:S(2)}) collective-permute-start(bf16[2,64,512]{2,1,0:T(8,128)(2,1)S(1)} %fusion.6), channel_id=1, source_target_pairs={{0,16},{1,17},{2,18},{3,19},{4,20},{5,21},{6,22},{7,23},{8,24},{9,... | collective-permute-start | bytes 393224 | tf_op jit(solution)/shard_map/ppermute | solution.py:508
  119.6 5.5 %collective-permute-start.20 = (bf16[544,512]{1,0:T(8,128)(2,1)S(1)}, bf16[544,512]{1,0:T(8,128)(2,1)S(1)}, u32[]{:S(2)}, u32[]{:S(2)}) collective-permute-start(bf16[544,512]{1,0:T(8,128)(2,1)S(1)} %maximum_select_fusion.mine_ref), channel_id=1, source_target_pairs={{0,2},{1,3},{2,0},{3,1},{4,6},{5,7},{6,4},{7,5},{8,10},{9,11},{10,... | collective-permute-start | bytes 1671176 | tf_op jit(solution)/shard_map/ppermute | solution.py:508
  (15 other events, 116.8 us)

commit v4 on v3

--- a/solution.py
+++ b/solution.py
@@ -190,6 +190,58 @@
         compiler_params=params(12),
         cost_estimate=cost(11),
         name="attn_bwd",
+    )(xt, qkv, att, do, gb, inv, vec, prob)
+
+
+def attn_bwd_both_kernel(scale, xt_ref, qkv_ref, att_all_ref, do_ref, gb_ref, inv_ref, vec_ref, prob_ref, g_all_ref, other_ref, mine_ref, dq_ref):
+    width, seq = xt_ref.shape
+    step = pl.program_id(0)
+    att_ref, g_ref = att_all_ref.at[step], g_all_ref.at[step]
+    dq_ref[...] = jnp.zeros_like(dq_ref)
+    for h in range(2):
+        head = lambda i: slice(i * PAIR + 64 * h, i * PAIR + 64 * h + 64)
+        own = head(0)
+        values = qkv_ref[head(2), :].T
+        scaled = do_ref[own, :].astype(F32) * inv_ref[h:h + 1, :]
+        delta = jnp.sum(scaled * att_ref[own, :].astype(F32), axis=0, keepdims=True)
+        scaled = scaled.astype(BF)
+        for kb in range(seq // BLK):
+            rows = slice(kb * BLK, (kb + 1) * BLK)
+            lo = kb * BLK
+            q, dout = qkv_ref[own, lo:], scaled[:, lo:]
+            p = jnp.concatenate([prob_ref[h, :, block_at(kb, qb)] for qb in range(kb, seq // BLK)], axis=1)
+            ds = (p.astype(F32) * (nn(values[rows], dout) - delta[:, lo:])).astype(BF)
+            g_ref[head(2), rows] = nt(dout, p).astype(BF)
+            g_ref[head(1), rows] = (nt(q, ds) * scale).astype(BF)
+            dq_ref[own, lo:] += nn(qkv_ref[head(1), rows], ds)
+    g_ref[0:PAIR, :] = (dq_ref[...] * scale).astype(BF)
+
+    @pl.when(step == 1)
+    def _():
+        grads = nt(xt_ref[...], jnp.concatenate([g_all_ref[0], g_all_ref[1]], axis=0)).astype(BF)
+        out = nt(gb_ref[...], jnp.concatenate([att_all_ref[0], att_all_ref[1]], axis=0)).astype(BF)
+        vec = jnp.concatenate([vec_ref[...], jnp.zeros((EXTRA - 8, 4 * PAIR), F32)], axis=0).astype(BF)
+        for i, ref in enumerate((other_ref, mine_ref)):
+            ref[0:width, 0:3 * PAIR] = grads[:, 3 * PAIR * i:3 * PAIR * (i + 1)]
+            ref[0:width, 3 * PAIR:] = out[:, PAIR * i:PAIR * (i + 1)]
+            ref[width:, :] = vec
+
+
+def attn_bwd_both(xt, qkv, att, do, gb, inv, vec, prob, scale):
+    width, seq = xt.shape
+    full = lambda shape: pl.BlockSpec(shape, lambda p: (0,) * len(shape))
+    own = lambda rows: pl.BlockSpec((None, rows, seq), lambda p: (p, 0, 0))
+    pay = (width + EXTRA, 4 * PAIR)
+    return pl.pallas_call(
+        functools.partial(attn_bwd_both_kernel, scale),
+        grid=(2,),
+        in_specs=[full((width, seq)), own(3 * PAIR), full((2, PAIR, seq)), own(PAIR), full((width, seq)), own(2), full(vec.shape), pl.BlockSpec((None, *prob.shape[1:]), lambda p: (p, 0, 0, 0))],
+        out_specs=[full((2, 3 * PAIR, seq)), full(pay), full(pay)],
+        out_shape=[jax.ShapeDtypeStruct((2, 3 * PAIR, seq), BF), jax.ShapeDtypeStruct(pay, BF), jax.ShapeDtypeStruct(pay, BF)],
+        scratch_shapes=[pltpu.VMEM((PAIR, seq), F32)],
+        compiler_params=params(12),
+        cost_estimate=cost(11),
+        name="attn_bwd_both",
     )(xt, qkv, att, do, gb, inv, vec, prob)
 
 
@@ -568,9 +620,9 @@
 
     ffgrad = lambda which, *earlier: wgrad(act_a, act_b, after(dh, *earlier), gf, low, which)
 
-    def bwd(group, do, *earlier):
+    def bwd(group, do, *earlier, run=attn_bwd):
         qkv, att, inv, prob = group
-        return attn_bwd(xt, qkv, att, after(do, *earlier), gb, inv, vec, prob, scale)
+        return run(xt, qkv, att, after(do, *earlier), gb, inv, vec, prob, scale)
 
     def halves(own, received, groups=1):
         pairs, rows, _ = own.shape
@@ -579,7 +631,7 @@
         both = [(own[:, :, i] + received[:, :, i]).reshape(pairs, rows // 2, width) for i in range(2)]
         return both[1], both[0]
 
-    g_far, pay_far_other, pay_far = bwd(far, do_far)
+    g_far, pay_far_other, pay_far = bwd(far, do_far, run=attn_bwd_both)
     if fast:
         crossed_pay = swap(pay_far_other, core_step)
         theirs = ffgrad(1, pay_far)

time: 128 us -> 127 us (level)
    pallas_call x2 -> x1, Pallas kernels: 16.7 us -> 8.37 us  [attn_bwd(): pl.pallas_call(functools.partial(attn_bwd_kernel, scale), grid=(2,), in_s...]
    pallas_call x0 -> x1, Pallas kernels: none -> 7.21 us  [attn_bwd_both(): pl.pallas_call(functools.partial(attn_bwd_both_kernel, scale), grid=(2,),...]
where the time goes in v4:
time: 127 us; the launch traced here: 125 us
  Pallas kernels  61.4 us (48%)
  starting transfers between devices  31.2 us (25%)
  waiting for transfers between devices  29.3 us (23%)
  other arithmetic  1.27 us (1%)
    ppermute x22, starting transfers between devices, swap(): return lax.ppermute(value, ('dp', 'head'), pairs)  31.2 us
    ppermute x22, waiting for transfers between devices, swap(): return lax.ppermute(value, ('dp', 'head'), pairs)  29.3 us
    pallas_call x4, Pallas kernels, attn_fwd(): pl.pallas_call(functools.partial(attn_fwd_kernel, scale, slot), grid=(1,)...  17.1 us
    pallas_call x1, Pallas kernels, second_part(): pl.pallas_call(functools.partial(second_kernel, len(wo), len(ffa), len(ff...  11.6 us
    pallas_call x1, Pallas kernels, attn_bwd(): pl.pallas_call(functools.partial(attn_bwd_kernel, scale), grid=(2,), in_s...  8.37 us
    pallas_call x1, Pallas kernels, attn_bwd_both(): pl.pallas_call(functools.partial(attn_bwd_both_kernel, scale), grid=(2,),...  7.21 us
    pallas_call x1, Pallas kernels, first_part(): pl.pallas_call(functools.partial(first_kernel, len(wo), len(ffw)), grid=(...  4.91 us
    pallas_call x2, Pallas kernels, wgrad(): pl.pallas_call(functools.partial(wgrad_kernel, which), out_shape=jax.Shap...  4.8 us
  transfers between devices with their start and end apart: 22, of which 15 were waited for; matrix products, arithmetic and copies ran while one was open for 2% of the time, Pallas kernels for 31%

profile of v4, /device:TPU:0, one launch (start us, length us, event | category | flops | bytes accessed | tf_op | source)
XLA Modules:
  0.0 125.3 jit_solution(12995737463149723126)
XLA Ops:
  2.3 4.1 %collective-permute-start = (bf16[2,64,512]{2,1,0:T(8,128)(2,1)S(1)}, bf16[2,64,512]{2,1,0:T(8,128)(2,1)S(1)}, u32[]{:S(2)}, u32[]{:S(2)}) collective-permute-start(bf16[2,64,512]{2,1,0:T(8,128)(2,1)S(1)} %get-tuple-element.93), channel_id=1, source_target_pairs={{0,16},{1,17},{2,18},{3,19},{4,20},{5,21},{6,22},{7,23},{8,24},{9,... | collective-permute-start | bytes 393224 | tf_op jit(solution)/shard_map/ppermute | solution.py:560
  8.5 4.2 %attn_fwd.4 = (bf16[2,384,1024]{2,1,0:T(8,128)(2,1)S(1)}, bf16[2,128,1024]{2,1,0:T(8,128)(2,1)S(1)}, f32[2,2,1024]{2,1,0:T(2,128)S(1)}, bf16[2,2,256,2560]{3,2,1,0:T(8,128)(2,1)}) custom-call(bf16[512,1024]{1,0:T(8,128)(2,1)S(1)} %get-tuple-element.90.xt_ref, bf16[512,512]{1,0:T(8,128)(2,1)S(1)} %get-tuple-element.94.w_ref.refs_3_.refs_9_, ...), custom_call_target="tpu_custom_call" | custom-call | flops 5000000000 | bytes 1048576 | tf_op jit(solution)/shard_map/attn_fwd/pallas_call | solution.py:131
  14.3 4.2 %attn_fwd.5 = (bf16[2,384,1024]{2,1,0:T(8,128)(2,1)S(1)}, bf16[2,128,1024]{2,1,0:T(8,128)(2,1)S(1)}, f32[2,2,1024]{2,1,0:T(2,128)S(1)}, bf16[2,2,256,2560]{3,2,1,0:T(8,128)(2,1)}) custom-call(bf16[512,1024]{1,0:T(8,128)(2,1)S(1)} %get-tuple-element.90.xt_ref, ...), custom_call_target="tpu_custom_call", output_to_operand_aliasing={{0}: (3, {}), {1}: (4, {}), {2}: (5, {}), {3}: (6, {})} | custom-call | flops 5000000000 | bytes 1048576 | tf_op jit(solution)/shard_map/attn_fwd/pallas_call | solution.py:131
  19.3 1.6 %collective-permute-start.4 = (bf16[2,256,512]{2,1,0:T(8,128)(2,1)S(1)}, bf16[2,256,512]{2,1,0:T(8,128)(2,1)S(1)}, u32[]{:S(2)}, u32[]{:S(2)}) collective-permute-start(bf16[2,256,512]{2,1,0:T(8,128)(2,1)S(1)} %get-tuple-element.173), channel_id=1, source_target_pairs={{0,8},{1,9},{2,3},{3,2},{4,12},{5,13},{6,7},{7,6},{8,0},{9,1},{10,... | collective-permute-start | bytes 1572872 | tf_op jit(solution)/shard_map/ppermute | solution.py:560
  20.9 4.2 %attn_fwd.6 = (bf16[2,384,1024]{2,1,0:T(8,128)(2,1)S(1)}, bf16[2,128,1024]{2,1,0:T(8,128)(2,1)S(1)}, f32[2,2,1024]{2,1,0:T(2,128)S(1)}, bf16[2,2,256,2560]{3,2,1,0:T(8,128)(2,1)}) custom-call(bf16[512,1024]{1,0:T(8,128)(2,1)S(1)} %get-tuple-element.90.xt_ref, bf16[512,512]{1,0:T(8,128)(2,1)S(1)} %collective-permute-done.1.w_ref.refs_5_.refs_11_, ...), custom_call_target="tpu_custom_call" | custom-call | flops 5000000000 | bytes 1048576 | tf_op jit(solution)/shard_map/attn_fwd/pallas_call | solution.py:131
  25.1 3.4 %collective-permute-done.4 = bf16[2,256,512]{2,1,0:T(8,128)(2,1)S(1)} collective-permute-done((bf16[2,256,512]{2,1,0:T(8,128)(2,1)S(1)}, bf16[2,256,512]{2,1,0:T(8,128)(2,1)S(1)}, u32[]{:S(2)}, u32[]{:S(2)}) %collective-permute-start.4) | collective-permute-done | bytes 524320 | tf_op jit(solution)/shard_map/ppermute | solution.py:560
  32.0 4.4 %attn_fwd.7 = (bf16[2,384,1024]{2,1,0:T(8,128)(2,1)S(1)}, bf16[2,128,1024]{2,1,0:T(8,128)(2,1)S(1)}, f32[2,2,1024]{2,1,0:T(2,128)S(1)}, bf16[2,2,256,2560]{3,2,1,0:T(8,128)(2,1)}) custom-call(bf16[512,1024]{1,0:T(8,128)(2,1)S(1)} %get-tuple-element.90.xt_ref, ...), custom_call_target="tpu_custom_call", output_to_operand_aliasing={{0}: (3, {}), {1}: (4, {}), {2}: (5, {}), {3}: (6, {})} | custom-call | flops 5000000000 | bytes 1048576 | tf_op jit(solution)/shard_map/attn_fwd/pallas_call | solution.py:131
  36.5 4.9 %first_part.1 = (bf16[1024,512]{1,0:T(8,128)(2,1)S(1)}, bf16[1024,1024]{1,0:T(8,128)(2,1)S(1)}, bf16[1024,1024]{1,0:T(8,128)(2,1)S(1)}, bf16[1024,512]{1,0:T(8,1...) custom-call(bf16[1024,512]{1,0:T(8,128)(2,1)S(1)} %copy-done, ...), custom_call_target="tpu_custom_call" | custom-call | flops 8000000000 | bytes 1048576 | tf_op jit(solution)/shard_map/first_part/pallas_call | solution.py:317
  41.5 2.5 %collective-permute-done.6.refs_14_ = bf16[2,512,512]{2,1,0:T(8,128)(2,1)S(1)} collective-permute-done((bf16[2,512,512]{2,1,0:T(8,128)(2,1)S(1)}, bf16[2,512,512]{2,1,0:T(8,128)(2,1)S(1)}, u32[]{:S(2)}, u32[]{:S(2)}) %collective-permute-start.6) | collective-permute-done | bytes 1048608 | tf_op jit(solution)/shard_map/ppermute | solution.py:560
  43.9 2.7 %collective-permute-done.7.refs_15_ = bf16[2,512,512]{2,1,0:T(8,128)(2,1)S(1)} collective-permute-done((bf16[2,512,512]{2,1,0:T(8,128)(2,1)S(1)}, bf16[2,512,512]{2,1,0:T(8,128)(2,1)S(1)}, u32[]{:S(2)}, u32[]{:S(2)}) %collective-permute-start.7) | collective-permute-done | bytes 1048608 | tf_op jit(solution)/shard_map/ppermute | solution.py:560
  46.6 11.6 %second_part.1 = (bf16[1024,512]{1,0:T(8,128)(2,1)}, bf16[1024,512]{1,0:T(8,128)(2,1)}, bf16[1024,1024]{1,0:T(8,128)(2,1)S(1)}, bf16[1024,2048]{1,0:T(8,128)(2,1...) custom-call(bf16[1024,512]{1,0:T(8,128)(2,1)S(1)} %copy-done.2, ...), custom_call_target="tpu_custom_call" | custom-call | flops 17999998976 | bytes 1048576 | tf_op jit(solution)/shard_map/second_part/pallas_call | solution.py:414
  58.3 7.2 %attn_bwd_both.1 = (bf16[2,384,1024]{2,1,0:T(8,128)(2,1)S(1)}, bf16[544,512]{1,0:T(8,128)(2,1)S(1)}, bf16[544,512]{1,0:T(8,128)(2,1)S(1)}) custom-call(bf16[512,1024]{1,0:T(8,128)(2,1)S(1)} %get-tuple-element.90.xt_ref, bf16[2,384,1024]{2,1,0:T(8,128)(2,1)S(1)} %get-tuple-element.125.qkv_ref, ...), custom_call_target="tpu_custom_call" | custom-call | flops 11000000512 | bytes 1048576 | tf_op jit(solution)/shard_map/attn_bwd_both/pallas_call | solution.py:235
  65.7 2.4 %wgrad.2 = bf16[2,2,512,512]{3,2,1,0:T(8,128)(2,1)S(1)} custom-call(bf16[1024,1024]{1,0:T(8,128)(2,1)S(1)} %get-tuple-element.133.act_a_ref, bf16[1024,1024]{1,0:T(8,128)(2,1)S(1)} %get-tuple-element.134.act_b_ref, bf16[1024,2048]{1,0:T(8,128)(2,1)S(1)} %get-tuple-element.147.dh_ref, bf16[1024,512]{1,0:T(8,128)(2,1)S(1)} %get-tuple-element.137.gf_ref, ...), custom_call_target="tpu_custom_call" | custom-call | flops 6000000000 | bytes 1048576 | tf_op jit(solution)/shard_map/wgrad/pallas_call | solution.py:436
  70.2 8.4 %attn_bwd.1 = (bf16[2,384,1024]{2,1,0:T(8,128)(2,1)}, bf16[544,512]{1,0:T(8,128)(2,1)S(1)}, bf16[544,512]{1,0:T(8,128)(2,1)S(1)}) custom-call(bf16[512,1024]{1,0:T(8,128)(2,1)S(1)} %get-tuple-element.90.xt_ref, bf16[2,384,1024]{2,1,0:T(8,128)(2,1)S(1)} %get-tuple-element.123.qkv_ref, bf16[2,128,1024]{2,1,0:T(8,128)(2,1)S(1)} %get-tuple-element.102.refs_0_.att_ref, ...), custom_call_target="tpu_custom_call" | custom-call | flops 11000000512 | bytes 1048576 | tf_op jit(solution)/shard_map/attn_bwd/pallas_call | solution.py:183
  78.6 2.4 %wgrad.3 = bf16[2,2,512,512]{3,2,1,0:T(8,128)(2,1)S(1)} custom-call(bf16[1024,1024]{1,0:T(8,128)(2,1)S(1)} %get-tuple-element.133.act_a_ref, bf16[1024,1024]{1,0:T(8,128)(2,1)S(1)} %copy-done.11, bf16[1024,2048]{1,0:T(8,128)(2,1)S(1)} %get-tuple-element.147.dh_ref, bf16[1024,512]{1,0:T(8,128)(2,1)S(1)} %get-tuple-element.137.gf_ref, ...), custom_call_target="tpu_custom_call" | custom-call | flops 6000000000 | bytes 1048576 | tf_op jit(solution)/shard_map/wgrad/pallas_call | solution.py:436
  85.5 3.7 %sgrad.1 = f32[1024,512]{1,0:T(8,128)} custom-call(f32[1024,512]{1,0:T(8,128)S(1)} %copy-done.8, bf16[2,384,1024]{2,1,0:T(8,128)(2,1)S(1)} %copy-done.9, bf16[2,384,1024]{2,1,0:T(8,128)(2,1)S(1)} %get-tuple-element.150.refs_1_, bf16[512,512]{1,0:T(8,128)(2,1)S(1)} %get-tuple-element.98.w_ref.refs_2_.refs_8_, ...), custom_call_target="tpu_custom_call" | custom-call | flops 4000000000 | bytes 1048576 | tf_op jit(solution)/shard_map/sgrad/pallas_call | solution.py:455
  89.2 4.1 %collective-permute-done.12 = bf16[272,512]{1,0:T(8,128)(2,1)S(1)} collective-permute-done((bf16[272,512]{1,0:T(8,128)(2,1)S(1)}, bf16[272,512]{1,0:T(8,128)(2,1)S(1)}, u32[]{:S(2)}, u32[]{:S(2)}) %collective-permute-start.12) | collective-permute-done | bytes 278560 | tf_op jit(solution)/shard_map/ppermute | solution.py:560
  93.4 1.6 %collective-permute-start.13 = (bf16[136,512]{1,0:T(8,128)(2,1)S(1)}, bf16[136,512]{1,0:T(8,128)(2,1)S(1)}, u32[]{:S(2)}, u32[]{:S(2)}) collective-permute-start(bf16[136,512]{1,0:T(8,128)(2,1)S(1)} %broadcast_select_fusion.1), channel_id=1, source_target_pairs={{0,8},{1,9},{2,6},{3,7},{4,12},{5,13},{6,2},{7,3},{8,0},{9,1},{10,... | collective-permute-start | bytes 417800 | tf_op jit(solution)/shard_map/ppermute | solution.py:560
  96.2 1.6 %collective-permute-start.16 = (bf16[2,256,512]{2,1,0:T(8,128)(2,1)S(1)}, bf16[2,256,512]{2,1,0:T(8,128)(2,1)S(1)}, u32[]{:S(2)}, u32[]{:S(2)}) collective-permute-start(bf16[2,256,512]{2,1,0:T(8,128)(2,1)S(1)} %bitcast.70), channel_id=1, source_target_pairs={{0,4},{1,5},{2,10},{3,11},{4,0},{5,1},{6,14},{7,15},{8,12},{9,13},... | collective-permute-start | bytes 1572872 | tf_op jit(solution)/shard_map/ppermute | solution.py:560
  98.6 2.1 %collective-permute-start.15 = (bf16[136,512]{1,0:T(8,128)(2,1)S(1)}, bf16[136,512]{1,0:T(8,128)(2,1)S(1)}, u32[]{:S(2)}, u32[]{:S(2)}) collective-permute-start(bf16[136,512]{1,0:T(8,128)(2,1)S(1)} %select_add_fusion.1), channel_id=1, source_target_pairs={{0,16},{1,17},{2,18},{3,19},{4,20},{5,21},{6,22},{7,23},{8,24},{9,... | collective-permute-start | bytes 417800 | tf_op jit(solution)/shard_map/ppermute | solution.py:560
  100.7 5.1 %collective-permute-done.16 = bf16[2,256,512]{2,1,0:T(8,128)(2,1)S(1)} collective-permute-done((bf16[2,256,512]{2,1,0:T(8,128)(2,1)S(1)}, bf16[2,256,512]{2,1,0:T(8,128)(2,1)S(1)}, u32[]{:S(2)}, u32[]{:S(2)}) %collective-permute-start.16) | collective-permute-done | bytes 524320 | tf_op jit(solution)/shard_map/ppermute | solution.py:560
  108.3 3.1 %collective-permute-done.17 = bf16[136,512]{1,0:T(8,128)(2,1)S(1)} collective-permute-done((bf16[136,512]{1,0:T(8,128)(2,1)S(1)}, bf16[136,512]{1,0:T(8,128)(2,1)S(1)}, u32[]{:S(2)}, u32[]{:S(2)}) %collective-permute-start.17) | collective-permute-done | bytes 139296 | tf_op jit(solution)/shard_map/ppermute | solution.py:560
  114.3 3.2 %collective-permute-start.21 = (bf16[2,64,512]{2,1,0:T(8,128)(2,1)S(1)}, bf16[2,64,512]{2,1,0:T(8,128)(2,1)S(1)}, u32[]{:S(2)}, u32[]{:S(2)}) collective-permute-start(bf16[2,64,512]{2,1,0:T(8,128)(2,1)S(1)} %fusion.6), channel_id=1, source_target_pairs={{0,16},{1,17},{2,18},{3,19},{4,20},{5,21},{6,22},{7,23},{8,24},{9,... | collective-permute-start | bytes 393224 | tf_op jit(solution)/shard_map/ppermute | solution.py:560
  118.4 3.8 %collective-permute-start.20 = (bf16[544,512]{1,0:T(8,128)(2,1)S(1)}, bf16[544,512]{1,0:T(8,128)(2,1)S(1)}, u32[]{:S(2)}, u32[]{:S(2)}) collective-permute-start(bf16[544,512]{1,0:T(8,128)(2,1)S(1)} %maximum_select_fusion.mine_ref), channel_id=1, source_target_pairs={{0,2},{1,3},{2,0},{3,1},{4,6},{5,7},{6,4},{7,5},{8,10},{9,11},{10,... | collective-permute-start | bytes 1671176 | tf_op jit(solution)/shard_map/ppermute | solution.py:560
  (95 shorter events, 27.7 us)
Async XLA Ops:
  2.3 10.5 %collective-permute-start = (bf16[2,64,512]{2,1,0:T(8,128)(2,1)S(1)}, bf16[2,64,512]{2,1,0:T(8,128)(2,1)S(1)}, u32[]{:S(2)}, u32[]{:S(2)}) collective-permute-start(bf16[2,64,512]{2,1,0:T(8,128)(2,1)S(1)} %get-tuple-element.93), channel_id=1, source_target_pairs={{0,16},{1,17},{2,18},{3,19},{4,20},{5,21},{6,22},{7,23},{8,24},{9,... | collective-permute-start | bytes 393224 | tf_op jit(solution)/shard_map/ppermute | solution.py:560
  6.4 14.6 %collective-permute-start.1 = (bf16[512,512]{1,0:T(8,128)(2,1)S(1)}, bf16[512,512]{1,0:T(8,128)(2,1)S(1)}, u32[]{:S(2)}, u32[]{:S(2)}) collective-permute-start(bf16[512,512]{1,0:T(8,128)(2,1)S(1)} %get-tuple-element.94.w_ref.refs_3_.refs_9_), channel_id=1, source_target_pairs={{0,1},{1,0},{2,3},{3,2},{4,5},{5,4},{6,7},{7,6},{8,9},{9,8},{10,11... | collective-permute-start | bytes 1572872 | tf_op jit(solution)/shard_map/ppermute | solution.py:560
  12.8 6.4 %collective-permute-start.3 = (bf16[2,128,512]{2,1,0:T(8,128)(2,1)S(1)}, bf16[2,128,512]{2,1,0:T(8,128)(2,1)S(1)}, u32[]{:S(2)}, u32[]{:S(2)}) collective-permute-start(bf16[2,128,512]{2,1,0:T(8,128)(2,1)S(1)} %get-tuple-element.177), channel_id=1, source_target_pairs={{0,4},{1,5},{2,10},{3,11},{4,0},{5,1},{6,14},{7,15},{8,12},{9,13},... | collective-permute-start | bytes 786440 | tf_op jit(solution)/shard_map/ppermute | solution.py:560
  19.3 9.2 %collective-permute-start.4 = (bf16[2,256,512]{2,1,0:T(8,128)(2,1)S(1)}, bf16[2,256,512]{2,1,0:T(8,128)(2,1)S(1)}, u32[]{:S(2)}, u32[]{:S(2)}) collective-permute-start(bf16[2,256,512]{2,1,0:T(8,128)(2,1)S(1)} %get-tuple-element.173), channel_id=1, source_target_pairs={{0,8},{1,9},{2,3},{3,2},{4,12},{5,13},{6,7},{7,6},{8,0},{9,1},{10,... | collective-permute-start | bytes 1572872 | tf_op jit(solution)/shard_map/ppermute | solution.py:560
  28.6 7.9 %collective-permute-start.5 = (bf16[2,512,512]{2,1,0:T(8,128)(2,1)S(1)}, bf16[2,512,512]{2,1,0:T(8,128)(2,1)S(1)}, u32[]{:S(2)}, u32[]{:S(2)}) collective-permute-start(bf16[2,512,512]{2,1,0:T(8,128)(2,1)S(1)} %constant_dynamic-update-slice_fusion.5.refs_6_.refs_12_), channel_id=1, source_target_pairs={{0,2},{1,3},{2,0},{3,1},{4,6},{5,7},{6,4},{7,5},{8,10},{9,11},{10,... | collective-permute-start | bytes 3145736 | tf_op jit(solution)/shard_map/ppermute | solution.py:560
  28.6 3.4 %collective-permute-start.2 = (bf16[512,512]{1,0:T(8,128)(2,1)S(1)}, bf16[512,512]{1,0:T(8,128)(2,1)S(1)}, u32[]{:S(2)}, u32[]{:S(2)}) collective-permute-start(bf16[512,512]{1,0:T(8,128)(2,1)S(1)} %collective-permute-done.1.w_ref.refs_5_.refs_11_), channel_id=1, source_target_pairs={{0,2},{1,3},{2,0},{3,1},{4,6},{5,7},{6,4},{7,5},{8,10},{9,11},{10,... | collective-permute-start | bytes 1572872 | tf_op jit(solution)/shard_map/ppermute | solution.py:560
  29.1 14.8 %collective-permute-start.6 = (bf16[2,512,512]{2,1,0:T(8,128)(2,1)S(1)}, bf16[2,512,512]{2,1,0:T(8,128)(2,1)S(1)}, u32[]{:S(2)}, u32[]{:S(2)}) collective-permute-start(bf16[2,512,512]{2,1,0:T(8,128)(2,1)S(1)} %constant_dynamic-update-slice_fusion.5.refs_6_.refs_12_), channel_id=1, source_target_pairs={{0,1},{1,0},{2,6},{3,7},{4,5},{5,4},{6,2},{7,3},{8,9},{9,8},{10,14... | collective-permute-start | bytes 3145736 | tf_op jit(solution)/shard_map/ppermute | solution.py:560
  36.5 33.7 %slice-start.2 = ((s8[5242880]{0:T(1024)(128)(4,1)}), s8[4194304]{0:T(1024)(128)(4,1)S(1)}, s32[]{:S(2)}) async-start(s8[5242880]{0:T(1024)(128)(4,1)} %bitcast.61), calls=%async_computation.2 | async-start | bytes 8388608
  43.9 2.7 %collective-permute-start.7 = (bf16[2,512,512]{2,1,0:T(8,128)(2,1)S(1)}, bf16[2,512,512]{2,1,0:T(8,128)(2,1)S(1)}, u32[]{:S(2)}, u32[]{:S(2)}) collective-permute-start(bf16[2,512,512]{2,1,0:T(8,128)(2,1)S(1)} %collective-permute-done.6.refs_14_), channel_id=1, source_target_pairs={{0,2},{1,3},{2,0},{3,1},{4,6},{5,7},{6,4},{7,5},{8,10},{9,11},{10,... | collective-permute-start | bytes 3145736 | tf_op jit(solution)/shard_map/ppermute | solution.py:560
  46.6 23.6 %slice-start.3 = ((s8[5242880]{0:T(1024)(128)(4,1)}), s8[1048576]{0:T(1024)(128)(4,1)S(1)}, s32[]{:S(2)}) async-start(s8[5242880]{0:T(1024)(128)(4,1)} %bitcast.61), calls=%async_computation.3 | async-start | bytes 2097152
  65.5 3.1 %collective-permute-start.8 = (bf16[544,512]{1,0:T(8,128)(2,1)S(1)}, bf16[544,512]{1,0:T(8,128)(2,1)S(1)}, u32[]{:S(2)}, u32[]{:S(2)}) collective-permute-start(bf16[544,512]{1,0:T(8,128)(2,1)S(1)} %get-tuple-element.132), channel_id=1, source_target_pairs={{0,2},{1,3},{2,0},{3,1},{4,6},{5,7},{6,4},{7,5},{8,10},{9,11},{10,... | collective-permute-start | bytes 1671176 | tf_op jit(solution)/shard_map/ppermute | solution.py:560
  68.1 12.9 %collective-permute-start.11 = (bf16[2,2,512,512]{3,2,1,0:T(8,128)(2,1)S(1)}, bf16[2,2,512,512]{3,2,1,0:T(8,128)(2,1)S(1)}, u32[]{:S(2)}, u32[]{:S(2)}) collective-permute-start(bf16[2,2,512,512]{3,2,1,0:T(8,128)(2,1)S(1)} %wgrad.2), channel_id=1, source_target_pairs={{0,2},{1,3},{2,0},{3,1},{4,6},{5,7},{6,4},{7,5},{8,10},{9,11},{10,... | collective-permute-start | bytes 6291464 | tf_op jit(solution)/shard_map/ppermute | solution.py:560
  68.7 14.7 %collective-permute-start.10 = (bf16[544,512]{1,0:T(8,128)(2,1)S(1)}, bf16[544,512]{1,0:T(8,128)(2,1)S(1)}, u32[]{:S(2)}, u32[]{:S(2)}) collective-permute-start(bf16[544,512]{1,0:T(8,128)(2,1)S(1)} %add.106), channel_id=1, source_target_pairs={{0,1},{1,0},{2,3},{3,2},{4,5},{5,4},{6,7},{7,6},{8,9},{9,8},{10,11... | collective-permute-start | bytes 1671176 | tf_op jit(solution)/shard_map/ppermute | solution.py:560
  78.6 3.3 %collective-permute-start.9 = (bf16[544,512]{1,0:T(8,128)(2,1)S(1)}, bf16[544,512]{1,0:T(8,128)(2,1)S(1)}, u32[]{:S(2)}, u32[]{:S(2)}) collective-permute-start(bf16[544,512]{1,0:T(8,128)(2,1)S(1)} %get-tuple-element.146), channel_id=1, source_target_pairs={{0,2},{1,3},{2,0},{3,1},{4,6},{5,7},{6,4},{7,5},{8,10},{9,11},{10,... | collective-permute-start | bytes 1671176 | tf_op jit(solution)/shard_map/ppermute | solution.py:560
  81.3 14.9 %collective-permute-start.14 = (bf16[2,512,512]{2,1,0:T(8,128)(2,1)S(1)}, bf16[2,512,512]{2,1,0:T(8,128)(2,1)S(1)}, u32[]{:S(2)}, u32[]{:S(2)}) collective-permute-start(bf16[2,512,512]{2,1,0:T(8,128)(2,1)S(1)} %get-tuple-element.168), channel_id=1, source_target_pairs={{0,1},{1,0},{2,6},{3,7},{4,5},{5,4},{6,2},{7,3},{8,9},{9,8},{10,14... | collective-permute-start | bytes 3145736 | tf_op jit(solution)/shard_map/ppermute | solution.py:560
  83.6 9.7 %collective-permute-start.12 = (bf16[272,512]{1,0:T(8,128)(2,1)S(1)}, bf16[272,512]{1,0:T(8,128)(2,1)S(1)}, u32[]{:S(2)}, u32[]{:S(2)}) collective-permute-start(bf16[272,512]{1,0:T(8,128)(2,1)S(1)} %broadcast_select_fusion), channel_id=1, source_target_pairs={{0,4},{1,5},{2,10},{3,11},{4,0},{5,1},{6,14},{7,15},{8,12},{9,13},... | collective-permute-start | bytes 835592 | tf_op jit(solution)/shard_map/ppermute | solution.py:560
  93.4 5.1 %collective-permute-start.13 = (bf16[136,512]{1,0:T(8,128)(2,1)S(1)}, bf16[136,512]{1,0:T(8,128)(2,1)S(1)}, u32[]{:S(2)}, u32[]{:S(2)}) collective-permute-start(bf16[136,512]{1,0:T(8,128)(2,1)S(1)} %broadcast_select_fusion.1), channel_id=1, source_target_pairs={{0,8},{1,9},{2,6},{3,7},{4,12},{5,13},{6,2},{7,3},{8,0},{9,1},{10,... | collective-permute-start | bytes 417800 | tf_op jit(solution)/shard_map/ppermute | solution.py:560
  96.2 9.6 %collective-permute-start.16 = (bf16[2,256,512]{2,1,0:T(8,128)(2,1)S(1)}, bf16[2,256,512]{2,1,0:T(8,128)(2,1)S(1)}, u32[]{:S(2)}, u32[]{:S(2)}) collective-permute-start(bf16[2,256,512]{2,1,0:T(8,128)(2,1)S(1)} %bitcast.70), channel_id=1, source_target_pairs={{0,4},{1,5},{2,10},{3,11},{4,0},{5,1},{6,14},{7,15},{8,12},{9,13},... | collective-permute-start | bytes 1572872 | tf_op jit(solution)/shard_map/ppermute | solution.py:560
  98.6 7.6 %collective-permute-start.15 = (bf16[136,512]{1,0:T(8,128)(2,1)S(1)}, bf16[136,512]{1,0:T(8,128)(2,1)S(1)}, u32[]{:S(2)}, u32[]{:S(2)}) collective-permute-start(bf16[136,512]{1,0:T(8,128)(2,1)S(1)} %select_add_fusion.1), channel_id=1, source_target_pairs={{0,16},{1,17},{2,18},{3,19},{4,20},{5,21},{6,22},{7,23},{8,24},{9,... | collective-permute-start | bytes 417800 | tf_op jit(solution)/shard_map/ppermute | solution.py:560
  106.3 5.2 %collective-permute-start.17 = (bf16[136,512]{1,0:T(8,128)(2,1)S(1)}, bf16[136,512]{1,0:T(8,128)(2,1)S(1)}, u32[]{:S(2)}, u32[]{:S(2)}) collective-permute-start(bf16[136,512]{1,0:T(8,128)(2,1)S(1)} %add.122), channel_id=1, source_target_pairs={{0,8},{1,9},{2,6},{3,7},{4,12},{5,13},{6,2},{7,3},{8,0},{9,1},{10,... | collective-permute-start | bytes 417800 | tf_op jit(solution)/shard_map/ppermute | solution.py:560
  107.8 6.5 %collective-permute-start.19 = (bf16[2,128,512]{2,1,0:T(8,128)(2,1)S(1)}, bf16[2,128,512]{2,1,0:T(8,128)(2,1)S(1)}, u32[]{:S(2)}, u32[]{:S(2)}) collective-permute-start(bf16[2,128,512]{2,1,0:T(8,128)(2,1)S(1)} %get-tuple-element.170), channel_id=1, source_target_pairs={{0,8},{1,9},{2,3},{3,2},{4,12},{5,13},{6,7},{7,6},{8,0},{9,1},{10,... | collective-permute-start | bytes 786440 | tf_op jit(solution)/shard_map/ppermute | solution.py:560
  111.6 6.6 %collective-permute-start.18 = (bf16[272,512]{1,0:T(8,128)(2,1)S(1)}, bf16[272,512]{1,0:T(8,128)(2,1)S(1)}, u32[]{:S(2)}, u32[]{:S(2)}) collective-permute-start(bf16[272,512]{1,0:T(8,128)(2,1)S(1)} %maximum_select_fusion.1), channel_id=1, source_target_pairs={{0,4},{1,5},{2,10},{3,11},{4,0},{5,1},{6,14},{7,15},{8,12},{9,13},... | collective-permute-start | bytes 835592 | tf_op jit(solution)/shard_map/ppermute | solution.py:560
  114.3 7.9 %collective-permute-start.21 = (bf16[2,64,512]{2,1,0:T(8,128)(2,1)S(1)}, bf16[2,64,512]{2,1,0:T(8,128)(2,1)S(1)}, u32[]{:S(2)}, u32[]{:S(2)}) collective-permute-start(bf16[2,64,512]{2,1,0:T(8,128)(2,1)S(1)} %fusion.6), channel_id=1, source_target_pairs={{0,16},{1,17},{2,18},{3,19},{4,20},{5,21},{6,22},{7,23},{8,24},{9,... | collective-permute-start | bytes 393224 | tf_op jit(solution)/shard_map/ppermute | solution.py:560
  118.4 5.4 %collective-permute-start.20 = (bf16[544,512]{1,0:T(8,128)(2,1)S(1)}, bf16[544,512]{1,0:T(8,128)(2,1)S(1)}, u32[]{:S(2)}, u32[]{:S(2)}) collective-permute-start(bf16[544,512]{1,0:T(8,128)(2,1)S(1)} %maximum_select_fusion.mine_ref), channel_id=1, source_target_pairs={{0,2},{1,3},{2,0},{3,1},{4,6},{5,7},{6,4},{7,5},{8,10},{9,11},{10,... | collective-permute-start | bytes 1671176 | tf_op jit(solution)/shard_map/ppermute | solution.py:560
  (16 other events, 128.3 us)
